TPU v7x, 32 devices: a whole 2x2x4 slice. The times are simulated.
32 devices in a mesh: dp: 2 (over y), context: 4 (over x, core), expert: 4 (over z).
Axes of the slice: x: 2, y: 2, z: 4, core: 2. Of those that a mesh axis runs over, the one named last changes fastest.
Arguments:
- tokens: bfloat16 [8, 512, 2048], P(('dp', 'expert'), 'context'), may hold values from -6 to 6
- routes: int32 [8, 512, 6], P(('dp', 'expert'), 'context'), may hold values from 0 to 15, all different within a row; in each aligned block of 128 rows (0 to 127, 128 to 255, ..., all dimensions but the last counted through in order) at most 54 rows name the same one
- grad_out: bfloat16 [8, 512, 2048], P(('dp', 'expert'), 'context'), may hold values from -6 to 6
- attn_gain: bfloat16 [2048], P(('dp', 'context')), may hold values from 0.25 to 1.75
- query_weight: bfloat16 [2048, 3072], P(('dp', 'context'), 'expert'), may hold values from -0.125 to 0.125
- latent_down: bfloat16 [2048, 576], P(('dp', 'context')), may hold values from -0.125 to 0.125
- latent_gain: bfloat16 [512], P(('dp', 'context')), may hold values from 0.25 to 1.75
- latent_up: bfloat16 [512, 4096], P(('dp', 'context'), 'expert'), may hold values from -0.25 to 0.25
- out_weight: bfloat16 [2048, 2048], P('expert', ('dp', 'context')), may hold values from -1 to 1
- ffn_gain: bfloat16 [2048], P(('dp', 'context')), may hold values from 0.25 to 1.75
- router_weight: bfloat16 [2048, 16], P(('dp', 'context')), may hold values from -0.0625 to 0.0625
- shared_gate: bfloat16 [2048, 2816], P(('dp', 'context'), 'expert'), may hold values from -0.125 to 0.125
- shared_up: bfloat16 [2048, 2816], P(('dp', 'context'), 'expert'), may hold values from -0.125 to 0.125
- shared_down: bfloat16 [2816, 2048], P('expert', ('dp', 'context')), may hold values from -0.109375 to 0.109375
- expert_gate: bfloat16 [16, 2048, 1408], P('expert', ('dp', 'context')), may hold values from -0.125 to 0.125
- expert_up: bfloat16 [16, 2048, 1408], P('expert', ('dp', 'context')), may hold values from -0.125 to 0.125
- expert_down: bfloat16 [16, 1408, 2048], P('expert', ('dp', 'context')), may hold values from -1.25 to 1.25
Outputs:
- block_out: bfloat16 [8, 512, 2048], P(('dp', 'expert'), 'context')
- grad_tokens: float32 [8, 512, 2048], P(('dp', 'expert'), 'context')
- grad_attn_gain: float32 [2048], P(('dp', 'context', 'expert'))
- grad_query_weight: float32 [2048, 3072], P(('dp', 'context'), 'expert')
- grad_latent_down: float32 [2048, 576], P(('dp', 'context', 'expert'))
- grad_latent_gain: float32 [512], P(('dp', 'context', 'expert'))
- grad_latent_up: float32 [512, 4096], P(('dp', 'context'), 'expert')
- grad_out_weight: float32 [2048, 2048], P('expert', ('dp', 'context'))
- grad_ffn_gain: float32 [2048], P(('dp', 'context', 'expert'))
- grad_router_weight: float32 [2048, 16], P(('dp', 'context', 'expert'))
- grad_shared_gate: float32 [2048, 2816], P(('dp', 'context'), 'expert')
- grad_shared_up: float32 [2048, 2816], P(('dp', 'context'), 'expert')
- grad_shared_down: float32 [2816, 2048], P('expert', ('dp', 'context'))
- grad_expert_gate: float32 [16, 2048, 1408], P('expert', ('dp', 'context'))
- grad_expert_up: float32 [16, 2048, 1408], P('expert', ('dp', 'context'))
- grad_expert_down: float32 [16, 1408, 2048], P('expert', ('dp', 'context'))
Inputs may be any that keep to these rules, and one draw needn't show every extreme that they name: `routes`: each token names 6 different experts. Among the tokens of one device (aligned blocks of 128 rows) no expert is named more than 54 times, and in every draw some expert is named exactly 54 times.
All inputs are finite; a program needn't handle non-finite values.
Results may differ from a plain program's by a relative error of at most 0.025.
Values may be sent and summed in bfloat16 or wider, within the bound.
A program may use at most 320 MiB of HBM per device.

v0:
```python
import jax
import jax.numpy as jnp
from jax import lax
from jax.experimental.layout import Layout, with_layout_constraint
from jax.sharding import PartitionSpec as P

D = 2048
NOPE = 128
ROPE = 64
VDIM = 128
LATENT = 512
TOPK = 6
PROMPT_DEV = 64
CONT_LEN = 64
TOK_DEV = 128


epsilon = 1e-06


def norm_rows(values, scale_gain):
    return (
        values * lax.rsqrt(jnp.mean(values * values, axis=-1, keepdims=True) + epsilon) * scale_gain
    )


def rotary_tables(places, half_size):
    frequency = 10000.0 ** (-jnp.arange(half_size, dtype=jnp.float32) / half_size)
    angles = places[:, None] * frequency[None, :]
    return (jnp.cos(angles), jnp.sin(angles))


def rotate(values, cosine, sine_part):
    half_size = values.shape[-1] // 2
    lower_half = values[..., :half_size]
    upper_half = values[..., half_size:]
    return jnp.concatenate(
        [
            lower_half * cosine - upper_half * sine_part,
            upper_half * cosine + lower_half * sine_part,
        ],
        axis=-1,
    )


def product(left_side, right_side):
    return jnp.dot(left_side, right_side, preferred_element_type=jnp.float32)


def product_left(left_side, right_side):
    return lax.dot_general(
        left_side, right_side, (((0,), (0,)), ((), ())), preferred_element_type=jnp.float32
    )


def product_right(left_side, right_side):
    return lax.dot_general(
        left_side, right_side, (((1,), (1,)), ((), ())), preferred_element_type=jnp.float32
    )


def against_rows(left_side, right_side):
    return lax.dot_general(
        left_side,
        right_side,
        (((left_side.ndim - 1,), (1,)), ((), ())),
        preferred_element_type=jnp.float32,
    )


PLANE = ("dp", "context")


def swap(values, axis, mask):
    count = lax.axis_size(axis)
    return lax.ppermute(values, axis, [(i, i ^ mask) for i in range(count)])


def place_pieces(pieces, index, count):
    first = pieces[0]
    whole = jnp.zeros((count,) + first.shape, first.dtype)
    for mask, piece in pieces.items():
        whole = lax.dynamic_update_slice(whole, piece[None], (index ^ mask,) + (0,) * first.ndim)
    return with_layout_constraint(whole, Layout(tuple(range(whole.ndim))))


def halves(values):
    middle_row = values.shape[0] // 2
    return values[:middle_row], values[middle_row:]


def plane_pieces(values):
    count = lax.axis_size(PLANE)
    if count == 8:
        by_two = swap(values, PLANE, 2)
        by_four = swap(values, PLANE, 4)
        upper = swap(halves(by_two)[0], PLANE, 4)
        lower = swap(halves(by_four)[1], PLANE, 2)
        pieces = {0: values, 2: by_two, 4: by_four, 6: jnp.concatenate([upper, lower], axis=0)}
        for mask in (0, 2, 4, 6):
            pieces[mask + 1] = swap(pieces[mask], PLANE, 1)
        return pieces
    pieces = {0: values}
    bit = 1
    while bit < count:
        for mask in range(bit):
            pieces[mask + bit] = swap(pieces[mask], PLANE, bit)
        bit *= 2
    return pieces


def plane_gather(values):
    count = lax.axis_size(PLANE)
    whole = place_pieces(plane_pieces(values), lax.axis_index(PLANE), count)
    return whole.reshape((count * values.shape[0],) + values.shape[1:])


def low(values):
    return values.astype(jnp.bfloat16)


def wide(values):
    return values.astype(jnp.float32)


def plane_scatter(values):
    count = lax.axis_size(PLANE)
    index = lax.axis_index(PLANE)
    blocks = values.reshape((count, values.shape[0] // count) + values.shape[1:])

    def part(mask):
        return lax.dynamic_index_in_dim(blocks, index ^ mask, 0, keepdims=False)

    sums = {}
    for mask in range(0, count, 2):
        sums[mask] = wide(part(mask)) + wide(swap(part(mask + 1), PLANE, 1))
    if count == 8:
        upper, lower = halves(low(sums[6]))
        by_four = jnp.concatenate(
            [
                low(halves(sums[4])[0] + wide(swap(upper, PLANE, 2))),
                low(halves(sums[4])[1]),
            ],
            axis=0,
        )
        by_two = jnp.concatenate(
            [
                low(halves(sums[2])[0]),
                low(halves(sums[2])[1] + wide(swap(lower, PLANE, 4))),
            ],
            axis=0,
        )
        return sums[0] + wide(swap(by_four, PLANE, 4)) + wide(swap(by_two, PLANE, 2))
    total = sums[0]
    for mask in range(2, count, 2):
        total = total + wide(swap(low(sums[mask]), PLANE, mask))
    return total


def axis_gather(values, axis):
    count = lax.axis_size(axis)
    pieces = {mask: swap(values, axis, mask) if mask else values for mask in range(count)}
    return place_pieces(pieces, lax.axis_index(axis), count)


def axis_scatter(blocks, axis):
    count = lax.axis_size(axis)
    index = lax.axis_index(axis)

    def part(mask):
        return lax.dynamic_index_in_dim(blocks, index ^ mask, 0, keepdims=False)

    total = wide(part(0))
    for mask in range(1, count):
        total = total + wide(swap(low(part(mask)), axis, mask))
    return total


def body(
    tokens,
    routes,
    grad_out,
    attn_gain,
    query_weight,
    latent_down,
    latent_gain,
    latent_up,
    out_weight,
    ffn_gain,
    router_weight,
    shared_gate,
    shared_up,
    shared_down,
    expert_gate,
    expert_up,
    expert_down,
):
    contexts = lax.axis_size("context")
    context_index = lax.axis_index("context")
    groups_local = lax.axis_size("expert")
    expert_index = lax.axis_index("expert")
    plane_count = lax.axis_size(PLANE)
    plane_index = lax.axis_index(PLANE)
    local_experts = expert_gate.shape[0]
    experts_all = router_weight.shape[1]
    copies = plane_count // local_experts
    expert_own = plane_index // copies
    query_cols = query_weight.shape[1]
    heads_local = query_cols // (NOPE + ROPE)
    down_cols = LATENT + ROPE
    shard_rows = query_weight.shape[0]
    latent_rows = latent_up.shape[0]
    prompt_len = PROMPT_DEV * contexts
    capacity = (TOK_DEV * TOPK * 9 + 8 * experts_all - 1) // (8 * experts_all)
    slots = groups_local * capacity
    token_count = groups_local * TOK_DEV
    score_scale = (NOPE + ROPE) ** (-0.5)

    used_cols = query_cols + down_cols
    extra_cols = experts_all + 3
    pad_cols = -(used_cols + extra_cols) % 128
    latent_gain_col = jnp.concatenate(
        [latent_gain, jnp.zeros((shard_rows - latent_gain.shape[0],), jnp.bfloat16)]
    )
    first_local = jnp.concatenate(
        [
            query_weight,
            latent_down,
            router_weight,
            attn_gain[:, None],
            ffn_gain[:, None],
            latent_gain_col[:, None],
            jnp.zeros((shard_rows, pad_cols), jnp.bfloat16),
        ],
        axis=1,
    )
    first_full = plane_gather(first_local)
    up_local = plane_gather(latent_up)
    out_local = plane_gather(out_weight.T)
    full_router = first_full[:, used_cols : used_cols + experts_all]
    full_attn_gain = first_full[:, used_cols + experts_all]
    full_ffn_gain = first_full[:, used_cols + experts_all + 1]
    full_latent_gain = first_full[:, used_cols + experts_all + 2].reshape(plane_count, shard_rows)
    full_latent_gain = full_latent_gain[:, : latent_gain.shape[0]].reshape(LATENT)

    within = jnp.arange(TOK_DEV, dtype=jnp.int32)
    query_places = jnp.where(
        within < PROMPT_DEV, context_index * PROMPT_DEV + within, prompt_len + within - PROMPT_DEV
    )
    key_places = jnp.arange(prompt_len + CONT_LEN, dtype=jnp.int32)
    allowed = key_places[None, :] <= query_places[:, None]
    cosine, sine_part = rotary_tables(query_places.astype(jnp.float32), ROPE // 2)
    cosine_heads = cosine[None, :, None, :]
    sine_heads = sine_part[None, :, None, :]
    source = wide(tokens[0])
    normed_low = low(norm_rows(source, wide(full_attn_gain)))

    def pack_latent(comp_rows, latent_scale):
        return jnp.concatenate(
            [
                norm_rows(comp_rows[..., :LATENT], latent_scale),
                rotate(comp_rows[..., LATENT:], cosine[None], sine_part[None]),
            ],
            axis=-1,
        )

    normed_all = axis_gather(normed_low, "expert")
    grad_all = axis_gather(grad_out[0], "expert")
    routes_all = axis_gather(routes[0], "expert")
    first_product = product(normed_all, first_full)
    compressed = first_product[..., query_cols:used_cols]
    packed = low(pack_latent(compressed, wide(full_latent_gain)))
    prompt_keys = axis_gather(packed[:, :PROMPT_DEV], "context")
    cont_keys = packed[:, PROMPT_DEV:]
    query_raw = first_product[..., :query_cols].reshape(
        groups_local, TOK_DEV, heads_local, NOPE + ROPE
    )
    query_rows = low(
        jnp.concatenate(
            [query_raw[..., :NOPE], rotate(query_raw[..., NOPE:], cosine_heads, sine_heads)], axis=-1
        )
    )
    query_nope = query_rows[..., :NOPE]
    query_rope = query_rows[..., NOPE:]
    prompt_latent = prompt_keys[..., :LATENT]
    prompt_rope = prompt_keys[..., LATENT:]
    cont_latent = cont_keys[..., :LATENT]
    cont_rope = cont_keys[..., LATENT:]
    prompt_exp = low(product(prompt_latent, up_local)).reshape(
        contexts, groups_local, PROMPT_DEV, heads_local, NOPE + VDIM
    )
    cont_exp = low(product(cont_latent, up_local)).reshape(
        groups_local, CONT_LEN, heads_local, NOPE + VDIM
    )
    prompt_knope = prompt_exp[..., :NOPE]
    prompt_values = prompt_exp[..., NOPE:]
    cont_knope = cont_exp[..., :NOPE]
    cont_values = cont_exp[..., NOPE:]

    def split_keys(values):
        return (
            values[..., :prompt_len].reshape(
                groups_local, heads_local, TOK_DEV, contexts, PROMPT_DEV
            ),
            values[..., prompt_len:],
        )

    def score_all():
        prompt_part = jnp.einsum(
            "gqhd,cgphd->ghqcp", query_nope, prompt_knope, preferred_element_type=jnp.float32
        )
        prompt_part = prompt_part + jnp.einsum(
            "gqhd,cgpd->ghqcp", query_rope, prompt_rope, preferred_element_type=jnp.float32
        )
        prompt_part = prompt_part.reshape(groups_local, heads_local, TOK_DEV, prompt_len)
        cont_part = jnp.einsum(
            "gqhd,gphd->ghqp", query_nope, cont_knope, preferred_element_type=jnp.float32
        )
        cont_part = cont_part + jnp.einsum(
            "gqhd,gpd->ghqp", query_rope, cont_rope, preferred_element_type=jnp.float32
        )
        raw_scores = jnp.concatenate([prompt_part, cont_part], axis=-1)
        return jnp.where(allowed, raw_scores * score_scale, -1e30)

    scores = score_all()
    top_score = jnp.max(scores, axis=-1, keepdims=True)
    exp_scores = jnp.exp(scores - top_score)
    totals = jnp.sum(exp_scores, axis=-1, keepdims=True)
    probs_all = exp_scores / totals
    probs_low = low(probs_all)
    probs_prompt, probs_cont = split_keys(probs_low)
    mixed_rows = jnp.einsum(
        "ghqcp,cgphd->gqhd", probs_prompt, prompt_values, preferred_element_type=jnp.float32
    )
    mixed_rows = mixed_rows + jnp.einsum(
        "ghqp,gphd->gqhd", probs_cont, cont_values, preferred_element_type=jnp.float32
    )
    mixed_all = low(mixed_rows.reshape(groups_local, TOK_DEV, heads_local * VDIM))
    partial_sum = against_rows(mixed_all, out_local)
    middle = source + axis_scatter(low(partial_sum), "expert")
    hidden_own = low(norm_rows(middle, wide(full_ffn_gain)))
    hidden_all = axis_gather(hidden_own, "expert")
    hidden_flat = hidden_all.reshape(token_count, D)
    grad_flat = grad_all.reshape(token_count, D)

    def fetch_expert(weight):
        pieces = {}
        for k in range(local_experts):
            part = lax.dynamic_index_in_dim(weight, expert_own ^ k, 0, keepdims=False)
            pieces[k * copies] = swap(part, PLANE, k * copies) if k else part
        for k in range(local_experts):
            for other in range(1, copies):
                pieces[k * copies + other] = swap(pieces[k * copies], PLANE, other)
        whole = place_pieces(pieces, plane_index, plane_count)
        return whole.reshape(plane_count * weight.shape[1], weight.shape[2])

    def return_expert(partial):
        rows = partial.shape[0] // plane_count
        blocks = partial.reshape(plane_count, rows, partial.shape[1])

        def part(mask):
            return lax.dynamic_index_in_dim(blocks, plane_index ^ mask, 0, keepdims=False)

        received = []
        for k in range(local_experts):
            total = wide(part(k * copies))
            for other in range(1, copies):
                total = total + wide(swap(part(k * copies + other), PLANE, other))
            received.append(wide(swap(low(total), PLANE, k * copies)) if k else total)
        order = []
        for e in range(local_experts):
            chosen = received[0]
            for k in range(1, local_experts):
                chosen = jnp.where(expert_own ^ k == e, received[k], chosen)
            order.append(chosen)
        return jnp.stack(order)

    def exchange(blocks):
        return [swap(blocks[k], PLANE, k * copies) if k else blocks[k] for k in range(local_experts)]

    slot_experts = expert_index * local_experts + (
        expert_own ^ jnp.arange(local_experts, dtype=jnp.int32)
    )
    expert_cols = jnp.arange(experts_all, dtype=jnp.int32)[:, None] == slot_experts[None, :]
    chosen_slots = jnp.any(routes_all[..., None] == slot_experts, axis=2)
    before = (within[:, None] > within[None, :]).astype(jnp.bfloat16)
    rank = jnp.einsum(
        "ts,gsl->gtl",
        before,
        chosen_slots.astype(jnp.bfloat16),
        preferred_element_type=jnp.float32,
    ).astype(jnp.int32)
    slot_of = jnp.where(
        chosen_slots,
        rank + capacity * jnp.arange(groups_local, dtype=jnp.int32)[:, None, None],
        -1,
    ).reshape(token_count, local_experts)
    picked = (
        slot_of.T[:, None, :] == jnp.arange(slots, dtype=jnp.int32)[None, :, None]
    )
    picked_low = picked.astype(jnp.bfloat16).reshape(local_experts * slots, token_count)
    gate_full = fetch_expert(expert_gate)
    up_full = fetch_expert(expert_up)
    down_full = fetch_expert(expert_down)
    grad_slots = low(product(picked_low, grad_flat)).reshape(local_experts, slots, D)
    grad_rows = jnp.concatenate(exchange(grad_slots), axis=0)
    hidden_slots = low(product(picked_low, hidden_flat)).reshape(local_experts, slots, D)
    hidden_rows = jnp.concatenate(exchange(hidden_slots), axis=0)
    logits = product(hidden_flat, full_router)
    expert_probs = jax.nn.softmax(logits, axis=-1)
    gate_tokens = jnp.sum(
        jnp.where(expert_cols[None], expert_probs[:, :, None], 0.0), axis=1
    )
    gate_slots = jnp.sum(jnp.where(picked, gate_tokens.T[:, None, :], 0.0), axis=-1)
    gate_rows = jnp.concatenate(exchange(gate_slots), axis=0)[:, None]
    grad_act = product_right(grad_rows, down_full)
    gate_expert = product(hidden_rows, gate_full)
    up_expert = product(hidden_rows, up_full)
    sigmoid_part = jax.nn.sigmoid(gate_expert)
    silu_part = gate_expert * sigmoid_part
    act_expert = silu_part * up_expert
    grad_gate_rows = jnp.sum(act_expert * grad_act, axis=-1)
    act_low = low(act_expert * gate_rows)
    grad_act = grad_act * gate_rows
    grad_gate_expert = low(
        grad_act * up_expert * sigmoid_part * (1.0 + gate_expert * (1.0 - sigmoid_part))
    )
    grad_up_expert = low(grad_act * silu_part)
    result = low(product(act_low, down_full)).reshape(local_experts, slots, D)
    result_back = jnp.concatenate(exchange(result), axis=0)
    routed_term = product_left(picked_low, result_back)
    grad_pair = low(
        product_right(grad_gate_expert, gate_full) + product_right(grad_up_expert, up_full)
    ).reshape(local_experts, slots, D)
    grad_pair_back = jnp.concatenate(exchange(grad_pair), axis=0)
    grad_routed = product_left(picked_low, grad_pair_back)
    grad_gate_back = jnp.stack(exchange(grad_gate_rows.reshape(local_experts, slots)))
    grad_expert_gate = return_expert(low(product_left(hidden_rows, grad_gate_expert)))
    grad_expert_up = return_expert(low(product_left(hidden_rows, grad_up_expert)))
    grad_expert_down = return_expert(low(product_left(act_low, grad_rows)))

    shared_full = plane_gather(jnp.concatenate([shared_gate, shared_up], axis=1))
    shared_cols = shared_gate.shape[1]
    shared_down_local = plane_gather(shared_down.T)
    shared_product = product(hidden_flat, shared_full)
    gate_shared = shared_product[:, :shared_cols]
    up_shared = shared_product[:, shared_cols:]
    sigmoid_shared = jax.nn.sigmoid(gate_shared)
    silu_shared = gate_shared * sigmoid_shared
    act_shared = low(silu_shared * up_shared)
    branch_out = low(product_right(act_shared, shared_down_local) + routed_term)
    final_rows = middle + axis_scatter(branch_out.reshape(groups_local, TOK_DEV, D), "expert")
    block_out = low(final_rows)
    grad_final = wide(grad_out[0])

    grad_gate_tokens = jnp.sum(jnp.where(picked, grad_gate_back[:, :, None], 0.0), axis=1).T
    grad_spread = jnp.sum(
        jnp.where(expert_cols[None], grad_gate_tokens[:, None, :], 0.0), axis=-1
    )
    weighted = jnp.sum(expert_probs * grad_spread, axis=-1, keepdims=True)
    grad_logits = expert_probs * (grad_spread - weighted)
    grad_router = lax.dot_general(
        wide(hidden_flat),
        grad_logits,
        (((0,), (0,)), ((), ())),
        precision=lax.Precision.HIGHEST,
    )
    grad_from_router = lax.dot_general(
        grad_logits,
        wide(full_router),
        (((1,), (1,)), ((), ())),
        precision=lax.Precision.HIGHEST,
    )
    grad_shared_down = low(product_left(grad_flat, act_shared))
    grad_act_shared = product(grad_flat, shared_down_local)
    grad_gate_shared = low(
        grad_act_shared * up_shared * sigmoid_shared * (1.0 + gate_shared * (1.0 - sigmoid_shared))
    )
    grad_up_shared = low(grad_act_shared * silu_shared)
    grad_shared = jnp.concatenate([grad_gate_shared, grad_up_shared], axis=1)
    grad_shared_first = low(product_left(hidden_flat, grad_shared))
    grad_hidden_part = low(
        product_right(grad_shared, shared_full) + grad_routed + grad_from_router
    )
    grad_hidden = axis_scatter(grad_hidden_part.reshape(groups_local, TOK_DEV, D), "expert")
    _, ffn_norm_back = jax.vjp(norm_rows, middle, wide(full_ffn_gain))
    grad_middle_norm, grad_ffn_gain = ffn_norm_back(grad_hidden)
    grad_middle = grad_final + grad_middle_norm
    branch_all = axis_gather(low(grad_middle), "expert")
    grad_out_weight = low(
        product_left(
            branch_all.reshape(token_count, D), mixed_all.reshape(token_count, heads_local * VDIM)
        )
    )
    grad_mixed = low(product(branch_all, out_local)).reshape(
        groups_local, TOK_DEV, heads_local, VDIM
    )
    grad_probs_prompt = jnp.einsum(
        "gqhd,cgphd->ghqcp", grad_mixed, prompt_values, preferred_element_type=jnp.float32
    )
    grad_probs_cont = jnp.einsum(
        "gqhd,gphd->ghqp", grad_mixed, cont_values, preferred_element_type=jnp.float32
    )
    grad_probs = jnp.concatenate(
        [
            grad_probs_prompt.reshape(groups_local, heads_local, TOK_DEV, prompt_len),
            grad_probs_cont,
        ],
        axis=-1,
    )
    delta_rows = jnp.sum(probs_all * grad_probs, axis=-1, keepdims=True)
    grad_raw = low(probs_all * (grad_probs - delta_rows) * score_scale)
    raw_prompt, raw_cont = split_keys(grad_raw)
    value_prompt = jnp.einsum(
        "ghqcp,gqhd->cgphd", probs_prompt, grad_mixed, preferred_element_type=jnp.float32
    )
    value_cont = jnp.einsum(
        "ghqp,gqhd->gphd", probs_cont, grad_mixed, preferred_element_type=jnp.float32
    )
    knope_prompt = jnp.einsum(
        "ghqcp,gqhd->cgphd", raw_prompt, query_nope, preferred_element_type=jnp.float32
    )
    knope_cont = jnp.einsum(
        "ghqp,gqhd->gphd", raw_cont, query_nope, preferred_element_type=jnp.float32
    )
    krope_prompt = jnp.einsum(
        "ghqcp,gqhd->cgpd", raw_prompt, query_rope, preferred_element_type=jnp.float32
    )
    krope_cont = jnp.einsum(
        "ghqp,gqhd->gpd", raw_cont, query_rope, preferred_element_type=jnp.float32
    )
    grad_query_nope = jnp.einsum(
        "ghqcp,cgphd->gqhd", raw_prompt, prompt_knope, preferred_element_type=jnp.float32
    )
    grad_query_nope = grad_query_nope + jnp.einsum(
        "ghqp,gphd->gqhd", raw_cont, cont_knope, preferred_element_type=jnp.float32
    )
    grad_query_rope = jnp.einsum(
        "ghqcp,cgpd->gqhd", raw_prompt, prompt_rope, preferred_element_type=jnp.float32
    )
    grad_query_rope = grad_query_rope + jnp.einsum(
        "ghqp,gpd->gqhd", raw_cont, cont_rope, preferred_element_type=jnp.float32
    )
    grad_query_raw = jnp.concatenate(
        [grad_query_nope, rotate(grad_query_rope, cosine_heads, -sine_heads)], axis=-1
    )
    grad_query_raw = low(
        grad_query_raw.reshape(groups_local, TOK_DEV, heads_local * (NOPE + ROPE))
    )
    grad_exp_prompt = low(
        jnp.concatenate([knope_prompt, value_prompt], axis=-1).reshape(
            contexts, groups_local, PROMPT_DEV, heads_local * (NOPE + VDIM)
        )
    )
    grad_exp_cont = low(
        jnp.concatenate([knope_cont, value_cont], axis=-1).reshape(
            groups_local, CONT_LEN, heads_local * (NOPE + VDIM)
        )
    )
    latent_prompt = jnp.einsum(
        "cgpf,lf->cgpl", grad_exp_prompt, up_local, preferred_element_type=jnp.float32
    )
    latent_cont = jnp.einsum(
        "gpf,lf->gpl", grad_exp_cont, up_local, preferred_element_type=jnp.float32
    )
    grad_prompt_keys = jnp.concatenate([latent_prompt, krope_prompt], axis=-1)
    grad_cont_keys = jnp.concatenate([latent_cont, krope_cont], axis=-1)
    prompt_sum = axis_scatter(grad_prompt_keys, "context")
    grad_packed = jnp.concatenate([prompt_sum, grad_cont_keys], axis=1)
    _, pack_back = jax.vjp(pack_latent, compressed, wide(full_latent_gain))
    grad_compressed, grad_latent_gain = pack_back(grad_packed)
    grad_first = jnp.concatenate(
        [
            grad_query_raw,
            low(grad_compressed),
            jnp.zeros((groups_local, TOK_DEV, first_full.shape[1] - used_cols), jnp.bfloat16),
        ],
        axis=-1,
    )
    grad_normed = axis_scatter(low(against_rows(grad_first, first_full)), "expert")
    _, attn_norm_back = jax.vjp(norm_rows, source, wide(full_attn_gain))
    grad_source_norm, grad_attn_gain = attn_norm_back(grad_normed)
    grad_tokens = grad_middle + grad_source_norm

    grad_latent_up = jnp.einsum(
        "cgpl,cgpf->lf", prompt_latent, grad_exp_prompt, preferred_element_type=jnp.float32
    )
    grad_latent_up = grad_latent_up + jnp.einsum(
        "gpl,gpf->lf", cont_latent, grad_exp_cont, preferred_element_type=jnp.float32
    )
    first_back = product_left(
        normed_all.reshape(token_count, D), grad_first.reshape(token_count, first_full.shape[1])
    )
    latent_gain_back = jnp.concatenate(
        [
            grad_latent_gain.reshape(plane_count, LATENT // plane_count),
            jnp.zeros((plane_count, shard_rows - LATENT // plane_count), jnp.float32),
        ],
        axis=1,
    ).reshape(D)
    extra_back = jnp.concatenate(
        [
            grad_router,
            grad_attn_gain[:, None],
            grad_ffn_gain[:, None],
            latent_gain_back[:, None],
            jnp.zeros((D, pad_cols), jnp.float32),
        ],
        axis=1,
    )
    first_back = low(jnp.concatenate([first_back[:, :used_cols], extra_back], axis=1))
    first_sum = plane_scatter(first_back)
    small_sum = first_sum[:, query_cols:]
    small_rows = shard_rows // groups_local
    small_own = axis_scatter(
        small_sum.reshape(groups_local, small_rows, small_sum.shape[1]), "expert"
    )
    latent_small = first_sum[: LATENT // plane_count, used_cols + experts_all + 2]
    latent_own = axis_scatter(
        latent_small.reshape(groups_local, LATENT // plane_count // groups_local), "expert"
    )
    up_sum = plane_scatter(low(grad_latent_up))
    out_sum = plane_scatter(grad_out_weight)
    shared_sum = plane_scatter(grad_shared_first)
    shared_down_sum = plane_scatter(grad_shared_down)
    return (
        block_out[None],
        grad_tokens[None],
        small_own[:, down_cols + experts_all],
        first_sum[:, :query_cols],
        small_own[:, :down_cols],
        latent_own,
        up_sum,
        out_sum.T,
        small_own[:, down_cols + experts_all + 1],
        small_own[:, down_cols : down_cols + experts_all],
        shared_sum[:, :shared_cols],
        shared_sum[:, shared_cols:],
        shared_down_sum.T,
        grad_expert_gate,
        grad_expert_up,
        grad_expert_down,
    )


def solution(mesh):
    in_specs = (
        P(("dp", "expert"), "context", None),
        P(("dp", "expert"), "context", None),
        P(("dp", "expert"), "context", None),
        P(("dp", "context")),
        P(("dp", "context"), "expert"),
        P(("dp", "context"), None),
        P(("dp", "context")),
        P(("dp", "context"), "expert"),
        P("expert", ("dp", "context")),
        P(("dp", "context")),
        P(("dp", "context"), None),
        P(("dp", "context"), "expert"),
        P(("dp", "context"), "expert"),
        P("expert", ("dp", "context")),
        P("expert", ("dp", "context"), None),
        P("expert", ("dp", "context"), None),
        P("expert", ("dp", "context"), None),
    )
    out_specs = (
        P(("dp", "expert"), "context", None),
        P(("dp", "expert"), "context", None),
        P(("dp", "context", "expert")),
        P(("dp", "context"), "expert"),
        P(("dp", "context", "expert"), None),
        P(("dp", "context", "expert")),
        P(("dp", "context"), "expert"),
        P("expert", ("dp", "context")),
        P(("dp", "context", "expert")),
        P(("dp", "context", "expert"), None),
        P(("dp", "context"), "expert"),
        P(("dp", "context"), "expert"),
        P("expert", ("dp", "context")),
        P("expert", ("dp", "context"), None),
        P("expert", ("dp", "context"), None),
        P("expert", ("dp", "context"), None),
    )
    return jax.shard_map(body, mesh=mesh, in_specs=in_specs, out_specs=out_specs, check_vma=False)
```

profile of v0, /device:TPU:0, one launch (start us, length us, event | category | flops | bytes accessed | tf_op | source)
XLA Modules:
  0.0 1298.0 jit_solution(1577008017340061709)
XLA Ops:
  102.9 28.4 %collective-permute-done.88 = bf16[128,2048]{1,0:T(8,128)(2,1)S(1)} collective-permute-done((bf16[128,2048]{1,0:T(8,128)(2,1)S(1)}, bf16[128,2048]{1,0:T(8,128)(2,1)S(1)}, u32[]{:S(2)}, u32[]{:S(2)}) %collective-permute-start.88) | collective-permute-done | bytes 524320 | tf_op jit(solution)/shard_map/ppermute | solution.py:76
  156.1 14.1 %collective-permute-done.58 = bf16[256,1408]{1,0:T(8,128)(2,1)S(1)} collective-permute-done((bf16[256,1408]{1,0:T(8,128)(2,1)S(1)}, bf16[256,1408]{1,0:T(8,128)(2,1)S(1)}, u32[]{:S(2)}, u32[]{:S(2)}) %collective-permute-start.58) | collective-permute-done | bytes 720928 | tf_op jit(solution)/shard_map/ppermute | solution.py:76
  173.5 26.3 %collective-permute-done.60 = bf16[256,1408]{1,0:T(8,128)(2,1)S(1)} collective-permute-done((bf16[256,1408]{1,0:T(8,128)(2,1)S(1)}, bf16[256,1408]{1,0:T(8,128)(2,1)S(1)}, u32[]{:S(2)}, u32[]{:S(2)}) %collective-permute-start.60) | collective-permute-done | bytes 720928 | tf_op jit(solution)/shard_map/ppermute | solution.py:76
  200.9 15.1 %collective-permute-done.36 = bf16[256,1408]{1,0:T(8,128)(2,1)S(1)} collective-permute-done((bf16[256,1408]{1,0:T(8,128)(2,1)S(1)}, bf16[256,1408]{1,0:T(8,128)(2,1)S(1)}, u32[]{:S(2)}, u32[]{:S(2)}) %collective-permute-start.36) | collective-permute-done | bytes 720928 | tf_op jit(solution)/shard_map/ppermute | solution.py:76
  219.5 17.0 %collective-permute-done.65 = bf16[256,1408]{1,0:T(8,128)(2,1)S(1)} collective-permute-done((bf16[256,1408]{1,0:T(8,128)(2,1)S(1)}, bf16[256,1408]{1,0:T(8,128)(2,1)S(1)}, u32[]{:S(2)}, u32[]{:S(2)}) %collective-permute-start.65) | collective-permute-done | bytes 720928 | tf_op jit(solution)/shard_map/ppermute | solution.py:76
  239.5 17.2 %collective-permute-done.67 = bf16[256,1408]{1,0:T(8,128)(2,1)} collective-permute-done((bf16[256,1408]{1,0:T(8,128)(2,1)S(1)}, bf16[256,1408]{1,0:T(8,128)(2,1)}, u32[]{:S(2)}, u32[]{:S(2)}) %collective-permute-start.67) | collective-permute-done | bytes 720928 | tf_op jit(solution)/shard_map/ppermute | solution.py:76
  274.7 12.5 collective-permute-done.77
  299.0 21.9 %collective-permute-done.38 = bf16[128,1408]{1,0:T(8,128)(2,1)S(1)} collective-permute-done((bf16[128,1408]{1,0:T(8,128)(2,1)S(1)}, bf16[128,1408]{1,0:T(8,128)(2,1)S(1)}, u32[]{:S(2)}, u32[]{:S(2)}) %collective-permute-start.38) | collective-permute-done | bytes 360480 | tf_op jit(solution)/shard_map/ppermute | solution.py:76
  360.5 21.8 %collective-permute-done.8 = bf16[128,2048]{1,0:T(8,128)(2,1)} collective-permute-done((bf16[128,2048]{1,0:T(8,128)(2,1)S(1)}, bf16[128,2048]{1,0:T(8,128)(2,1)}, u32[]{:S(2)}, u32[]{:S(2)}) %collective-permute-start.8) | collective-permute-done | bytes 524320 | tf_op jit(solution)/shard_map/ppermute | solution.py:76
  468.1 12.9 collective-permute-done.32
  481.1 21.9 %collective-permute-done.31 = bf16[128,2048]{1,0:T(8,128)(2,1)} collective-permute-done((bf16[128,2048]{1,0:T(8,128)(2,1)S(1)}, bf16[128,2048]{1,0:T(8,128)(2,1)}, u32[]{:S(2)}, u32[]{:S(2)}) %collective-permute-start.31) | collective-permute-done | bytes 524320 | tf_op jit(solution)/shard_map/ppermute | solution.py:76
  513.3 13.6 %collective-permute-done.33 = bf16[128,2048]{1,0:T(8,128)(2,1)S(1)} collective-permute-done((bf16[128,2048]{1,0:T(8,128)(2,1)S(1)}, bf16[128,2048]{1,0:T(8,128)(2,1)S(1)}, u32[]{:S(2)}, u32[]{:S(2)}) %collective-permute-start.33) | collective-permute-done | bytes 524320 | tf_op jit(solution)/shard_map/ppermute | solution.py:76
  527.0 19.3 %collective-permute-done.34 = bf16[128,2048]{1,0:T(8,128)(2,1)S(1)} collective-permute-done((bf16[128,2048]{1,0:T(8,128)(2,1)S(1)}, bf16[128,2048]{1,0:T(8,128)(2,1)S(1)}, u32[]{:S(2)}, u32[]{:S(2)}) %collective-permute-start.34) | collective-permute-done | bytes 524320 | tf_op jit(solution)/shard_map/ppermute | solution.py:76
  624.0 18.0 %collective-permute-done.156 = bf16[128,704]{0,1:T(8,128)(2,1)S(1)} collective-permute-done((bf16[128,704]{0,1:T(8,128)(2,1)S(1)}, bf16[128,704]{0,1:T(8,128)(2,1)S(1)}, u32[]{:S(2)}, u32[]{:S(2)}) %collective-permute-start.156) | collective-permute-done | bytes 180256 | tf_op jit(solution)/shard_map/ppermute | solution.py:76
  650.5 17.5 %collective-permute-done.55 = bf16[216,2048]{1,0:T(8,128)(2,1)S(1)} collective-permute-done((bf16[216,2048]{1,0:T(8,128)(2,1)S(1)}, bf16[216,2048]{1,0:T(8,128)(2,1)S(1)}, u32[]{:S(2)}, u32[]{:S(2)}) %collective-permute-start.55) | collective-permute-done | bytes 884768 | tf_op jit(solution)/shard_map/ppermute | solution.py:76
  688.4 12.2 multiply_reduce_fusion
  806.4 14.0 %collective-permute-done.96 = bf16[216,2048]{1,0:T(8,128)(2,1)S(1)} collective-permute-done((bf16[216,2048]{1,0:T(8,128)(2,1)S(1)}, bf16[216,2048]{1,0:T(8,128)(2,1)S(1)}, u32[]{:S(2)}, u32[]{:S(2)}) %collective-permute-start.96) | collective-permute-done | bytes 884768 | tf_op jit(solution)/shard_map/ppermute | solution.py:76
  822.2 17.3 %collective-permute-done.95 = bf16[216,2048]{1,0:T(8,128)(2,1)S(1)} collective-permute-done((bf16[216,2048]{1,0:T(8,128)(2,1)S(1)}, bf16[216,2048]{1,0:T(8,128)(2,1)S(1)}, u32[]{:S(2)}, u32[]{:S(2)}) %collective-permute-start.95) | collective-permute-done | bytes 884768 | tf_op jit(solution)/shard_map/ppermute | solution.py:76
  858.4 18.0 %collective-permute-done.83 = bf16[216,2048]{1,0:T(8,128)(2,1)S(1)} collective-permute-done((bf16[216,2048]{1,0:T(8,128)(2,1)S(1)}, bf16[216,2048]{1,0:T(8,128)(2,1)S(1)}, u32[]{:S(2)}, u32[]{:S(2)}) %collective-permute-start.83) | collective-permute-done | bytes 884768 | tf_op jit(solution)/shard_map/ppermute | solution.py:76
  910.1 12.1 collective-permute-done.102
  923.1 27.6 %collective-permute-done.101 = bf16[128,2048]{1,0:T(8,128)(2,1)S(1)} collective-permute-done((bf16[128,2048]{1,0:T(8,128)(2,1)S(1)}, bf16[128,2048]{1,0:T(8,128)(2,1)S(1)}, u32[]{:S(2)}, u32[]{:S(2)}) %collective-permute-start.101) | collective-permute-done | bytes 524320 | tf_op jit(solution)/shard_map/ppermute | solution.py:76
  958.0 13.0 %collective-permute-done.159 = bf16[256,1408]{1,0:T(8,128)(2,1)} collective-permute-done((bf16[256,1408]{1,0:T(8,128)(2,1)}, bf16[256,1408]{1,0:T(8,128)(2,1)}, u32[]{:S(2)}, u32[]{:S(2)}) %collective-permute-start.159) | collective-permute-done | bytes 720928 | tf_op jit(solution)/shard_map/ppermute | solution.py:76
  1173.7 21.1 %collective-permute-done.110 = bf16[128,2048]{1,0:T(8,128)(2,1)} collective-permute-done((bf16[128,2048]{1,0:T(8,128)(2,1)}, bf16[128,2048]{1,0:T(8,128)(2,1)}, u32[]{:S(2)}, u32[]{:S(2)}) %collective-permute-start.110) | collective-permute-done | bytes 524320 | tf_op jit(solution)/shard_map/ppermute | solution.py:76
  1254.2 24.2 %collective-permute-done.86 = bf16[128,2048]{1,0:T(8,128)(2,1)S(1)} collective-permute-done((bf16[128,2048]{1,0:T(8,128)(2,1)S(1)}, bf16[128,2048]{1,0:T(8,128)(2,1)S(1)}, u32[]{:S(2)}, u32[]{:S(2)}) %collective-permute-start.86) | collective-permute-done | bytes 524320 | tf_op jit(solution)/shard_map/ppermute | solution.py:76
  (1141 shorter events, 856.4 us)
Async XLA Ops:
  2.1 60.7 %collective-permute-start.54 = (s32[128,6]{1,0:T(8,128)}, s32[128,6]{1,0:T(8,128)}, u32[]{:S(2)}, u32[]{:S(2)}) collective-permute-start(s32[128,6]{1,0:T(8,128)} %bitcast.86), channel_id=1, source_target_pairs={{0,3},{1,2},{2,1},{3,0},{4,7},{5,6},{6,5},{7,4},{8,11},{9,10},{10,... | collective-permute-start | bytes 9224 | tf_op jit(solution)/shard_map/ppermute | solution.py:76
  7.8 60.9 %collective-permute-start.14 = (bf16[64,1024]{1,0:T(8,128)(2,1)}, bf16[64,1024]{1,0:T(8,128)(2,1)}, u32[]{:S(2)}, u32[]{:S(2)}) collective-permute-start(bf16[64,1024]{1,0:T(8,128)(2,1)} %param.24), channel_id=1, source_target_pairs={{0,8},{4,12},{8,0},{12,4},{16,24},{20,28},{24,16},{28,20},{1,9},{5... | collective-permute-start | bytes 393224 | tf_op jit(solution)/shard_map/ppermute | solution.py:76
  9.5 71.7 %collective-permute-start.18 = (bf16[64,1024]{1,0:T(8,128)(2,1)}, bf16[64,1024]{1,0:T(8,128)(2,1)}, u32[]{:S(2)}, u32[]{:S(2)}) collective-permute-start(bf16[64,1024]{1,0:T(8,128)(2,1)} %param.24), channel_id=1, source_target_pairs={{0,4},{4,0},{8,12},{12,8},{16,20},{20,16},{24,28},{28,24},{1,5},{5... | collective-permute-start | bytes 393224 | tf_op jit(solution)/shard_map/ppermute | solution.py:76
  83.6 70.5 %collective-permute-start.48 = (bf16[256,704]{1,0:T(8,128)(2,1)S(1)}, bf16[256,704]{1,0:T(8,128)(2,1)S(1)}, u32[]{:S(2)}, u32[]{:S(2)}) collective-permute-start(bf16[256,704]{1,0:T(8,128)(2,1)S(1)} %bitcast.826), channel_id=1, source_target_pairs={{0,4},{4,0},{8,12},{12,8},{16,20},{20,16},{24,28},{28,24},{1,5},{5... | collective-permute-start | bytes 1081352 | tf_op jit(solution)/shard_map/ppermute | solution.py:76
  102.1 234.4 %collective-permute-start.4 = (bf16[256,1408]{1,0:T(8,128)(2,1)S(1)}, bf16[256,1408]{1,0:T(8,128)(2,1)S(1)}, u32[]{:S(2)}, u32[]{:S(2)}) collective-permute-start(bf16[256,1408]{1,0:T(8,128)(2,1)S(1)} %concatenate.129), channel_id=1, source_target_pairs={{0,4},{4,0},{8,12},{12,8},{16,20},{20,16},{24,28},{28,24},{1,5},{5... | collective-permute-start | bytes 2162696 | tf_op jit(solution)/shard_map/ppermute | solution.py:76
  131.3 87.8 %collective-permute-start.1 = (bf16[256,1408]{1,0:T(8,128)(2,1)S(1)}, bf16[256,1408]{1,0:T(8,128)(2,1)S(1)}, u32[]{:S(2)}, u32[]{:S(2)}) collective-permute-start(bf16[256,1408]{1,0:T(8,128)(2,1)S(1)} %concatenate.129), channel_id=1, source_target_pairs={{0,16},{4,20},{8,24},{12,28},{16,0},{20,4},{24,8},{28,12},{1,17},{... | collective-permute-start | bytes 2162696 | tf_op jit(solution)/shard_map/ppermute | solution.py:76
  154.1 64.4 %collective-permute-start = (bf16[256,1408]{1,0:T(8,128)(2,1)S(1)}, bf16[256,1408]{1,0:T(8,128)(2,1)S(1)}, u32[]{:S(2)}, u32[]{:S(2)}) collective-permute-start(bf16[256,1408]{1,0:T(8,128)(2,1)S(1)} %concatenate.129), channel_id=1, source_target_pairs={{0,8},{4,12},{8,0},{12,4},{16,24},{20,28},{24,16},{28,20},{1,9},{5... | collective-permute-start | bytes 2162696 | tf_op jit(solution)/shard_map/ppermute | solution.py:76
  216.0 119.5 %collective-permute-start.40 = (bf16[256,1408]{1,0:T(8,128)(2,1)S(1)}, bf16[256,1408]{1,0:T(8,128)(2,1)S(1)}, u32[]{:S(2)}, u32[]{:S(2)}) collective-permute-start(bf16[256,1408]{1,0:T(8,128)(2,1)S(1)} %copy-done.114), channel_id=1, source_target_pairs={{0,4},{4,0},{8,12},{12,8},{16,20},{20,16},{24,28},{28,24},{1,5},{5... | collective-permute-start | bytes 2162696 | tf_op jit(solution)/shard_map/ppermute | solution.py:76
  217.0 73.1 %collective-permute-start.78 = (bf16[176,2048]{1,0:T(8,128)(2,1)S(1)}, bf16[176,2048]{1,0:T(8,128)(2,1)S(1)}, u32[]{:S(2)}, u32[]{:S(2)}) collective-permute-start(bf16[176,2048]{1,0:T(8,128)(2,1)S(1)} %copy-done.102), channel_id=1, source_target_pairs={{0,4},{4,0},{8,12},{12,8},{16,20},{20,16},{24,28},{28,24},{1,5},{5... | collective-permute-start | bytes 2162696 | tf_op jit(solution)/shard_map/ppermute | solution.py:76
  290.0 395.7 %collective-permute-start.93 = (bf16[216,2048]{1,0:T(8,128)(2,1)}, bf16[216,2048]{1,0:T(8,128)(2,1)}, u32[]{:S(2)}, u32[]{:S(2)}) collective-permute-start(bf16[216,2048]{1,0:T(8,128)(2,1)} %get-tuple-element.190), channel_id=1, source_target_pairs={{0,24},{4,28},{8,16},{12,20},{16,8},{20,12},{24,0},{28,4},{1,25},{... | collective-permute-start | bytes 2654216 | tf_op jit(solution)/shard_map/ppermute | solution.py:76
  343.7 113.0 %collective-permute-start.80 = (bf16[176,2048]{1,0:T(8,128)(2,1)}, bf16[176,2048]{1,0:T(8,128)(2,1)}, u32[]{:S(2)}, u32[]{:S(2)}) collective-permute-start(bf16[176,2048]{1,0:T(8,128)(2,1)} %collective-permute-done.76), channel_id=1, source_target_pairs={{0,4},{4,0},{8,12},{12,8},{16,20},{20,16},{24,28},{28,24},{1,5},{5... | collective-permute-start | bytes 2162696 | tf_op jit(solution)/shard_map/ppermute | solution.py:76
  345.3 113.8 %collective-permute-start.71 = (bf16[256,1408]{1,0:T(8,128)(2,1)}, bf16[256,1408]{1,0:T(8,128)(2,1)}, u32[]{:S(2)}, u32[]{:S(2)}) collective-permute-start(bf16[256,1408]{1,0:T(8,128)(2,1)} %collective-permute-done.67), channel_id=1, source_target_pairs={{0,4},{4,0},{8,12},{12,8},{16,20},{20,16},{24,28},{28,24},{1,5},{5... | collective-permute-start | bytes 2162696 | tf_op jit(solution)/shard_map/ppermute | solution.py:76
  650.5 137.1 %collective-permute-start.150 = (bf16[256,704]{0,1:T(8,128)(2,1)}, bf16[256,704]{0,1:T(8,128)(2,1)}, u32[]{:S(2)}, u32[]{:S(2)}) collective-permute-start(bf16[256,704]{0,1:T(8,128)(2,1)} %bitcast.755), channel_id=1, source_target_pairs={{0,4},{4,0},{8,12},{12,8},{16,20},{20,16},{24,28},{28,24},{1,5},{5... | collective-permute-start | bytes 1081352 | tf_op jit(solution)/shard_map/ppermute | solution.py:76
  668.0 119.6 %collective-permute-start.157 = (bf16[256,704]{0,1:T(8,128)(2,1)}, bf16[256,704]{0,1:T(8,128)(2,1)}, u32[]{:S(2)}, u32[]{:S(2)}) collective-permute-start(bf16[256,704]{0,1:T(8,128)(2,1)} %pad_maximum_fusion.21), channel_id=1, source_target_pairs={{0,8},{4,12},{8,0},{12,4},{16,24},{20,28},{24,16},{28,20},{1,9},{5... | collective-permute-start | bytes 1081352 | tf_op jit(solution)/shard_map/ppermute | solution.py:76
  714.6 73.5 %collective-permute-start.154 = (bf16[256,704]{0,1:T(8,128)(2,1)}, bf16[256,704]{0,1:T(8,128)(2,1)S(1)}, u32[]{:S(2)}, u32[]{:S(2)}) collective-permute-start(bf16[256,704]{0,1:T(8,128)(2,1)} %pad_maximum_fusion.20), channel_id=1, source_target_pairs={{0,16},{4,20},{8,24},{12,28},{16,0},{20,4},{24,8},{28,12},{1,17},{... | collective-permute-start | bytes 1081352 | tf_op jit(solution)/shard_map/ppermute | solution.py:76
  716.3 74.9 %collective-permute-start.145 = (bf16[128,1408]{0,1:T(8,128)(2,1)}, bf16[128,1408]{0,1:T(8,128)(2,1)}, u32[]{:S(2)}, u32[]{:S(2)}) collective-permute-start(bf16[128,1408]{0,1:T(8,128)(2,1)} %get-tuple-element.257), channel_id=1, source_target_pairs={{0,8},{4,12},{8,0},{12,4},{16,24},{20,28},{24,16},{28,20},{1,9},{5... | collective-permute-start | bytes 1081352 | tf_op jit(solution)/shard_map/ppermute | solution.py:76
  717.2 75.1 %collective-permute-start.148 = (bf16[128,1408]{0,1:T(8,128)(2,1)}, bf16[128,1408]{0,1:T(8,128)(2,1)}, u32[]{:S(2)}, u32[]{:S(2)}) collective-permute-start(bf16[128,1408]{0,1:T(8,128)(2,1)} %get-tuple-element.258), channel_id=1, source_target_pairs={{0,16},{4,20},{8,24},{12,28},{16,0},{20,4},{24,8},{28,12},{1,17},{... | collective-permute-start | bytes 1081352 | tf_op jit(solution)/shard_map/ppermute | solution.py:76
  802.5 84.1 %collective-permute-start.142 = (bf16[256,1408]{0,1:T(8,128)(2,1)S(1)}, bf16[256,1408]{0,1:T(8,128)(2,1)S(1)}, u32[]{:S(2)}, u32[]{:S(2)}) collective-permute-start(bf16[256,1408]{0,1:T(8,128)(2,1)S(1)} %bitcast.833), channel_id=1, source_target_pairs={{0,4},{4,0},{8,12},{12,8},{16,20},{20,16},{24,28},{28,24},{1,5},{5... | collective-permute-start | bytes 2162696 | tf_op jit(solution)/shard_map/ppermute | solution.py:76
  820.5 56.0 %collective-permute-start.83 = (bf16[216,2048]{1,0:T(8,128)(2,1)S(1)}, bf16[216,2048]{1,0:T(8,128)(2,1)S(1)}, u32[]{:S(2)}, u32[]{:S(2)}) collective-permute-start(bf16[216,2048]{1,0:T(8,128)(2,1)S(1)} %get-tuple-element.183), channel_id=1, source_target_pairs={{0,16},{4,20},{8,24},{12,28},{16,0},{20,4},{24,8},{28,12},{1,17},{... | collective-permute-start | bytes 2654216 | tf_op jit(solution)/shard_map/ppermute | solution.py:76
  840.6 133.9 %collective-permute-start.178 = (bf16[176,2048]{1,0:T(8,128)(2,1)}, bf16[176,2048]{1,0:T(8,128)(2,1)}, u32[]{:S(2)}, u32[]{:S(2)}) collective-permute-start(bf16[176,2048]{1,0:T(8,128)(2,1)} %get-tuple-element.136), channel_id=1, source_target_pairs={{0,4},{4,0},{8,12},{12,8},{16,20},{20,16},{24,28},{28,24},{1,5},{5... | collective-permute-start | bytes 2162696 | tf_op jit(solution)/shard_map/ppermute | solution.py:76
  858.4 96.1 %collective-permute-start.164 = (bf16[256,1408]{1,0:T(8,128)(2,1)}, bf16[256,1408]{1,0:T(8,128)(2,1)}, u32[]{:S(2)}, u32[]{:S(2)}) collective-permute-start(bf16[256,1408]{1,0:T(8,128)(2,1)} %get-tuple-element.150), channel_id=1, source_target_pairs={{0,4},{4,0},{8,12},{12,8},{16,20},{20,16},{24,28},{28,24},{1,5},{5... | collective-permute-start | bytes 2162696 | tf_op jit(solution)/shard_map/ppermute | solution.py:76
  954.9 59.9 %collective-permute-start.171 = (bf16[256,1408]{1,0:T(8,128)(2,1)S(1)}, bf16[256,1408]{1,0:T(8,128)(2,1)S(1)}, u32[]{:S(2)}, u32[]{:S(2)}) collective-permute-start(bf16[256,1408]{1,0:T(8,128)(2,1)S(1)} %copy-done.120), channel_id=1, source_target_pairs={{0,4},{4,0},{8,12},{12,8},{16,20},{20,16},{24,28},{28,24},{1,5},{5... | collective-permute-start | bytes 2162696 | tf_op jit(solution)/shard_map/ppermute | solution.py:76
  1077.0 154.5 %collective-permute-start.134 = (bf16[256,512]{0,1:T(8,128)(2,1)}, bf16[256,512]{0,1:T(8,128)(2,1)}, u32[]{:S(2)}, u32[]{:S(2)}) collective-permute-start(bf16[256,512]{0,1:T(8,128)(2,1)} %bitcast.842), channel_id=1, source_target_pairs={{0,4},{4,0},{8,12},{12,8},{16,20},{20,16},{24,28},{28,24},{1,5},{5... | collective-permute-start | bytes 786440 | tf_op jit(solution)/shard_map/ppermute | solution.py:76
  1115.9 97.9 %collective-permute-start.135 = (bf16[256,512]{0,1:T(8,128)(2,1)}, bf16[256,512]{0,1:T(8,128)(2,1)}, u32[]{:S(2)}, u32[]{:S(2)}) collective-permute-start(bf16[256,512]{0,1:T(8,128)(2,1)} %bitcast.242), channel_id=1, source_target_pairs={{0,4},{4,0},{8,12},{12,8},{16,20},{20,16},{24,28},{28,24},{1,5},{5... | collective-permute-start | bytes 786440 | tf_op jit(solution)/shard_map/ppermute | solution.py:76
  (362 other events, 7029.1 us)
where the time goes:
time: 1300 us
  waiting for transfers between devices  590 us (45%)
  local copies, waits for them, and re-layouts  241 us (19%)
  starting transfers between devices  188 us (14%)
  matrix products  188 us (14%)
  other arithmetic  85.9 us (7%)
    ppermute x179, waiting for transfers between devices, swap(): return lax.ppermute(values, axis, [(i, i ^ mask) for i in range(count)])  590 us
    ppermute x179, starting transfers between devices, swap(): return lax.ppermute(values, axis, [(i, i ^ mask) for i in range(count)])  188 us
    dot_general x12, matrix products, product(): return jnp.dot(left_side, right_side, preferred_element_type=jnp.float32)  58 us
    dynamic_update_slice x80, local copies, waits for them, and re-layouts, place_pieces(): lax.dynamic_update_slice(whole, piece[None], (index ^ mask,) + (0,) * fir...  56.9 us
    dot_general x9, matrix products, product_left(): lax.dot_general(left_side, right_side, (((0,), (0,)), ((), ())), preferre...  46.2 us
    dot_general x5, matrix products, product_right(): lax.dot_general(left_side, right_side, (((1,), (1,)), ((), ())), preferre...  43.3 us
    unnamed x442, local copies, waits for them, and re-layouts  41 us
  transfers between devices with their start and end apart: 179, of which 64 were waited for; matrix products, arithmetic and copies ran while one was open for 35% of the time, Pallas kernels for 0%

commit v1 on v0

v1 whole, which is shorter than its diff:
```python
import jax
import jax.numpy as jnp
from jax import lax
from jax.experimental import pallas as pl
from jax.experimental.pallas import tpu as pltpu
from jax.experimental.layout import Layout, with_layout_constraint
from jax.sharding import PartitionSpec as P

D = 2048
NOPE = 128
ROPE = 64
VDIM = 128
LATENT = 512
TOPK = 6
PROMPT_DEV = 64
CONT_LEN = 64
TOK_DEV = 128


epsilon = 1e-06


def norm_rows(values, scale_gain):
    return (
        values * lax.rsqrt(jnp.mean(values * values, axis=-1, keepdims=True) + epsilon) * scale_gain
    )


def rotary_tables(places, half_size):
    frequency = 10000.0 ** (-jnp.arange(half_size, dtype=jnp.float32) / half_size)
    angles = places[:, None] * frequency[None, :]
    return (jnp.cos(angles), jnp.sin(angles))


def rotate(values, cosine, sine_part):
    half_size = values.shape[-1] // 2
    lower_half = values[..., :half_size]
    upper_half = values[..., half_size:]
    return jnp.concatenate(
        [
            lower_half * cosine - upper_half * sine_part,
            upper_half * cosine + lower_half * sine_part,
        ],
        axis=-1,
    )


def product(left_side, right_side):
    return jnp.dot(left_side, right_side, preferred_element_type=jnp.float32)


def product_left(left_side, right_side):
    return lax.dot_general(
        left_side, right_side, (((0,), (0,)), ((), ())), preferred_element_type=jnp.float32
    )


def product_right(left_side, right_side):
    return lax.dot_general(
        left_side, right_side, (((1,), (1,)), ((), ())), preferred_element_type=jnp.float32
    )


def against_rows(left_side, right_side):
    return lax.dot_general(
        left_side,
        right_side,
        (((left_side.ndim - 1,), (1,)), ((), ())),
        preferred_element_type=jnp.float32,
    )


DP_AXIS, CONTEXT_AXIS, EXPERT_AXIS = "dp", "context", "expert"
PLANE = (DP_AXIS, CONTEXT_AXIS)


def swap(values, axis, mask):
    count = lax.axis_size(axis)
    return lax.ppermute(values, axis, [(i, i ^ mask) for i in range(count)])


def place_pieces(pieces, index, count):
    first = pieces[0]
    whole = jnp.zeros((count,) + first.shape, first.dtype)
    for mask, piece in pieces.items():
        whole = lax.dynamic_update_slice(whole, piece[None], (index ^ mask,) + (0,) * first.ndim)
    return with_layout_constraint(whole, Layout(tuple(range(whole.ndim))))


def low(values):
    return values.astype(jnp.bfloat16)


def wide(values):
    return values.astype(jnp.float32)


def axis_gather(values, axis):
    count = lax.axis_size(axis)
    pieces = {mask: swap(values, axis, mask) if mask else values for mask in range(count)}
    return place_pieces(pieces, lax.axis_index(axis), count)


def axis_scatter(blocks, axis):
    count = lax.axis_size(axis)
    index = lax.axis_index(axis)

    def part(mask):
        return lax.dynamic_index_in_dim(blocks, index ^ mask, 0, keepdims=False)

    total = wide(part(0))
    for mask in range(1, count):
        total = total + wide(swap(low(part(mask)), axis, mask))
    return total


MESH_ID = pl.DeviceIdType.MESH
ANY = pl.BlockSpec(memory_space=pl.ANY)
INSIDE = pl.BlockSpec(memory_space=pltpu.VMEM)


def plane_here():
    return lax.axis_index(DP_AXIS) * lax.axis_size(CONTEXT_AXIS) + lax.axis_index(CONTEXT_AXIS)


def plane_device(mask):
    contexts = lax.axis_size(CONTEXT_AXIS)
    other = jnp.bitwise_xor(plane_here(), mask)
    return {DP_AXIS: other // contexts, CONTEXT_AXIS: lax.rem(other, contexts)}


def line_device(offset):
    return {EXPERT_AXIS: lax.axis_index(EXPERT_AXIS) + offset}


def signal(device):
    pl.semaphore_signal(
        pltpu.get_barrier_semaphore(), inc=1, device_id=device, device_id_type=MESH_ID
    )


def meet(masks, line):
    count = len(masks)
    for mask in masks:
        signal(plane_device(mask))
    if line:
        place, last = lax.axis_index(EXPERT_AXIS), lax.axis_size(EXPERT_AXIS) - 1
        pl.when(place > 0)(lambda: signal(line_device(-1)))
        pl.when(place < last)(lambda: signal(line_device(1)))
        count = count + jnp.where(place > 0, 1, 0) + jnp.where(place < last, 1, 0)
    pl.semaphore_wait(pltpu.get_barrier_semaphore(), count)


def remote(source, target, send, recv, device):
    return pltpu.make_async_remote_copy(
        src_ref=source,
        dst_ref=target,
        send_sem=send,
        recv_sem=recv,
        device_id=device,
        device_id_type=MESH_ID,
    )


def arrived(target, send, recv):
    remote(target, target, send, recv, plane_device(1)).wait_recv()


def run_tasks(*tasks):
    active = list(tasks)
    while active:
        for task in list(active):
            if next(task, None) is None:
                active.remove(task)


def plane_gather_task(source, target, own, send, recv):
    rows = source.shape[0]
    half = rows // 2
    here = plane_here()

    def slot(mask, first=0, count=rows):
        start = pl.multiple_of(jnp.bitwise_xor(here, mask) * rows + first, 16)
        return target.at[pl.ds(start, count)]

    def go(number, source_ref, target_ref, mask):
        copy = remote(source_ref, target_ref, send.at[number], recv.at[number], plane_device(mask))
        copy.start()
        return copy

    def got(number, ref):
        arrived(ref, send.at[number], recv.at[number])

    local = pltpu.make_async_copy(source, slot(0), own)
    copies = [go(0, source, slot(0), 2), go(1, source, slot(0), 4)]
    yield 1
    copies.append(go(4, source, slot(0), 1))
    local.start()
    yield 1
    got(0, slot(2))
    copies.append(go(2, slot(2, 0, half), slot(2, 0, half), 4))
    copies.append(go(5, slot(2), slot(2), 1))
    yield 1
    got(1, slot(4))
    copies.append(go(3, slot(4, half, half), slot(4, half, half), 2))
    copies.append(go(6, slot(4), slot(4), 1))
    yield 1
    got(2, slot(6, 0, half))
    copies.append(go(7, slot(6, 0, half), slot(6, 0, half), 1))
    yield 1
    got(3, slot(6, half, half))
    copies.append(go(8, slot(6, half, half), slot(6, half, half), 1))
    yield 1
    got(4, slot(1))
    got(5, slot(3))
    got(6, slot(5))
    got(7, slot(7, 0, half))
    got(8, slot(7, half, half))
    local.wait()
    for copy in copies:
        copy.wait_send()


def expert_fetch_task(source, target, stage, own, send, recv):
    if source.shape[0] == 1:
        load = pltpu.make_async_copy(source.at[0], stage, own)
        load.start()
        load.wait()
        yield from plane_gather_task(stage, target, own, send, recv)
        return
    rows = source.shape[1]
    here = plane_here()
    expert_own = here // 2

    def slot(mask):
        start = pl.multiple_of(jnp.bitwise_xor(here, mask) * rows, 16)
        return target.at[pl.ds(start, rows)]

    def go(number, source_ref, target_ref, mask):
        copy = remote(source_ref, target_ref, send.at[number], recv.at[number], plane_device(mask))
        copy.start()
        return copy

    def got(number, ref):
        arrived(ref, send.at[number], recv.at[number])

    copies = []
    for k in (3, 1, 2):
        copies.append(go(k, source.at[jnp.bitwise_xor(expert_own, k)], slot(0), 2 * k))
    load = pltpu.make_async_copy(source.at[expert_own], stage, own)
    load.start()
    yield 1
    load.wait()
    local = pltpu.make_async_copy(stage, slot(0), own)
    local.start()
    copies.append(go(0, stage, slot(0), 1))
    for k in (1, 2, 3):
        yield 1
        got(k, slot(2 * k))
        copies.append(go(4 + k, slot(2 * k), slot(2 * k), 1))
    yield 1
    got(0, slot(1))
    for k in (1, 2, 3):
        got(4 + k, slot(2 * k + 1))
    local.wait()
    for copy in copies:
        copy.wait_send()


LINE_PARTS = 4


def line_gather_steps(target, send, recv, rows):
    place, count = lax.axis_index(EXPERT_AXIS), lax.axis_size(EXPERT_AXIS)
    part = rows // LINE_PARTS

    def piece(block, c):
        return target.at[block, pl.ds(c * part, part)]

    def copy(way, distance, c, source=None):
        block = place - way * distance
        ref = piece(block, c)
        return remote(
            ref if source is None else source,
            ref,
            send.at[(way + 1) // 2, distance, c],
            recv.at[(way + 1) // 2, distance, c],
            line_device(way),
        )

    def has_next(way):
        return place < count - 1 if way == 1 else place > 0

    def has_block(way, distance):
        return place - distance >= 0 if way == 1 else place + distance < count

    def begin(c, source):
        for way in (1, -1):
            pl.when(has_next(way))(lambda way=way: copy(way, 0, c, source).start())

    def forward(c, distance):
        for way in (1, -1):

            @pl.when(has_block(way, distance))
            def _(way=way):
                ref = piece(place - way * distance, c)
                arrived(
                    ref,
                    send.at[(way + 1) // 2, distance - 1, c],
                    recv.at[(way + 1) // 2, distance - 1, c],
                )
                if distance < count - 1:
                    pl.when(has_next(way))(lambda: copy(way, distance, c).start())

    def finish(source):
        for c in range(LINE_PARTS):
            for way in (1, -1):
                for distance in range(count - 1):

                    @pl.when(jnp.logical_and(has_next(way), has_block(way, distance)))
                    def _(way=way, distance=distance, c=c):
                        copy(way, distance, c, source(c) if distance == 0 else None).wait_send()

    return begin, forward, finish


def line_gather_task(source, target, own, send, recv):
    rows = source.shape[0]
    part = rows // LINE_PARTS
    count = lax.axis_size(EXPERT_AXIS)
    begin, forward, finish = line_gather_steps(target, send, recv, rows)
    local = pltpu.make_async_copy(source, target.at[lax.axis_index(EXPERT_AXIS)], own)
    for c in range(LINE_PARTS):
        begin(c, source.at[pl.ds(c * part, part)])
    local.start()
    yield 1
    for distance in range(1, count):
        for c in range(LINE_PARTS):
            forward(c, distance)
        yield 1
    local.wait()
    finish(lambda c: source.at[pl.ds(c * part, part)])


def line_semaphores():
    count = lax.axis_size(EXPERT_AXIS)
    return [pltpu.SemaphoreType.DMA((2, count, LINE_PARTS))] * 2


def line_reduce_steps(partial, inbox, send, recv):
    place, count = lax.axis_index(EXPERT_AXIS), lax.axis_size(EXPERT_AXIS)
    rows = partial.shape[1]
    part = rows // LINE_PARTS

    def span(c):
        return pl.ds(c * part, part)

    def box(way, distance, c):
        return inbox.at[distance if way == 1 else count - distance, span(c)]

    def copy(way, distance, c, source):
        side = (way + 1) // 2
        return remote(
            source,
            box(way, distance - 1, c),
            send.at[side, distance, c],
            recv.at[side, distance - 1, c],
            line_device(way),
        )

    def wait_inbox(way, distance, c):
        side = (way + 1) // 2
        arrived(box(way, distance, c), send.at[side, distance, c], recv.at[side, distance, c])

    def has_source(way):
        return place > 0 if way == 1 else place < count - 1

    def has_target(way, distance):
        return place + distance < count if way == 1 else place - distance >= 0

    def step(c, distance):
        for way in (1, -1):
            mine = partial.at[place + way * distance, span(c)]

            def pass_on(way=way, mine=mine):
                came = box(way, distance, c)
                wait_inbox(way, distance, c)
                came[...] = low(wide(mine[...]) + wide(came[...]))
                copy(way, distance, c, came).start()

            def send_first(way=way, mine=mine):
                copy(way, distance, c, mine).start()

            valid = has_target(way, distance)
            if distance < count - 1:
                pl.when(jnp.logical_and(valid, has_source(way)))(pass_on)
                pl.when(jnp.logical_and(valid, jnp.logical_not(has_source(way))))(send_first)
            else:
                pl.when(valid)(send_first)

    def total(c, result):
        result[span(c)] = result[span(c)] + wide(partial[place, span(c)])
        for way in (1, -1):

            @pl.when(has_source(way))
            def _(way=way):
                wait_inbox(way, 0, c)
                result[span(c)] = result[span(c)] + wide(box(way, 0, c)[...])

    def stages(result, done):
        for t in range(LINE_PARTS + count - 1):
            for c in range(LINE_PARTS):
                distance = count - 1 - (t - c)
                if 1 <= distance <= count - 1:
                    step(c, distance)
                elif distance == 0:
                    total(c, result)
                    done(span(c), c)
            yield 1

    def finish():
        for c in range(LINE_PARTS):
            for way in (1, -1):
                for distance in range(1, count):
                    pl.when(has_target(way, distance))(
                        lambda way=way, distance=distance, c=c: copy(
                            way, distance, c, partial.at[place + way * distance, span(c)]
                        ).wait_send()
                    )

    return stages, finish


def gather_semaphores():
    return [
        pltpu.SemaphoreType.DMA(()),
        pltpu.SemaphoreType.DMA((9,)),
        pltpu.SemaphoreType.DMA((9,)),
    ]


def kernel_params(number):
    return pltpu.CompilerParams(
        collective_id=number,
        has_side_effects=True,
        vmem_limit_bytes=(52 if lax.axis_size(EXPERT_AXIS) <= 4 else 60) << 20,
    )


def opening(tokens, gains, matrices):
    count = lax.axis_size(EXPERT_AXIS)
    rows, width = tokens.shape
    number = len(matrices)
    planes = lax.axis_size(PLANE)
    depth = gains.shape[1]

    def kernel(*refs):
        tokens_ref, gains_ref = refs[:2]
        sources = refs[2 : 2 + number]
        gains_all, normed_all = refs[2 + number : 4 + number]
        targets = refs[4 + number : 4 + 2 * number]
        scratch = list(refs[4 + 2 * number :])
        normed, gain_box, gain_send, gain_recv = scratch[:4]
        line = scratch[4:7]
        semaphores = scratch[7:]
        meet(range(1, planes), True)
        here = plane_here()
        sends = []
        for mask in range(1, planes):
            copy = remote(
                gains_ref,
                gain_box.at[here],
                gain_send.at[mask],
                gain_recv.at[mask],
                plane_device(mask),
            )
            copy.start()
            sends.append(copy)
        tasks = [
            plane_gather_task(sources[i], targets[i], *semaphores[3 * i : 3 * i + 3])
            for i in range(number)
        ]
        for task in tasks:
            next(task)
        for task in tasks:
            next(task)
        gain_box[here] = gains_ref[...]
        values = wide(tokens_ref[...])
        scale = lax.rsqrt(jnp.mean(values * values, axis=-1, keepdims=True) + epsilon)
        for mask in range(1, planes):
            other = gain_box.at[jnp.bitwise_xor(here, mask)]
            arrived(other, gain_send.at[mask], gain_recv.at[mask])
        for i in range(planes):
            columns = slice(i * depth, (i + 1) * depth)
            normed[:, columns] = low(
                wide(tokens_ref[:, columns]) * scale * gain_box[i, 0:1, :]
            )
        gains_all[...] = gain_box[...]
        rows_task = line_gather_task(normed, normed_all, *line)
        next(rows_task)
        next(rows_task)
        for task in tasks:
            next(task)
        for task in tasks:
            next(task)
        run_tasks(rows_task, *tasks)
        for copy in sends:
            copy.wait_send()

    shapes = [
        jax.ShapeDtypeStruct((planes,) + gains.shape, jnp.float32),
        jax.ShapeDtypeStruct((count, rows, width), jnp.bfloat16),
    ] + [jax.ShapeDtypeStruct((planes * m.shape[0], m.shape[1]), m.dtype) for m in matrices]
    scratch = [
        pltpu.VMEM((rows, width), jnp.bfloat16),
        pltpu.VMEM((planes,) + gains.shape, jnp.float32),
        pltpu.SemaphoreType.DMA((planes,)),
        pltpu.SemaphoreType.DMA((planes,)),
        pltpu.SemaphoreType.DMA(()),
    ]
    scratch += line_semaphores()
    for _ in matrices:
        scratch += gather_semaphores()
    results = pl.pallas_call(
        kernel,
        out_shape=shapes,
        in_specs=[INSIDE] * (2 + number),
        out_specs=[INSIDE, ANY] + [ANY] * number,
        scratch_shapes=scratch,
        compiler_params=kernel_params(1),
        cost_estimate=pl.CostEstimate(
            flops=60_000_000, bytes_accessed=150_000_000, transcendentals=0
        ),
        name="opening",
    )(tokens, gains, *matrices)
    return results[0], results[1], results[2:]


def middle_sum(partial, source, gain, matrices, experts, before):
    count, rows, width = partial.shape
    planes = lax.axis_size(PLANE)
    number, routed = len(matrices), len(experts)

    def kernel(*refs):
        position = 3 + number + routed + 1
        partial_ref, source_ref, gain_ref = refs[:3]
        sources = refs[3 : 3 + number]
        expert_refs = refs[3 + number : position - 1]
        middle_ref, hidden_all = refs[position : position + 2]
        targets = refs[position + 2 : position + 2 + number + routed]
        scratch = list(refs[position + 2 + number + routed :])
        inbox, hidden, reduce_send, reduce_recv, own, line_send, line_recv = scratch[:7]
        stages = scratch[7 : 7 + routed]
        semaphores = scratch[7 + routed :]
        meet((1, 2, 4, 6), True)
        reduce_stages, reduce_finish = line_reduce_steps(
            partial_ref, inbox, reduce_send, reduce_recv
        )
        begin, forward, finish = line_gather_steps(hidden_all, line_send, line_recv, rows)
        part = rows // LINE_PARTS

        def ready(span, c):
            values = middle_ref[span]
            scale = lax.rsqrt(jnp.mean(values * values, axis=-1, keepdims=True) + epsilon)
            hidden[span] = low(values * scale * gain_ref[...])
            begin(c, hidden.at[span])

        def line_task():
            middle_ref[...] = wide(source_ref[...])
            yield from reduce_stages(middle_ref, ready)
            local = pltpu.make_async_copy(hidden, hidden_all.at[lax.axis_index(EXPERT_AXIS)], own)
            local.start()
            for distance in range(1, count):
                for c in range(LINE_PARTS):
                    forward(c, distance)
                yield 1
            local.wait()
            finish(lambda c: hidden.at[pl.ds(c * part, part)])
            reduce_finish()

        tasks = [
            plane_gather_task(sources[i], targets[i], *semaphores[3 * i : 3 * i + 3])
            for i in range(number)
        ] + [
            expert_fetch_task(
                expert_refs[i],
                targets[number + i],
                stages[i],
                *semaphores[3 * (number + i) : 3 * (number + i) + 3],
            )
            for i in range(routed)
        ]
        for task in tasks:
            next(task)
        for task in tasks:
            next(task)
        run_tasks(line_task())
        run_tasks(*tasks)

    shapes = (
        [
            jax.ShapeDtypeStruct((rows, width), jnp.float32),
            jax.ShapeDtypeStruct((count, rows, width), jnp.bfloat16),
        ]
        + [jax.ShapeDtypeStruct((planes * m.shape[0], m.shape[1]), m.dtype) for m in matrices]
        + [jax.ShapeDtypeStruct((planes * e.shape[1], e.shape[2]), e.dtype) for e in experts]
    )
    scratch = [
        pltpu.VMEM((count + 1, rows, width), jnp.bfloat16),
        pltpu.VMEM((rows, width), jnp.bfloat16),
    ]
    scratch += line_semaphores() + [pltpu.SemaphoreType.DMA(())] + line_semaphores()
    scratch += [pltpu.VMEM(e.shape[1:], e.dtype) for e in experts]
    for _ in range(number + routed):
        scratch += gather_semaphores()
    results = pl.pallas_call(
        kernel,
        out_shape=shapes,
        in_specs=[INSIDE] * (3 + number) + [ANY] * (routed + 1),
        out_specs=[INSIDE] + [ANY] * (1 + number + routed),
        scratch_shapes=scratch,
        compiler_params=kernel_params(2),
        cost_estimate=pl.CostEstimate(
            flops=60_000_000, bytes_accessed=300_000_000, transcendentals=0
        ),
        name="middle_sum",
    )(partial, source, gain, *matrices, *experts, before)
    return results[0], results[1], results[2 : 2 + number], results[2 + number :]


def add_rows(target, first, second):
    def tile(i, carry):
        span = pl.ds(pl.multiple_of(i * 16, 16), 16)
        target[span] = (wide(first[span]) + wide(second[span])).astype(target.dtype)
        return carry

    lax.fori_loop(0, target.shape[0] // 16, tile, 0)


def expert_return_task(source, result, mine, came, load, send, recv):
    rows = mine.shape[1]
    here = plane_here()
    expert_own = here // 2

    def slot(mask):
        return source.at[pl.ds(pl.multiple_of(jnp.bitwise_xor(here, mask) * rows, 16), rows)]

    def go(number, source_ref, target_ref, mask):
        copy = remote(source_ref, target_ref, send.at[number], recv.at[number], plane_device(mask))
        copy.start()
        return copy

    copies, loads = [], {}

    def cross(k):
        copies.append(go(k, slot(2 * k + 1), came.at[k], 1))
        loads[k] = pltpu.make_async_copy(slot(2 * k), mine.at[k], load.at[k])
        loads[k].start()

    cross(3)
    yield 1
    for k, following in ((3, 1), (1, 2), (2, 0), (0, None)):
        if following is not None:
            cross(following)
        arrived(came.at[k], send.at[k], recv.at[k])
        loads[k].wait()
        add_rows(mine.at[k], mine.at[k], came.at[k])
        if k:
            copies.append(go(4 + k, mine.at[k], result.at[expert_own], 2 * k))
        else:
            local = pltpu.make_async_copy(mine.at[0], result.at[expert_own], load.at[0])
            local.start()
        yield 1
    for k in (3, 1, 2):
        arrived(
            result.at[jnp.bitwise_xor(expert_own, k)], send.at[4 + k], recv.at[4 + k]
        )
    local.wait()
    for copy in copies:
        copy.wait_send()


def expert_return_scratch(rows, columns):
    return [
        pltpu.VMEM((4, rows, columns), jnp.bfloat16),
        pltpu.VMEM((4, rows, columns), jnp.bfloat16),
        pltpu.SemaphoreType.DMA((4,)),
        pltpu.SemaphoreType.DMA((8,)),
        pltpu.SemaphoreType.DMA((8,)),
    ]


def plane_scatter_task(source, result, mine, came, box, last, load, send, recv):
    rows = mine.shape[1]
    half = rows // 2
    here = plane_here()
    upper, lower = pl.ds(0, half), pl.ds(half, half)

    def slot(mask):
        return source.at[pl.ds(pl.multiple_of(jnp.bitwise_xor(here, mask) * rows, 16), rows)]

    def go(number, source_ref, target_ref, mask):
        copy = remote(source_ref, target_ref, send.at[number], recv.at[number], plane_device(mask))
        copy.start()
        return copy

    def got(number, ref):
        arrived(ref, send.at[number], recv.at[number])

    copies, loads = [], {}

    def cross(k):
        copies.append(go(k, slot(2 * k + 1), came.at[k], 1))
        loads[k] = pltpu.make_async_copy(slot(2 * k), mine.at[k], load.at[k])
        loads[k].start()

    cross(3)
    yield 1
    for k, following in ((3, 1), (1, 2), (2, 0)):
        cross(following)
        got(k, came.at[k])
        loads[k].wait()
        add_rows(mine.at[k], mine.at[k], came.at[k])
        if k == 3:
            copies.append(go(4, mine.at[3, upper], box.at[0], 2))
            copies.append(go(5, mine.at[3, lower], box.at[1], 4))
        elif k == 1:
            copies.append(go(6, mine.at[1, upper], last.at[0, upper], 2))
        else:
            copies.append(go(7, mine.at[2, lower], last.at[1, lower], 4))
        yield 1
    got(4, box.at[0])
    add_rows(mine.at[2, upper], mine.at[2, upper], box.at[0])
    copies.append(go(8, mine.at[2, upper], last.at[1, upper], 4))
    yield 1
    got(5, box.at[1])
    add_rows(mine.at[1, lower], mine.at[1, lower], box.at[1])
    copies.append(go(9, mine.at[1, lower], last.at[0, lower], 2))
    yield 1
    got(0, came.at[0])
    loads[0].wait()
    add_rows(result, mine.at[0], came.at[0])
    got(6, last.at[0, upper])
    got(7, last.at[1, lower])
    yield 1
    got(9, last.at[0, lower])
    add_rows(result, result, last.at[0])
    got(8, last.at[1, upper])
    add_rows(result, result, last.at[1])
    for copy in copies:
        copy.wait_send()


def plane_scatter_scratch(rows, columns):
    return [
        pltpu.VMEM((4, rows, columns), jnp.bfloat16),
        pltpu.VMEM((4, rows, columns), jnp.bfloat16),
        pltpu.VMEM((2, rows // 2, columns), jnp.bfloat16),
        pltpu.VMEM((2, rows, columns), jnp.bfloat16),
        pltpu.SemaphoreType.DMA((4,)),
        pltpu.SemaphoreType.DMA((10,)),
        pltpu.SemaphoreType.DMA((10,)),
    ]


def norm_back(values, gain, grad):
    scale = lax.rsqrt(jnp.mean(values * values, axis=-1, keepdims=True) + epsilon)
    scaled = gain * grad
    mean = jnp.mean(values * scaled, axis=-1, keepdims=True)
    part = jnp.sum(values * scale * grad, axis=0, keepdims=True)
    return scale * scaled - values * (scale * scale * scale * mean), part


def branch_sum(partial, middle, gain, grad_out, experts, local_experts, later):
    count, rows, width = partial.shape
    planes = lax.axis_size(PLANE)
    routed, waiting = len(experts), len(later)

    def kernel(*refs):
        partial_ref, middle_ref, gain_ref, grad_ref = refs[:4]
        expert_refs = refs[4 : 4 + routed]
        outputs = refs[4 + routed + waiting :]
        grad_middle, grad_gain, branch_all = outputs[:3]
        results = outputs[3 : 3 + routed]
        scratch = list(outputs[3 + routed + waiting :])
        inbox, branch, reduce_send, reduce_recv, own, line_send, line_recv = scratch[:7]
        rest = scratch[7:]
        meet((1, 2, 4, 6), True)
        reduce_stages, reduce_finish = line_reduce_steps(
            partial_ref, inbox, reduce_send, reduce_recv
        )
        begin, forward, finish = line_gather_steps(branch_all, line_send, line_recv, rows)
        part = rows // LINE_PARTS

        def ready(span, c):
            back, gain_part = norm_back(middle_ref[span], gain_ref[...], grad_middle[span])
            grad_gain[...] = gain_part if c == 0 else grad_gain[...] + gain_part
            back = wide(grad_ref[span]) + back
            grad_middle[span] = back
            branch[span] = low(back)
            begin(c, branch.at[span])

        def line_task():
            grad_middle[...] = jnp.zeros((rows, width), jnp.float32)
            yield from reduce_stages(grad_middle, ready)
            local = pltpu.make_async_copy(branch, branch_all.at[lax.axis_index(EXPERT_AXIS)], own)
            local.start()
            for distance in range(1, count):
                for c in range(LINE_PARTS):
                    forward(c, distance)
                yield 1
            local.wait()
            finish(lambda c: branch.at[pl.ds(c * part, part)])
            reduce_finish()

        task_kind = plane_scatter_task if local_experts == 1 else expert_return_task
        size = len(rest) // routed
        tasks = [
            task_kind(
                expert_refs[i], results[i], *rest[size * i : size * (i + 1)]
            )
            for i in range(routed)
        ]
        line = line_task()
        for stage in range(5):
            for task in tasks:
                next(task)
            if stage:
                next(line)
        run_tasks(line)
        run_tasks(*tasks)

    shapes = [
        jax.ShapeDtypeStruct((rows, width), jnp.float32),
        jax.ShapeDtypeStruct((1, width), jnp.float32),
        jax.ShapeDtypeStruct((count, rows, width), jnp.bfloat16),
    ]
    scratch = [
        pltpu.VMEM((count + 1, rows, width), jnp.bfloat16),
        pltpu.VMEM((rows, width), jnp.bfloat16),
    ]
    scratch += line_semaphores() + [pltpu.SemaphoreType.DMA(())] + line_semaphores()
    for expert in experts:
        shard, columns = expert.shape[0] // planes, expert.shape[1]
        if local_experts == 1:
            shapes.append(jax.ShapeDtypeStruct((shard, columns), jnp.float32))
            scratch += plane_scatter_scratch(shard, columns)
        else:
            shapes.append(jax.ShapeDtypeStruct((local_experts, shard, columns), jnp.bfloat16))
            scratch += expert_return_scratch(shard, columns)
    shapes += [jax.ShapeDtypeStruct(x.shape, x.dtype) for x in later]
    results = pl.pallas_call(
        kernel,
        out_shape=shapes,
        in_specs=[INSIDE] * 4 + [ANY] * (routed + waiting),
        out_specs=[INSIDE, INSIDE, ANY]
        + [INSIDE if local_experts == 1 else ANY] * routed
        + [ANY] * waiting,
        input_output_aliases={4 + routed + i: 3 + routed + i for i in range(waiting)},
        scratch_shapes=scratch,
        compiler_params=kernel_params(3),
        cost_estimate=pl.CostEstimate(
            flops=60_000_000, bytes_accessed=300_000_000, transcendentals=0
        ),
        name="branch_sum",
    )(partial, middle, gain, grad_out, *experts, *later)
    grads = [
        wide(r).reshape((local_experts,) + r.shape[-2:]) for r in results[3 : 3 + routed]
    ]
    return results[0], results[1][0], results[2], grads, results[3 + routed :]


def meet_all():
    planes, count = lax.axis_size(PLANE), lax.axis_size(EXPERT_AXIS)
    for mask in range(1, planes):
        signal(plane_device(mask))
    for mask in range(1, count):
        signal({EXPERT_AXIS: jnp.bitwise_xor(lax.axis_index(EXPERT_AXIS), mask)})
    pl.semaphore_wait(pltpu.get_barrier_semaphore(), planes + count - 2)


def closing(partial, ready_before, source, gain, grad_middle, gain_grads, matrices, spread):
    count, rows, width = partial.shape
    planes = lax.axis_size(PLANE)
    number = len(matrices)
    depth = gain_grads.shape[2]
    shard, columns = matrices[0].shape[0] // planes, matrices[0].shape[1]
    thin = shard // count

    def kernel(*refs):
        partial_ref, _, source_ref, gain_ref, middle_ref, gains_ref = refs[:6]
        sources = refs[6 : 6 + number]
        grad_tokens, gains_out, thin_out = refs[6 + number : 9 + number]
        results = refs[9 + number : 9 + 2 * number]
        scratch = list(refs[9 + 2 * number :])
        inbox, reduce_send, reduce_recv, gain_row = scratch[:4]
        gain_part, gain_box, gain_send, gain_recv = scratch[4:8]
        gain_held, gain_far, far_send, far_recv, thin_box, thin_send, thin_recv = scratch[8:15]
        rest = scratch[15:]
        meet_all()
        place = lax.axis_index(EXPERT_AXIS)
        here = plane_here()
        reduce_stages, reduce_finish = line_reduce_steps(
            partial_ref, inbox, reduce_send, reduce_recv
        )

        def ready(span, c):
            back, row = norm_back(wide(source_ref[span]), gain_ref[...], grad_tokens[span])
            gain_row[...] = row if c == 0 else gain_row[...] + row
            grad_tokens[span] = middle_ref[span] + back

        def line_task():
            grad_tokens[...] = jnp.zeros((rows, width), jnp.float32)
            yield from reduce_stages(grad_tokens, ready)
            gain_part[...] = gains_ref[...]
            for i in range(planes):
                gain_part[i, 0:1, :] = gain_row[:, i * depth : (i + 1) * depth]
            copies = []
            for mask in range(1, planes):
                copy = remote(
                    gain_part.at[jnp.bitwise_xor(here, mask)],
                    gain_box.at[mask],
                    gain_send.at[mask],
                    gain_recv.at[mask],
                    plane_device(mask),
                )
                copy.start()
                copies.append(copy)
            gain_total = gain_part[here]
            yield 1
            for mask in range(1, planes):
                arrived(gain_box.at[mask], gain_send.at[mask], gain_recv.at[mask])
                gain_total = gain_total + gain_box[mask]
            gain_held[...] = gain_total
            for mask in range(1, count):
                copy = remote(
                    gain_held,
                    gain_far.at[mask],
                    far_send.at[mask],
                    far_recv.at[mask],
                    {EXPERT_AXIS: jnp.bitwise_xor(place, mask)},
                )
                copy.start()
                copies.append(copy)
            yield 1
            for mask in range(1, count):
                arrived(gain_far.at[mask], far_send.at[mask], far_recv.at[mask])
                gain_total = gain_total + gain_far[mask]
            gains_out[...] = gain_total
            for copy in copies:
                copy.wait_send()
            reduce_finish()

        def first_task(task):
            yield from task
            copies = []

            def piece(mask):
                start = pl.multiple_of(jnp.bitwise_xor(place, mask) * thin, 8 if thin % 8 == 0 else thin)
                return results[0].at[pl.ds(start, thin), pl.ds(spread, columns - spread)]

            for mask in range(1, count):
                copy = remote(
                    piece(mask),
                    thin_box.at[mask],
                    thin_send.at[mask],
                    thin_recv.at[mask],
                    {EXPERT_AXIS: jnp.bitwise_xor(place, mask)},
                )
                copy.start()
                copies.append(copy)
            yield 1
            total = piece(0)[...]
            for mask in range(1, count):
                arrived(thin_box.at[mask], thin_send.at[mask], thin_recv.at[mask])
                total = total + thin_box[mask]
            thin_out[...] = total
            for copy in copies:
                copy.wait_send()

        size = len(rest) // number
        tasks = [
            plane_scatter_task(sources[i], results[i], *rest[size * i : size * (i + 1)])
            for i in range(number)
        ]
        tasks[0] = first_task(tasks[0])
        line = line_task()
        for stage in range(6):
            for task in tasks:
                next(task)
            if stage:
                next(line)
        run_tasks(line, *tasks)

    shapes = [
        jax.ShapeDtypeStruct((rows, width), jnp.float32),
        jax.ShapeDtypeStruct(gain_grads.shape[1:], jnp.float32),
        jax.ShapeDtypeStruct((thin, columns - spread), jnp.float32),
    ] + [jax.ShapeDtypeStruct((m.shape[0] // planes, m.shape[1]), jnp.float32) for m in matrices]
    scratch = [pltpu.VMEM((count + 1, rows, width), jnp.bfloat16)]
    scratch += line_semaphores()
    scratch += [
        pltpu.VMEM((1, width), jnp.float32),
        pltpu.VMEM(gain_grads.shape, jnp.float32),
        pltpu.VMEM(gain_grads.shape, jnp.float32),
        pltpu.SemaphoreType.DMA((planes,)),
        pltpu.SemaphoreType.DMA((planes,)),
        pltpu.VMEM(gain_grads.shape[1:], jnp.float32),
        pltpu.VMEM((count,) + gain_grads.shape[1:], jnp.float32),
        pltpu.SemaphoreType.DMA((count,)),
        pltpu.SemaphoreType.DMA((count,)),
        pltpu.VMEM((count, thin, columns - spread), jnp.float32),
        pltpu.SemaphoreType.DMA((count,)),
        pltpu.SemaphoreType.DMA((count,)),
    ]
    for m in matrices:
        scratch += plane_scatter_scratch(m.shape[0] // planes, m.shape[1])
    results = pl.pallas_call(
        kernel,
        out_shape=shapes,
        in_specs=[INSIDE, ANY] + [INSIDE] * 4 + [ANY] * number,
        out_specs=[INSIDE] * (3 + number),
        scratch_shapes=scratch,
        compiler_params=kernel_params(4),
        cost_estimate=pl.CostEstimate(
            flops=60_000_000, bytes_accessed=200_000_000, transcendentals=0
        ),
        name="closing",
    )(partial, ready_before, source, gain, grad_middle, gain_grads, *matrices)
    return results[:3], results[3:]


def silu_back(gate, up, grad):
    sigmoid_part = 1.0 / (1.0 + jnp.exp(-gate))
    silu_part = gate * sigmoid_part
    slope = sigmoid_part * (1.0 + gate * (1.0 - sigmoid_part))
    return silu_part * up, grad * up * slope, grad * silu_part


def row_copies(source, target, send, recv, copies):
    return [
        remote(source(k), target(k), send.at[k], recv.at[k], plane_device(k * copies))
        for k in (3, 1, 2)
    ]


def shared_and_rows(hidden, grads, weights, hidden_slots, grad_slots, gates, copies):
    tokens, width = hidden.shape
    columns = weights.shape[1] // 3
    pieces, slots = hidden_slots.shape[:2]
    exchanged = copies > 0
    tall = max(t for t in (256, 128, tokens) if tokens % t == 0)
    wide_part = 256

    def kernel(*refs):
        hidden_any, grads_any, weights_any, rows_any, grad_rows_any, gates_ref = refs[:6]
        act_out, back_out, weight_grads = refs[6:9]
        outputs = refs[9:12]
        scratch = refs[12:] if exchanged else refs[9:]
        hid, grd, wts, both, load = scratch[:5]
        loads = [
            pltpu.make_async_copy(hidden_any, hid, load.at[0]),
            pltpu.make_async_copy(weights_any, wts, load.at[1]),
            pltpu.make_async_copy(grads_any, grd, load.at[2]),
        ]
        moves = []
        if exchanged:
            semaphores = scratch[5:]
            meet([k * copies for k in (1, 2, 3)], False)
            for i, source in enumerate((gates_ref, rows_any, grad_rows_any)):
                moves += row_copies(
                    lambda k, source=source: source.at[k],
                    lambda k, i=i: outputs[i].at[k - 1],
                    semaphores[2 * i],
                    semaphores[2 * i + 1],
                    copies,
                )
            for move in moves:
                move.start()
        for copy in loads:
            copy.start()
        for copy in loads:
            copy.wait()

        def rows_tile(i, carry):
            span = pl.ds(pl.multiple_of(i * tall, 16), tall)
            gate = product(hid[span], wts[:, :columns])
            up = product(hid[span], wts[:, columns : 2 * columns])
            grad = product(grd[span], wts[:, 2 * columns :])
            act, dgate, dup = silu_back(gate, up, grad)
            act_out[span] = low(act)
            both[span, :columns] = low(dgate)
            both[span, columns:] = low(dup)
            back_out[span] = product_right(both[span], wts[:, : 2 * columns])
            return carry

        lax.fori_loop(0, tokens // tall, rows_tile, 0)

        def weights_tile(i, carry):
            span = pl.ds(pl.multiple_of(i * wide_part, wide_part), wide_part)
            weight_grads[span, : 2 * columns] = low(product_left(hid[:, span], both[...]))
            weight_grads[span, 2 * columns :] = low(product_left(grd[:, span], act_out[...]))
            return carry

        lax.fori_loop(0, width // wide_part, weights_tile, 0)
        for move in moves:
            move.wait()

    shapes = [
        jax.ShapeDtypeStruct((tokens, columns), jnp.bfloat16),
        jax.ShapeDtypeStruct((tokens, width), jnp.float32),
        jax.ShapeDtypeStruct(weights.shape, jnp.bfloat16),
    ]
    out_specs = [INSIDE] * 3
    scratch = [
        pltpu.VMEM(hidden.shape, jnp.bfloat16),
        pltpu.VMEM(grads.shape, jnp.bfloat16),
        pltpu.VMEM(weights.shape, jnp.bfloat16),
        pltpu.VMEM((tokens, 2 * columns), jnp.bfloat16),
        pltpu.SemaphoreType.DMA((3,)),
    ]
    if exchanged:
        shapes += [jax.ShapeDtypeStruct((3,) + x.shape[1:], x.dtype) for x in (gates, hidden_slots, grad_slots)]
        out_specs += [INSIDE, ANY, ANY]
        scratch += [pltpu.SemaphoreType.DMA((4,))] * 6
    results = pl.pallas_call(
        kernel,
        out_shape=shapes,
        in_specs=[ANY] * 5 + [INSIDE],
        out_specs=out_specs,
        scratch_shapes=scratch,
        compiler_params=kernel_params(5) if exchanged else pltpu.CompilerParams(vmem_limit_bytes=60 << 20),
        cost_estimate=pl.CostEstimate(
            flops=12 * tokens * width * columns, bytes_accessed=120_000_000, transcendentals=0
        ),
        name="shared_and_rows",
    )(hidden, grads, weights, hidden_slots, grad_slots, gates)
    return results[:3], results[3:]


def routed_expert(hidden_slots, grad_slots, hidden_far, grad_far, gates, weights, copies):
    slots, width = hidden_slots.shape[1:]
    gate_full, up_full, down_full = weights
    units = gate_full.shape[1]
    exchanged = copies > 0

    def kernel(*refs):
        far = 2 if exchanged else 0
        hidden_any, grad_any = refs[:2]
        hidden_far_any, grad_far_any = refs[2:4] if exchanged else (None, None)
        gates_ref, wg_any, wu_any, wd_any = refs[2 + far : 6 + far]
        pair_back, result_back, scale_back, dwg, dwu, dwd = refs[6 + far : 12 + far]
        scratch = refs[12 + far :]
        wg, wu, wd, hid, grd, act, dgate, dup, pair, result, scale = scratch[:11]
        tile_up, tile_down, load, own, store = scratch[11:16]
        semaphores = scratch[16:]

        def piece(ref, ref_far, k):
            return ref.at[k] if k == 0 or not exchanged else ref_far.at[k - 1]

        if exchanged:
            meet([k * copies for k in (1, 2, 3)], False)
        loads = {}

        def fetch(number, source, target):
            loads[number] = pltpu.make_async_copy(source, target, load.at[number])
            loads[number].start()

        fetch(0, wg_any, wg)
        for k in range(4):
            fetch(3 + k, piece(hidden_any, hidden_far_any, k), hid.at[pl.ds(k * slots, slots)])
        fetch(1, wu_any, wu)
        fetch(2, wd_any, wd)
        for k in range(4):
            fetch(7 + k, piece(grad_any, grad_far_any, k), grd.at[pl.ds(k * slots, slots)])
        for number in (0, 3, 4, 5, 6, 1, 2, 7, 8, 9, 10):
            loads[number].wait()

        def back(k, which):
            source, target = ((pair, pair_back), (result, result_back), (scale, scale_back))[which]
            return remote(
                source.at[k],
                target.at[k],
                semaphores[2 * which].at[k],
                semaphores[2 * which + 1].at[k],
                plane_device(k * copies),
            )

        def deliver(k, which):
            if exchanged:
                pl.when(k > 0)(lambda: back(k, which).start())

        def first(i, carry):
            k = 3 - i
            span = pl.ds(pl.multiple_of(k * slots, 16), slots)
            gate = product(hid[span], wg[...])
            up = product(hid[span], wu[...])
            grad = product_right(grd[span], wd[...])
            gates_here = gates_ref[span]
            act_part, dgate_part, dup_part = silu_back(gate, up, grad)
            scale[k] = jnp.broadcast_to(
                jnp.sum(act_part * grad, axis=-1, keepdims=True), scale.shape[1:]
            )
            act[span] = low(act_part * gates_here)
            dgate[span] = low(dgate_part * gates_here)
            dup[span] = low(dup_part * gates_here)
            pair[k] = low(product_right(dgate[span], wg[...]) + product_right(dup[span], wu[...]))
            deliver(k, 0)
            deliver(k, 2)
            return carry

        lax.fori_loop(0, 4, first, 0)

        def second(i, carry):
            k = 3 - i
            span = pl.ds(pl.multiple_of(k * slots, 16), slots)
            result[k] = low(product(act[span], wd[...]))
            deliver(k, 1)
            return carry

        lax.fori_loop(0, 4, second, 0)
        kept = []
        for which, (source, target) in enumerate(
            ((pair, pair_back), (result, result_back), (scale, scale_back))
        ):
            for k in range(1 if exchanged else 4):
                copy = pltpu.make_async_copy(source.at[k], target.at[k], own.at[which, k])
                copy.start()
                kept.append(copy)

        def tiles(count, rows, buffer, target, compute):
            def put(i, slot):
                start = pl.multiple_of(i * rows, 16)
                return pltpu.make_async_copy(
                    buffer.at[slot], target.at[pl.ds(start, rows)], store.at[slot]
                )

            def tile(i, carry):
                slot = lax.rem(i, 2)
                pl.when(i >= 2)(lambda: put(i - 2, slot).wait())
                buffer[slot] = compute(pl.ds(pl.multiple_of(i * rows, rows), rows))
                put(i, slot).start()
                return carry

            lax.fori_loop(0, count, tile, 0)
            for i in (count - 2, count - 1):
                put(i, i % 2).wait()

        tiles(width // 256, 256, tile_up, dwg, lambda s: low(product_left(hid[:, s], dgate[...])))
        tiles(width // 256, 256, tile_up, dwu, lambda s: low(product_left(hid[:, s], dup[...])))
        tiles(units // 128, 128, tile_down, dwd, lambda s: low(product_left(act[:, s], grd[...])))
        for copy in kept:
            copy.wait()
        if exchanged:
            for which in (0, 2, 1):
                for k in (3, 2, 1):
                    back(k, which).wait()

    shapes = [
        jax.ShapeDtypeStruct((4, slots, width), jnp.bfloat16),
        jax.ShapeDtypeStruct((4, slots, width), jnp.bfloat16),
        jax.ShapeDtypeStruct((4, slots, 128), jnp.float32),
    ] + [jax.ShapeDtypeStruct(w.shape, jnp.bfloat16) for w in weights]
    rows = 4 * slots
    scratch = [pltpu.VMEM(w.shape, jnp.bfloat16) for w in weights]
    scratch += [pltpu.VMEM((rows, width), jnp.bfloat16)] * 2
    scratch += [pltpu.VMEM((rows, units), jnp.bfloat16)] * 3
    scratch += [pltpu.VMEM((4, slots, width), jnp.bfloat16)] * 2
    scratch += [pltpu.VMEM((4, slots, 128), jnp.float32)]
    scratch += [
        pltpu.VMEM((2, 256, units), jnp.bfloat16),
        pltpu.VMEM((2, 128, width), jnp.bfloat16),
        pltpu.SemaphoreType.DMA((11,)),
        pltpu.SemaphoreType.DMA((3, 4)),
        pltpu.SemaphoreType.DMA((2,)),
    ]
    if exchanged:
        scratch += [pltpu.SemaphoreType.DMA((4,))] * 6
    operands = [hidden_slots, grad_slots] + ([hidden_far, grad_far] if exchanged else [])
    results = pl.pallas_call(
        kernel,
        out_shape=shapes,
        in_specs=[ANY] * len(operands) + [INSIDE] + [ANY] * 3,
        out_specs=[ANY] * 6,
        scratch_shapes=scratch,
        compiler_params=pltpu.CompilerParams(
            collective_id=6, has_side_effects=True, vmem_limit_bytes=60 << 20
        )
        if exchanged
        else pltpu.CompilerParams(vmem_limit_bytes=60 << 20),
        cost_estimate=pl.CostEstimate(
            flops=18 * rows * units * width, bytes_accessed=200_000_000, transcendentals=0
        ),
        name="routed_expert",
    )(*operands, gates, *weights)
    return results


def body(
    tokens,
    routes,
    grad_out,
    attn_gain,
    query_weight,
    latent_down,
    latent_gain,
    latent_up,
    out_weight,
    ffn_gain,
    router_weight,
    shared_gate,
    shared_up,
    shared_down,
    expert_gate,
    expert_up,
    expert_down,
):
    contexts = lax.axis_size(CONTEXT_AXIS)
    context_index = lax.axis_index(CONTEXT_AXIS)
    groups_local = lax.axis_size(EXPERT_AXIS)
    expert_index = lax.axis_index(EXPERT_AXIS)
    plane_count = lax.axis_size(PLANE)
    plane_index = lax.axis_index(PLANE)
    local_experts = expert_gate.shape[0]
    experts_all = router_weight.shape[1]
    copies = plane_count // local_experts
    expert_own = plane_index // copies
    query_cols = query_weight.shape[1]
    heads_local = query_cols // (NOPE + ROPE)
    down_cols = LATENT + ROPE
    shard_rows = query_weight.shape[0]
    latent_rows = latent_up.shape[0]
    prompt_len = PROMPT_DEV * contexts
    capacity = (TOK_DEV * TOPK * 9 + 8 * experts_all - 1) // (8 * experts_all)
    slots = groups_local * capacity
    slots = -(-slots // 16) * 16 if local_experts > 1 else -(-slots // 64) * 64
    token_count = groups_local * TOK_DEV
    score_scale = (NOPE + ROPE) ** (-0.5)

    used_cols = query_cols + down_cols
    extra_cols = experts_all + 3
    pad_cols = -(used_cols + extra_cols) % 128
    gains = jnp.stack(
        [
            wide(attn_gain),
            wide(ffn_gain),
            jnp.pad(wide(latent_gain), (0, shard_rows - latent_gain.shape[0])),
        ]
        + [jnp.zeros((shard_rows,), jnp.float32)] * 5
    )
    first_local = jnp.concatenate(
        [
            query_weight,
            latent_down,
            router_weight,
            jnp.zeros((shard_rows, 3 + pad_cols), jnp.bfloat16),
        ],
        axis=1,
    )
    gains_all, normed_all, (first_full, up_local, out_local) = opening(
        tokens[0], gains, [first_local, latent_up, out_weight.T]
    )
    full_router = first_full[:, used_cols : used_cols + experts_all]
    full_attn_gain = gains_all[:, 0].reshape(D)
    full_ffn_gain = gains_all[:, 1].reshape(D)
    full_latent_gain = gains_all[:, 2, : latent_gain.shape[0]].reshape(LATENT)

    within = jnp.arange(TOK_DEV, dtype=jnp.int32)
    query_places = jnp.where(
        within < PROMPT_DEV, context_index * PROMPT_DEV + within, prompt_len + within - PROMPT_DEV
    )
    key_places = jnp.arange(prompt_len + CONT_LEN, dtype=jnp.int32)
    allowed = key_places[None, :] <= query_places[:, None]
    cosine, sine_part = rotary_tables(query_places.astype(jnp.float32), ROPE // 2)
    cosine_heads = cosine[None, :, None, :]
    sine_heads = sine_part[None, :, None, :]
    source = wide(tokens[0])

    def pack_latent(comp_rows, latent_scale):
        return jnp.concatenate(
            [
                norm_rows(comp_rows[..., :LATENT], latent_scale),
                rotate(comp_rows[..., LATENT:], cosine[None], sine_part[None]),
            ],
            axis=-1,
        )

    grad_own, routes_own, _ = lax.optimization_barrier((grad_out[0], routes[0], gains_all))
    grad_all = axis_gather(grad_own, EXPERT_AXIS)
    routes_all = axis_gather(routes_own, EXPERT_AXIS)
    first_product = product(normed_all, first_full)
    compressed = first_product[..., query_cols:used_cols]
    packed = low(pack_latent(compressed, wide(full_latent_gain)))
    prompt_keys = axis_gather(packed[:, :PROMPT_DEV], CONTEXT_AXIS)
    cont_keys = packed[:, PROMPT_DEV:]
    query_raw = first_product[..., :query_cols].reshape(
        groups_local, TOK_DEV, heads_local, NOPE + ROPE
    )
    query_rows = low(
        jnp.concatenate(
            [query_raw[..., :NOPE], rotate(query_raw[..., NOPE:], cosine_heads, sine_heads)], axis=-1
        )
    )
    query_nope = query_rows[..., :NOPE]
    query_rope = query_rows[..., NOPE:]
    prompt_latent = prompt_keys[..., :LATENT]
    prompt_rope = prompt_keys[..., LATENT:]
    cont_latent = cont_keys[..., :LATENT]
    cont_rope = cont_keys[..., LATENT:]
    prompt_exp = low(product(prompt_latent, up_local)).reshape(
        contexts, groups_local, PROMPT_DEV, heads_local, NOPE + VDIM
    )
    cont_exp = low(product(cont_latent, up_local)).reshape(
        groups_local, CONT_LEN, heads_local, NOPE + VDIM
    )
    prompt_knope = prompt_exp[..., :NOPE]
    prompt_values = prompt_exp[..., NOPE:]
    cont_knope = cont_exp[..., :NOPE]
    cont_values = cont_exp[..., NOPE:]

    def split_keys(values):
        return (
            values[..., :prompt_len].reshape(
                groups_local, heads_local, TOK_DEV, contexts, PROMPT_DEV
            ),
            values[..., prompt_len:],
        )

    def score_all():
        prompt_part = jnp.einsum(
            "gqhd,cgphd->ghqcp", query_nope, prompt_knope, preferred_element_type=jnp.float32
        )
        prompt_part = prompt_part + jnp.einsum(
            "gqhd,cgpd->ghqcp", query_rope, prompt_rope, preferred_element_type=jnp.float32
        )
        prompt_part = prompt_part.reshape(groups_local, heads_local, TOK_DEV, prompt_len)
        cont_part = jnp.einsum(
            "gqhd,gphd->ghqp", query_nope, cont_knope, preferred_element_type=jnp.float32
        )
        cont_part = cont_part + jnp.einsum(
            "gqhd,gpd->ghqp", query_rope, cont_rope, preferred_element_type=jnp.float32
        )
        raw_scores = jnp.concatenate([prompt_part, cont_part], axis=-1)
        return jnp.where(allowed, raw_scores * score_scale, -1e30)

    scores = score_all()
    top_score = jnp.max(scores, axis=-1, keepdims=True)
    exp_scores = jnp.exp(scores - top_score)
    totals = jnp.sum(exp_scores, axis=-1, keepdims=True)
    probs_all = exp_scores / totals
    probs_low = low(probs_all)
    probs_prompt, probs_cont = split_keys(probs_low)
    mixed_rows = jnp.einsum(
        "ghqcp,cgphd->gqhd", probs_prompt, prompt_values, preferred_element_type=jnp.float32
    )
    mixed_rows = mixed_rows + jnp.einsum(
        "ghqp,gphd->gqhd", probs_cont, cont_values, preferred_element_type=jnp.float32
    )
    mixed_all = low(mixed_rows.reshape(groups_local, TOK_DEV, heads_local * VDIM))
    partial_sum = against_rows(mixed_all, out_local)
    shared_cols = shared_gate.shape[1]
    shared_pad = -(-shared_cols // 128) * 128

    def padded(weight):
        return jnp.pad(weight, ((0, 0), (0, shared_pad - shared_cols)))

    shared_own, _ = lax.optimization_barrier(
        (
            jnp.concatenate(
                [padded(shared_gate), padded(shared_up), padded(shared_down.T)], axis=1
            ),
            gains_all,
        )
    )
    shared_whole = lax.all_gather(shared_own, PLANE, axis=0, tiled=True)
    grad_flat = grad_all.reshape(token_count, D)
    slot_experts = expert_index * local_experts + (
        expert_own ^ jnp.arange(local_experts, dtype=jnp.int32)
    )
    expert_cols = jnp.arange(experts_all, dtype=jnp.int32)[:, None] == slot_experts[None, :]
    chosen_slots = jnp.any(routes_all[..., None] == slot_experts, axis=2)
    before = (within[:, None] > within[None, :]).astype(jnp.bfloat16)
    rank = jnp.einsum(
        "ts,gsl->gtl",
        before,
        chosen_slots.astype(jnp.bfloat16),
        preferred_element_type=jnp.float32,
    ).astype(jnp.int32)
    slot_of = jnp.where(
        chosen_slots,
        rank + capacity * jnp.arange(groups_local, dtype=jnp.int32)[:, None, None],
        -1,
    ).reshape(token_count, local_experts)
    picked = (
        slot_of.T[:, None, :] == jnp.arange(slots, dtype=jnp.int32)[None, :, None]
    )
    picked_low = picked.astype(jnp.bfloat16).reshape(local_experts * slots, token_count)
    piece_slots = slots * local_experts // 4
    grad_slots = low(product(picked_low, grad_flat)).reshape(4, piece_slots, D)
    middle, hidden_all, _, (gate_full, up_full, down_full) = middle_sum(
        low(partial_sum),
        tokens[0],
        full_ffn_gain[None],
        [],
        [expert_gate, expert_up, expert_down],
        grad_slots,
    )
    hidden_flat = hidden_all.reshape(token_count, D)

    hidden_slots = low(product(picked_low, hidden_flat)).reshape(4, piece_slots, D)
    logits = product(hidden_flat, full_router)
    expert_probs = jax.nn.softmax(logits, axis=-1)
    gate_tokens = jnp.sum(jnp.where(expert_cols[None], expert_probs[:, :, None], 0.0), axis=1)
    gate_slots = jnp.sum(jnp.where(picked, gate_tokens.T[:, None, :], 0.0), axis=-1)
    gate_slots = gate_slots.reshape(4, piece_slots)
    gates_padded = jnp.broadcast_to(
        jnp.pad(gate_slots, ((0, 0), (0, -piece_slots % 128)))[:, None], (4, 8, -(-piece_slots // 128) * 128)
    )
    row_hops = copies if local_experts > 1 else 0
    (act_shared, shared_hidden, shared_grads), far = shared_and_rows(
        hidden_flat, grad_flat, shared_whole, hidden_slots, grad_slots, gates_padded, row_hops
    )
    gates_far, hidden_far, grad_far = far if far else (None, None, None)
    if far:
        gate_slots = jnp.concatenate([gate_slots[:1], gates_far[:, 0, :piece_slots]], axis=0)
    pair_back, result, scale_back, *expert_partials = routed_expert(
        hidden_slots,
        grad_slots,
        hidden_far,
        grad_far,
        gate_slots.reshape(-1, 1),
        [gate_full, up_full, down_full],
        row_hops,
    )
    grad_gate_back = scale_back[:, :, 0].reshape(local_experts, slots)
    grad_routed = product_left(picked_low, pair_back.reshape(-1, D))
    grad_gate_tokens = jnp.sum(jnp.where(picked, grad_gate_back[:, :, None], 0.0), axis=1).T
    grad_spread = jnp.sum(
        jnp.where(expert_cols[None], grad_gate_tokens[:, None, :], 0.0), axis=-1
    )
    weighted = jnp.sum(expert_probs * grad_spread, axis=-1, keepdims=True)
    grad_logits = expert_probs * (grad_spread - weighted)
    grad_router = lax.dot_general(
        grad_logits,
        wide(hidden_flat),
        (((0,), (0,)), ((), ())),
        precision=lax.Precision.HIGHEST,
    )
    grad_from_router = lax.dot_general(
        grad_logits,
        wide(full_router),
        (((1,), (1,)), ((), ())),
        precision=lax.Precision.HIGHEST,
    )
    grad_hidden_part = low(
        shared_hidden + grad_routed + grad_from_router
    )
    grad_middle, grad_ffn_gain, branch_all, expert_grads, (result, shared_grads) = branch_sum(
        grad_hidden_part.reshape(groups_local, TOK_DEV, D),
        middle,
        full_ffn_gain[None],
        grad_out[0],
        expert_partials,
        local_experts,
        [result.reshape(-1, D), shared_grads],
    )
    shared_grads = wide(lax.psum_scatter(shared_grads, PLANE, scatter_dimension=0, tiled=True))
    routed_term = product_left(picked_low, result)
    branch_out = low(
        product_right(act_shared, shared_whole[:, 2 * shared_pad :]) + routed_term
    )
    grad_out_weight = low(
        product_left(
            branch_all.reshape(token_count, D), mixed_all.reshape(token_count, heads_local * VDIM)
        )
    )
    grad_mixed = low(product(branch_all, out_local)).reshape(
        groups_local, TOK_DEV, heads_local, VDIM
    )
    grad_probs_prompt = jnp.einsum(
        "gqhd,cgphd->ghqcp", grad_mixed, prompt_values, preferred_element_type=jnp.float32
    )
    grad_probs_cont = jnp.einsum(
        "gqhd,gphd->ghqp", grad_mixed, cont_values, preferred_element_type=jnp.float32
    )
    grad_probs = jnp.concatenate(
        [
            grad_probs_prompt.reshape(groups_local, heads_local, TOK_DEV, prompt_len),
            grad_probs_cont,
        ],
        axis=-1,
    )
    delta_rows = jnp.sum(probs_all * grad_probs, axis=-1, keepdims=True)
    grad_raw = low(probs_all * (grad_probs - delta_rows) * score_scale)
    raw_prompt, raw_cont = split_keys(grad_raw)
    value_prompt = jnp.einsum(
        "ghqcp,gqhd->cgphd", probs_prompt, grad_mixed, preferred_element_type=jnp.float32
    )
    value_cont = jnp.einsum(
        "ghqp,gqhd->gphd", probs_cont, grad_mixed, preferred_element_type=jnp.float32
    )
    knope_prompt = jnp.einsum(
        "ghqcp,gqhd->cgphd", raw_prompt, query_nope, preferred_element_type=jnp.float32
    )
    knope_cont = jnp.einsum(
        "ghqp,gqhd->gphd", raw_cont, query_nope, preferred_element_type=jnp.float32
    )
    krope_prompt = jnp.einsum(
        "ghqcp,gqhd->cgpd", raw_prompt, query_rope, preferred_element_type=jnp.float32
    )
    krope_cont = jnp.einsum(
        "ghqp,gqhd->gpd", raw_cont, query_rope, preferred_element_type=jnp.float32
    )
    grad_query_nope = jnp.einsum(
        "ghqcp,cgphd->gqhd", raw_prompt, prompt_knope, preferred_element_type=jnp.float32
    )
    grad_query_nope = grad_query_nope + jnp.einsum(
        "ghqp,gphd->gqhd", raw_cont, cont_knope, preferred_element_type=jnp.float32
    )
    grad_query_rope = jnp.einsum(
        "ghqcp,cgpd->gqhd", raw_prompt, prompt_rope, preferred_element_type=jnp.float32
    )
    grad_query_rope = grad_query_rope + jnp.einsum(
        "ghqp,gpd->gqhd", raw_cont, cont_rope, preferred_element_type=jnp.float32
    )
    grad_query_raw = jnp.concatenate(
        [grad_query_nope, rotate(grad_query_rope, cosine_heads, -sine_heads)], axis=-1
    )
    grad_query_raw = low(
        grad_query_raw.reshape(groups_local, TOK_DEV, heads_local * (NOPE + ROPE))
    )
    grad_exp_prompt = low(
        jnp.concatenate([knope_prompt, value_prompt], axis=-1).reshape(
            contexts, groups_local, PROMPT_DEV, heads_local * (NOPE + VDIM)
        )
    )
    grad_exp_cont = low(
        jnp.concatenate([knope_cont, value_cont], axis=-1).reshape(
            groups_local, CONT_LEN, heads_local * (NOPE + VDIM)
        )
    )
    latent_prompt = jnp.einsum(
        "cgpf,lf->cgpl", grad_exp_prompt, up_local, preferred_element_type=jnp.float32
    )
    latent_cont = jnp.einsum(
        "gpf,lf->gpl", grad_exp_cont, up_local, preferred_element_type=jnp.float32
    )
    grad_prompt_keys = jnp.concatenate([latent_prompt, krope_prompt], axis=-1)
    grad_cont_keys = jnp.concatenate([latent_cont, krope_cont], axis=-1)
    prompt_sum = axis_scatter(grad_prompt_keys, CONTEXT_AXIS)
    grad_packed = jnp.concatenate([prompt_sum, grad_cont_keys], axis=1)
    _, pack_back = jax.vjp(pack_latent, compressed, wide(full_latent_gain))
    grad_compressed, grad_latent_gain = pack_back(grad_packed)
    grad_first = jnp.concatenate(
        [
            grad_query_raw,
            low(grad_compressed),
            jnp.zeros((groups_local, TOK_DEV, first_full.shape[1] - used_cols), jnp.bfloat16),
        ],
        axis=-1,
    )
    grad_normed_part = low(against_rows(grad_first, first_full))

    grad_latent_up = jnp.einsum(
        "cgpl,cgpf->lf", prompt_latent, grad_exp_prompt, preferred_element_type=jnp.float32
    )
    grad_latent_up = grad_latent_up + jnp.einsum(
        "gpl,gpf->lf", cont_latent, grad_exp_cont, preferred_element_type=jnp.float32
    )
    first_back = product_left(
        normed_all.reshape(token_count, D), grad_first.reshape(token_count, first_full.shape[1])
    )
    gain_rows = jnp.concatenate(
        [
            jnp.zeros((plane_count, 1, shard_rows), jnp.float32),
            grad_ffn_gain.reshape(plane_count, 1, shard_rows),
            jnp.pad(
                grad_latent_gain.reshape(plane_count, 1, latent_rows),
                ((0, 0), (0, 0), (0, shard_rows - latent_rows)),
            ),
            grad_router.reshape(experts_all, plane_count, shard_rows).transpose(1, 0, 2),
            jnp.zeros((plane_count, -(3 + experts_all) % 8, shard_rows), jnp.float32),
        ],
        axis=1,
    )
    block_out = low(
        middle + axis_scatter(branch_out.reshape(groups_local, TOK_DEV, D), EXPERT_AXIS)
    )
    (grad_tokens, gain_sum, down_own), sums = closing(
        grad_normed_part,
        block_out,
        tokens[0],
        full_attn_gain[None],
        grad_middle,
        gain_rows,
        [low(first_back), low(grad_latent_up), grad_out_weight],
        query_cols // 128 * 128,
    )
    first_sum, up_sum, out_sum = sums
    small_rows = shard_rows // groups_local
    small_own = lax.dynamic_slice_in_dim(gain_sum, expert_index * small_rows, small_rows, 1)
    latent_small = latent_rows // groups_local
    latent_own = lax.dynamic_slice_in_dim(gain_sum[2], expert_index * latent_small, latent_small, 0)
    down_start = query_cols % 128
    return (
        block_out[None],
        grad_tokens[None],
        small_own[0],
        first_sum[:, :query_cols],
        down_own[:, down_start : down_start + down_cols],
        latent_own,
        up_sum,
        out_sum.T,
        small_own[1],
        small_own[3 : 3 + experts_all].T,
        shared_grads[:, :shared_cols],
        shared_grads[:, shared_pad : shared_pad + shared_cols],
        shared_grads[:, 2 * shared_pad : 2 * shared_pad + shared_cols].T,
        *expert_grads,
    )


def solution(mesh):
    in_specs = (
        P((DP_AXIS, EXPERT_AXIS), CONTEXT_AXIS, None),
        P((DP_AXIS, EXPERT_AXIS), CONTEXT_AXIS, None),
        P((DP_AXIS, EXPERT_AXIS), CONTEXT_AXIS, None),
        P((DP_AXIS, CONTEXT_AXIS)),
        P((DP_AXIS, CONTEXT_AXIS), EXPERT_AXIS),
        P((DP_AXIS, CONTEXT_AXIS), None),
        P((DP_AXIS, CONTEXT_AXIS)),
        P((DP_AXIS, CONTEXT_AXIS), EXPERT_AXIS),
        P(EXPERT_AXIS, (DP_AXIS, CONTEXT_AXIS)),
        P((DP_AXIS, CONTEXT_AXIS)),
        P((DP_AXIS, CONTEXT_AXIS), None),
        P((DP_AXIS, CONTEXT_AXIS), EXPERT_AXIS),
        P((DP_AXIS, CONTEXT_AXIS), EXPERT_AXIS),
        P(EXPERT_AXIS, (DP_AXIS, CONTEXT_AXIS)),
        P(EXPERT_AXIS, (DP_AXIS, CONTEXT_AXIS), None),
        P(EXPERT_AXIS, (DP_AXIS, CONTEXT_AXIS), None),
        P(EXPERT_AXIS, (DP_AXIS, CONTEXT_AXIS), None),
    )
    out_specs = (
        P((DP_AXIS, EXPERT_AXIS), CONTEXT_AXIS, None),
        P((DP_AXIS, EXPERT_AXIS), CONTEXT_AXIS, None),
        P((DP_AXIS, CONTEXT_AXIS, EXPERT_AXIS)),
        P((DP_AXIS, CONTEXT_AXIS), EXPERT_AXIS),
        P((DP_AXIS, CONTEXT_AXIS, EXPERT_AXIS), None),
        P((DP_AXIS, CONTEXT_AXIS, EXPERT_AXIS)),
        P((DP_AXIS, CONTEXT_AXIS), EXPERT_AXIS),
        P(EXPERT_AXIS, (DP_AXIS, CONTEXT_AXIS)),
        P((DP_AXIS, CONTEXT_AXIS, EXPERT_AXIS)),
        P((DP_AXIS, CONTEXT_AXIS, EXPERT_AXIS), None),
        P((DP_AXIS, CONTEXT_AXIS), EXPERT_AXIS),
        P((DP_AXIS, CONTEXT_AXIS), EXPERT_AXIS),
        P(EXPERT_AXIS, (DP_AXIS, CONTEXT_AXIS)),
        P(EXPERT_AXIS, (DP_AXIS, CONTEXT_AXIS), None),
        P(EXPERT_AXIS, (DP_AXIS, CONTEXT_AXIS), None),
        P(EXPERT_AXIS, (DP_AXIS, CONTEXT_AXIS), None),
    )
    return jax.shard_map(body, mesh=mesh, in_specs=in_specs, out_specs=out_specs, check_vma=False)
```

time: 1300 us -> 765 us (0.59)
  waiting for transfers between devices: 590 us -> 10.7 us
  Pallas kernels: 0 us -> 525 us
  starting transfers between devices: 188 us -> 14.5 us
  local copies, waits for them, and re-layouts: 241 us -> 80.9 us
  matrix products: 188 us -> 77.3 us
  other arithmetic: 85.9 us -> 31.3 us
    ppermute x179 -> x15, waiting for transfers between devices: 590 us -> 10.7 us  [swap(): return lax.ppermute(values, axis, [(i, i ^ mask) for i in range(count)])]
    pallas_call x0 -> x6, Pallas kernels: none -> 525 us  [the longest x1 111 us: middle_sum(): pl.pallas_call(kernel, out_shape=shapes, in_specs=[INSIDE] * (3 + number)...]
    ppermute x179 -> x15, starting transfers between devices: 188 us -> 14.4 us  [swap(): return lax.ppermute(values, axis, [(i, i ^ mask) for i in range(count)])]
    dynamic_update_slice x80 -> x11, local copies, waits for them, and re-layouts: 56.9 us -> 16.4 us  [place_pieces(): lax.dynamic_update_slice(whole, piece[None], (index ^ mask,) + (0,) * fir...]
    dot_general x5 -> x1, matrix products: 43.3 us -> 4.15 us  [product_right(): lax.dot_general(left_side, right_side, (((1,), (1,)), ((), ())), preferre...]
    dot_general x9 -> x4, matrix products: 46.2 us -> 13.3 us  [product_left(): lax.dot_general(left_side, right_side, (((0,), (0,)), ((), ())), preferre...]
    dot_general x12 -> x7, matrix products: 58 us -> 25.3 us  [product(): return jnp.dot(left_side, right_side, preferred_element_type=jnp.float32)]
    dynamic_slice x11 -> x1, local copies, waits for them, and re-layouts: 25.5 us -> 0.58 us  [body(): lax.dynamic_slice_in_dim(gain_sum[2], expert_index * latent_small, latent...]
  transfers between devices with their start and end apart: 179 -> 17, of which waited for: 64 -> 3; matrix products, arithmetic and copies ran while one was open for 35% -> 20% of each run, Pallas kernels for 0% -> 24%
where the time goes in v1:
time: 765 us; the launch traced here: 756 us
  Pallas kernels  525 us (69%)
  local copies, waits for them, and re-layouts  80.9 us (11%)
  matrix products  77.3 us (10%)
  other arithmetic  31.3 us (4%)
  between operations  15.9 us (2%)
  starting transfers between devices  14.5 us (2%)
  waiting for transfers between devices  10.7 us (1%)
    pallas_call x1, Pallas kernels, middle_sum(): pl.pallas_call(kernel, out_shape=shapes, in_specs=[INSIDE] * (3 + number)...  111 us
    pallas_call x1, Pallas kernels, routed_expert(): pl.pallas_call(kernel, out_shape=shapes, in_specs=[ANY] * len(operands) +...  105 us
    pallas_call x1, Pallas kernels, branch_sum(): pl.pallas_call(kernel, out_shape=shapes, in_specs=[INSIDE] * 4 + [ANY] *...  104 us
    pallas_call x1, Pallas kernels, shared_and_rows(): pl.pallas_call(kernel, out_shape=shapes, in_specs=[ANY] * 5 + [INSIDE], o...  88.6 us
    pallas_call x1, Pallas kernels, closing(): pl.pallas_call(kernel, out_shape=shapes, in_specs=[INSIDE, ANY] + [INSIDE...  69.1 us
    pallas_call x1, Pallas kernels, opening(): pl.pallas_call(kernel, out_shape=shapes, in_specs=[INSIDE] * (2 + number)...  47.3 us
    dot_general x7, matrix products, product(): return jnp.dot(left_side, right_side, preferred_element_type=jnp.float32)  25.3 us
    unnamed x225, local copies, waits for them, and re-layouts  23.8 us
  transfers between devices with their start and end apart: 17, of which 3 were waited for; matrix products, arithmetic and copies ran while one was open for 20% of the time, Pallas kernels for 24%

profile of v1, /device:TPU:0, one launch (start us, length us, event | category | flops | bytes accessed | tf_op | source)
XLA Modules:
  0.0 755.8 jit_solution(12024721274205377446)
XLA Ops:
  15.5 47.3 %opening.1 = (f32[8,8,256]{2,1,0:T(8,128)S(1)}, bf16[4,128,2048]{2,1,0:T(8,128)(2,1)}, bf16[2048,1408]{1,0:T(8,128)(2,1)}, bf16[512,1024]{1,0:T(8,128)(2,1)}, bf16[2048,512]{1,0:T(8,128)(2,1)}) custom-call(bf16[128,2048]{1,0:T(8,128)(2,1)S(1)} %bitcast.284, f32[8,256]{1,0:T(8,128)S(1)} %stack.31.refs_1_, bf16[256,1408]{1,0:T(8,128)(2,1)S(1)} %concatenate.54.refs_2_, ...), custom_call_target="tpu_custom_call" | custom-call | flops 60000000 | bytes 150000000 | tf_op jit(solution)/shard_map/opening/pallas_call | solution.py:524
  64.6 6.4 fusion.4
  97.6 2.8 collective-permute-done.5
  109.9 3.8 convolution_convert_fusion.3
  113.7 4.8 reshape.385
  131.2 7.5 collective-permute-done.7
  142.5 5.5 convolution_convert_fusion.1
  148.0 111.0 %middle_sum.1 = (f32[128,2048]{1,0:T(8,128)S(1)}, bf16[4,128,2048]{2,1,0:T(8,128)(2,1)}, bf16[2048,1408]{1,0:T(8,128)(2,1)}, bf16[2048,1408]{1,0:T(8,128)(2,1)}, bf16[1408,2048]{1,0:T(8,128)(2,1)}) custom-call(bf16[4,128,2048]{2,1,0:T(8,128)(2,1)} %convolution_convert_fusion.2.refs_0_, bf16[128,2048]{1,0:T(8,128)(2,1)S(1)} %bitcast.285, ...), custom_call_target="tpu_custom_call" | custom-call | flops 60000000 | bytes 300000000 | tf_op jit(solution)/shard_map/middle_sum/pallas_call | solution.py:616
  263.2 3.9 convolution_convert_fusion
  267.1 88.6 %shared_and_rows.1 = (bf16[512,768]{1,0:T(8,128)(2,1)S(1)}, f32[512,2048]{1,0:T(8,128)}, bf16[2048,2304]{1,0:T(8,128)(2,1)}, f32[3,8,256]{2,1,0:T(8,128)S(1)}, b...) custom-call(bf16[512,2048]{1,0:T(8,128)(2,1)} %bitcast.312, bf16[512,2048]{1,0:T(8,128)(2,1)} %bitcast.45.refs_1_, ...), custom_call_target="tpu_custom_call" | custom-call | flops 9663676416 | bytes 120000000 | tf_op jit(solution)/shard_map/shared_and_rows/pallas_call | solution.py:1126
  356.9 105.2 %routed_expert.1 = (bf16[4,224,2048]{2,1,0:T(8,128)(2,1)}, bf16[4,224,2048]{2,1,0:T(8,128)(2,1)}, f32[4,224,128]{2,1,0:T(8,128)}, bf16[2048,1408]{1,0:T(8,128)(2...) custom-call(bf16[4,224,2048]{2,1,0:T(8,128)(2,1)} %bitcast.341, bf16[4,224,2048]{2,1,0:T(8,128)(2,1)} %bitcast.319, ...), custom_call_target="tpu_custom_call" | custom-call | flops 46506442752 | bytes 200000000 | tf_op jit(solution)/shard_map/routed_expert/pallas_call | solution.py:1280
  463.9 3.3 fusion.85
  472.1 103.9 %branch_sum.1 = (f32[128,2048]{1,0:T(8,128)S(1)}, f32[1,2048]{1,0:T(1,128)S(1)}, bf16[4,128,2048]{2,1,0:T(8,128)(2,1)}, bf16[4,256,1408]{2,1,0:T(8,128)(2,1)}, b...) custom-call(bf16[4,128,2048]{2,1,0:T(8,128)(2,1)} %bitcast.307, ...), custom_call_target="tpu_custom_call", output_to_operand_aliasing={{6}: (7, {}), {7}: (8, {})} | custom-call | flops 60000000 | bytes 300000000 | tf_op jit(solution)/shard_map/branch_sum/pallas_call | solution.py:852
  577.4 4.3 copy.261
  581.8 4.2 fusion.8
  605.2 2.9 convert_element_type.176
  609.4 3.3 fusion.52
  621.3 2.7 bitcast_convert_fusion.1.refs_8_
  627.5 4.9 convert_element_type.193
  632.3 2.9 convert_element_type.194
  635.3 3.3 convert_element_type.195
  652.6 7.4 fusion.10.refs_0_
  660.0 5.5 bitcast_convert_fusion.refs_6_
  667.6 69.1 %closing.1 = (f32[128,2048]{1,0:T(8,128)}, f32[24,256]{1,0:T(8,128)S(1)}, f32[64,640]{1,0:T(8,128)S(1)}, f32[256,1408]{1,0:T(8,128)}, f32[64,1024]{1,0:T(8,128)S(1)}, /*index=5*/f32[256,512]{1,0:T(8,128)S(1)}) custom-call(bf16[4,128,2048]{2,1,0:T(8,128)(2,1)} %fusion.10.refs_0_, bf16[128,2048]{1,0:T(8,128)(2,1)S(1)} %fusion.51.refs_1_, ...), custom_call_target="tpu_custom_call" | custom-call | flops 60000000 | bytes 200000000 | tf_op jit(solution)/shard_map/closing/pallas_call | solution.py:1018
  (398 shorter events, 135.3 us)
Async XLA Ops:
  7.2 259.9 %all-gather.2.cloned.1.call-start = ((), (), s32[]{:S(2)}) async-start(), calls=%async_computation.1 | async-start | bytes 10616832 | tf_op jit(solution)/shard_map/all_gather | solution.py:1475
  62.8 678.7 %reduce-scatter.2.cloned.1.call-start = ((), (), s32[]{:S(2)}) async-start(), calls=%async_computation.2 | async-start | bytes 10616832 | tf_op jit(solution)/shard_map/reduce_scatter | solution.py:1567
  74.7 29.3 %collective-permute-start = (bf16[4,64,576]{2,1,0:T(8,128)(2,1)}, bf16[4,64,576]{2,1,0:T(8,128)(2,1)}, u32[]{:S(2)}, u32[]{:S(2)}) collective-permute-start(bf16[4,64,576]{2,1,0:T(8,128)(2,1)} %get-tuple-element.180), channel_id=1, source_target_pairs={{0,4},{4,0},{8,12},{12,8},{1,5},{5,1},{9,13},{13,9},{2,6},{6,2},{1... | collective-permute-start | bytes 884744 | tf_op jit(solution)/shard_map/ppermute | solution.py:79
  75.1 31.3 %collective-permute-start.1 = (bf16[4,64,576]{2,1,0:T(8,128)(2,1)}, bf16[4,64,576]{2,1,0:T(8,128)(2,1)}, u32[]{:S(2)}, u32[]{:S(2)}) collective-permute-start(bf16[4,64,576]{2,1,0:T(8,128)(2,1)} %get-tuple-element.180), channel_id=1, source_target_pairs={{0,8},{4,12},{8,0},{12,4},{1,9},{5,13},{9,1},{13,5},{2,10},{6,14},... | collective-permute-start | bytes 884744 | tf_op jit(solution)/shard_map/ppermute | solution.py:79
  76.3 31.9 %collective-permute-start.2 = (bf16[4,64,576]{2,1,0:T(8,128)(2,1)}, bf16[4,64,576]{2,1,0:T(8,128)(2,1)}, u32[]{:S(2)}, u32[]{:S(2)}) collective-permute-start(bf16[4,64,576]{2,1,0:T(8,128)(2,1)} %get-tuple-element.180), channel_id=1, source_target_pairs={{0,12},{4,8},{8,4},{12,0},{1,13},{5,9},{9,5},{13,1},{2,14},{6,10},... | collective-permute-start | bytes 884744 | tf_op jit(solution)/shard_map/ppermute | solution.py:79
  77.3 16.4 %collective-permute-start.3 = (s32[128,6]{1,0:T(8,128)}, s32[128,6]{1,0:T(8,128)}, u32[]{:S(2)}, u32[]{:S(2)}) collective-permute-start(s32[128,6]{1,0:T(8,128)} %bitcast.31), channel_id=1, source_target_pairs={{0,1},{1,0},{2,3},{3,2},{4,5},{5,4},{6,7},{7,6},{8,9},{9,8},{10,11... | collective-permute-start | bytes 9224 | tf_op jit(solution)/shard_map/ppermute | solution.py:79
  78.6 17.1 %collective-permute-start.4 = (s32[128,6]{1,0:T(8,128)}, s32[128,6]{1,0:T(8,128)}, u32[]{:S(2)}, u32[]{:S(2)}) collective-permute-start(s32[128,6]{1,0:T(8,128)} %bitcast.31), channel_id=1, source_target_pairs={{0,2},{1,3},{2,0},{3,1},{4,6},{5,7},{6,4},{7,5},{8,10},{9,11},{10,... | collective-permute-start | bytes 9224 | tf_op jit(solution)/shard_map/ppermute | solution.py:79
  87.6 175.1 %copy-start.97 = (pred[16,4]{0,1:T(4,128)(4,1)}, pred[16,4]{0,1:T(4,128)(4,1)S(1)}, u32[]{:S(2)}) copy-start(pred[16,4]{0,1:T(4,128)(4,1)S(1)} %iota_compare_fusion.8) | copy-start | bytes 196
  93.7 6.6 collective-permute-start.5
  95.7 33.5 %collective-permute-start.6 = (bf16[128,2048]{1,0:T(8,128)(2,1)S(1)}, bf16[128,2048]{1,0:T(8,128)(2,1)}, u32[]{:S(2)}, u32[]{:S(2)}) collective-permute-start(bf16[128,2048]{1,0:T(8,128)(2,1)S(1)} %bitcast.287), channel_id=1, source_target_pairs={{0,1},{1,0},{2,3},{3,2},{4,5},{5,4},{6,7},{7,6},{8,9},{9,8},{10,11... | collective-permute-start | bytes 1572872 | tf_op jit(solution)/shard_map/ppermute | solution.py:79
  100.3 38.3 %collective-permute-start.7 = (bf16[128,2048]{1,0:T(8,128)(2,1)S(1)}, bf16[128,2048]{1,0:T(8,128)(2,1)}, u32[]{:S(2)}, u32[]{:S(2)}) collective-permute-start(bf16[128,2048]{1,0:T(8,128)(2,1)S(1)} %bitcast.288), channel_id=1, source_target_pairs={{0,2},{1,3},{2,0},{3,1},{4,6},{5,7},{6,4},{7,5},{8,10},{9,11},{10,... | collective-permute-start | bytes 1572872 | tf_op jit(solution)/shard_map/ppermute | solution.py:79
  103.0 159.9 %copy-start.78 = (s32[4,512]{1,0:T(4,128)}, s32[4,512]{1,0:T(4,128)S(1)}, u32[]{:S(2)}) copy-start(s32[4,512]{1,0:T(4,128)S(1)} %fusion.47) | copy-start | bytes 24580
  104.0 36.5 %collective-permute-start.8 = (bf16[128,2048]{1,0:T(8,128)(2,1)S(1)}, bf16[128,2048]{1,0:T(8,128)(2,1)}, u32[]{:S(2)}, u32[]{:S(2)}) collective-permute-start(bf16[128,2048]{1,0:T(8,128)(2,1)S(1)} %bitcast.289), channel_id=1, source_target_pairs={{0,3},{1,2},{2,1},{3,0},{4,7},{5,6},{6,5},{7,4},{8,11},{9,10},{10,... | collective-permute-start | bytes 1572872 | tf_op jit(solution)/shard_map/ppermute | solution.py:79
  262.7 201.1 %copy-start.61 = (f32[512,16]{0,1:T(8,128)}, f32[512,16]{0,1:T(8,128)S(1)}, u32[]{:S(2)}) copy-start(f32[512,16]{0,1:T(8,128)S(1)} %fusion.119) | copy-start | bytes 98308
  267.1 88.7 %slice-start = ((f32[4,224]{1,0:T(4,128)}), f32[1,224]{1,0:T(1,128)S(1)}, s32[]{:S(2)}) async-start(f32[4,224]{1,0:T(4,128)} %copy-done.88), calls=%async_computation.3 | async-start | bytes 2048 | tf_op jit(solution)/shard_map/slice | solution.py:1525
  356.9 106.5 %copy-start.79 = (s32[4,512]{1,0:T(4,128)S(1)}, s32[4,512]{1,0:T(4,128)}, u32[]{:S(2)}) copy-start(s32[4,512]{1,0:T(4,128)} %copy-done.78) | copy-start | bytes 24580
  356.9 106.8 %copy-start.98 = (pred[16,4]{0,1:T(4,128)(4,1)S(1)}, pred[16,4]{0,1:T(4,128)(4,1)}, u32[]{:S(2)}) copy-start(pred[16,4]{0,1:T(4,128)(4,1)} %copy-done.97) | copy-start | bytes 196
  589.7 75.9 %collective-permute-start.11 = (bf16[128,2048]{1,0:T(8,128)(2,1)}, bf16[128,2048]{1,0:T(8,128)(2,1)}, u32[]{:S(2)}, u32[]{:S(2)}) collective-permute-start(bf16[128,2048]{1,0:T(8,128)(2,1)} %get-tuple-element.187), channel_id=1, source_target_pairs={{0,3},{1,2},{2,1},{3,0},{4,7},{5,6},{6,5},{7,4},{8,11},{9,10},{10,... | collective-permute-start | bytes 1572872 | tf_op jit(solution)/shard_map/ppermute | solution.py:79
  591.2 74.4 %collective-permute-start.10 = (bf16[128,2048]{1,0:T(8,128)(2,1)}, bf16[128,2048]{1,0:T(8,128)(2,1)}, u32[]{:S(2)}, u32[]{:S(2)}) collective-permute-start(bf16[128,2048]{1,0:T(8,128)(2,1)} %get-tuple-element.188), channel_id=1, source_target_pairs={{0,2},{1,3},{2,0},{3,1},{4,6},{5,7},{6,4},{7,5},{8,10},{9,11},{10,... | collective-permute-start | bytes 1572872 | tf_op jit(solution)/shard_map/ppermute | solution.py:79
  613.8 27.3 %collective-permute-start.14 = (bf16[4,64,576]{2,1,0:T(8,128)(2,1)}, bf16[4,64,576]{2,1,0:T(8,128)(2,1)}, u32[]{:S(2)}, u32[]{:S(2)}) collective-permute-start(bf16[4,64,576]{2,1,0:T(8,128)(2,1)} %get-tuple-element.185), channel_id=1, source_target_pairs={{0,12},{4,8},{8,4},{12,0},{1,13},{5,9},{9,5},{13,1},{2,14},{6,10},... | collective-permute-start | bytes 884744 | tf_op jit(solution)/shard_map/ppermute | solution.py:79
  613.8 29.0 %collective-permute-start.13 = (bf16[4,64,576]{2,1,0:T(8,128)(2,1)}, bf16[4,64,576]{2,1,0:T(8,128)(2,1)}, u32[]{:S(2)}, u32[]{:S(2)}) collective-permute-start(bf16[4,64,576]{2,1,0:T(8,128)(2,1)} %get-tuple-element.184), channel_id=1, source_target_pairs={{0,8},{4,12},{8,0},{12,4},{1,9},{5,13},{9,1},{13,5},{2,10},{6,14},... | collective-permute-start | bytes 884744 | tf_op jit(solution)/shard_map/ppermute | solution.py:79
  614.7 28.1 %collective-permute-start.12 = (bf16[4,64,576]{2,1,0:T(8,128)(2,1)}, bf16[4,64,576]{2,1,0:T(8,128)(2,1)}, u32[]{:S(2)}, u32[]{:S(2)}) collective-permute-start(bf16[4,64,576]{2,1,0:T(8,128)(2,1)} %get-tuple-element.183), channel_id=1, source_target_pairs={{0,4},{4,0},{8,12},{12,8},{1,5},{5,1},{9,13},{13,9},{2,6},{6,2},{1... | collective-permute-start | bytes 884744 | tf_op jit(solution)/shard_map/ppermute | solution.py:79
  641.1 24.5 %collective-permute-start.9 = (bf16[128,2048]{1,0:T(8,128)(2,1)}, bf16[128,2048]{1,0:T(8,128)(2,1)}, u32[]{:S(2)}, u32[]{:S(2)}) collective-permute-start(bf16[128,2048]{1,0:T(8,128)(2,1)} %get-tuple-element.186), channel_id=1, source_target_pairs={{0,1},{1,0},{2,3},{3,2},{4,5},{5,4},{6,7},{7,6},{8,9},{9,8},{10,11... | collective-permute-start | bytes 1572872 | tf_op jit(solution)/shard_map/ppermute | solution.py:79
  667.5 69.1 %copy-start.4 = (bf16[128,2048]{1,0:T(8,128)(2,1)}, bf16[128,2048]{1,0:T(8,128)(2,1)S(1)}, u32[]{:S(2)}) copy-start(bf16[128,2048]{1,0:T(8,128)(2,1)S(1)} %fusion.51.refs_1_) | copy-start | bytes 1572868
  (99 other events, 407.8 us)
Sparse Core Ops, SparseCore 0:
  62.9 65.7 all-gather.1
  577.1 88.8 reduce-scatter.1

commit v2 on v1

--- a/solution.py
+++ b/solution.py
@@ -536,19 +536,30 @@
     return results[0], results[1], results[2:]
 
 
-def middle_sum(partial, source, gain, matrices, experts, before):
-    count, rows, width = partial.shape
-    planes = lax.axis_size(PLANE)
-    number, routed = len(matrices), len(experts)
+def head_mask(head, heads, rope):
+    lanes = lax.broadcasted_iota(jnp.int32, (1, rope), 1)
+    return jnp.where(lax.rem(lanes, rope // 2) // (ROPE // 2) == head, 1.0, 0.0)
+
+
+def middle_sum(query_nope, query_rope, keys, tiled, up, out, source, gain, experts, grads):
+    count, rows = query_nope.shape[:2]
+    key_count, rope = keys.shape[1], query_rope.shape[2]
+    heads = query_nope.shape[2] // NOPE
+    width = source.shape[1]
+    planes, contexts = lax.axis_size(PLANE), lax.axis_size(CONTEXT_AXIS)
+    routed = len(experts)
+    score_scale = (NOPE + ROPE) ** (-0.5)
 
     def kernel(*refs):
-        position = 3 + number + routed + 1
-        partial_ref, source_ref, gain_ref = refs[:3]
-        sources = refs[3 : 3 + number]
-        expert_refs = refs[3 + number : position - 1]
-        middle_ref, hidden_all = refs[position : position + 2]
-        targets = refs[position + 2 : position + 2 + number + routed]
-        scratch = list(refs[position + 2 + number + routed :])
+        nope_ref, rope_ref, keys_ref, tiled_ref, up_ref, out_ref, source_ref, gain_ref = refs[:8]
+        expert_refs = refs[8 : 8 + routed]
+        grads_ref = refs[8 + routed]
+        outputs = refs[9 + routed :]
+        middle_ref, hidden_all, grads_all, mixed, probs, expanded = outputs[:6]
+        targets = outputs[6 : 6 + routed]
+        scratch = list(outputs[6 + routed :])
+        grads_line = [scratch.pop() for _ in range(3)][::-1]
+        partial_ref = scratch.pop(0)
         inbox, hidden, reduce_send, reduce_recv, own, line_send, line_recv = scratch[:7]
         stages = scratch[7 : 7 + routed]
         semaphores = scratch[7 + routed :]
@@ -579,53 +590,81 @@
             reduce_finish()
 
         tasks = [
-            plane_gather_task(sources[i], targets[i], *semaphores[3 * i : 3 * i + 3])
-            for i in range(number)
-        ] + [
             expert_fetch_task(
-                expert_refs[i],
-                targets[number + i],
-                stages[i],
-                *semaphores[3 * (number + i) : 3 * (number + i) + 3],
+                expert_refs[i], targets[i], stages[i], *semaphores[3 * i : 3 * i + 3]
             )
             for i in range(routed)
         ]
         for task in tasks:
             next(task)
+        grads_task = line_gather_task(grads_ref, grads_all, *grads_line)
+        next(grads_task)
         for task in tasks:
             next(task)
+        here = lax.axis_index(CONTEXT_AXIS)
+        row = lax.broadcasted_iota(jnp.int32, (rows, key_count), 0)
+        place = jnp.where(
+            row < PROMPT_DEV,
+            here * PROMPT_DEV + row,
+            contexts * PROMPT_DEV + row - PROMPT_DEV,
+        )
+        allowed = lax.broadcasted_iota(jnp.int32, (rows, key_count), 1) <= place
+
+        def attend(g, carry):
+            expanded[g] = low(product(keys_ref[g, :, :LATENT], up_ref[...]))
+            for h in range(heads):
+                start = h * (NOPE + VDIM)
+                scores = product_right(
+                    nope_ref[g, :, h * NOPE : (h + 1) * NOPE],
+                    expanded[g, :, start : start + NOPE],
+                ) + product_right(
+                    rope_ref[g] * low(head_mask(h, heads, rope)), tiled_ref[g]
+                )
+                scores = jnp.where(allowed, scores * score_scale, -1e30)
+                powers = jnp.exp(scores - jnp.max(scores, axis=-1, keepdims=True))
+                weights = low(powers / jnp.sum(powers, axis=-1, keepdims=True))
+                probs[g, h] = weights
+                mixed[g, :, h * VDIM : (h + 1) * VDIM] = low(
+                    product(weights, expanded[g, :, start + NOPE : start + NOPE + VDIM])
+                )
+            partial_ref[g] = low(product_right(mixed[g], out_ref[...]))
+            return carry
+
+        lax.fori_loop(0, count, attend, 0)
         run_tasks(line_task())
-        run_tasks(*tasks)
-
-    shapes = (
-        [
-            jax.ShapeDtypeStruct((rows, width), jnp.float32),
-            jax.ShapeDtypeStruct((count, rows, width), jnp.bfloat16),
-        ]
-        + [jax.ShapeDtypeStruct((planes * m.shape[0], m.shape[1]), m.dtype) for m in matrices]
-        + [jax.ShapeDtypeStruct((planes * e.shape[1], e.shape[2]), e.dtype) for e in experts]
-    )
+        run_tasks(grads_task, *tasks)
+
+    shapes = [
+        jax.ShapeDtypeStruct((rows, width), jnp.float32),
+        jax.ShapeDtypeStruct((count, rows, width), jnp.bfloat16),
+        jax.ShapeDtypeStruct((count, rows, width), jnp.bfloat16),
+        jax.ShapeDtypeStruct((count, rows, heads * VDIM), jnp.bfloat16),
+        jax.ShapeDtypeStruct((count, heads, rows, key_count), jnp.bfloat16),
+        jax.ShapeDtypeStruct((count, key_count, up.shape[1]), jnp.bfloat16),
+    ] + [jax.ShapeDtypeStruct((planes * e.shape[1], e.shape[2]), e.dtype) for e in experts]
     scratch = [
+        pltpu.VMEM((count, rows, width), jnp.bfloat16),
         pltpu.VMEM((count + 1, rows, width), jnp.bfloat16),
         pltpu.VMEM((rows, width), jnp.bfloat16),
     ]
     scratch += line_semaphores() + [pltpu.SemaphoreType.DMA(())] + line_semaphores()
     scratch += [pltpu.VMEM(e.shape[1:], e.dtype) for e in experts]
-    for _ in range(number + routed):
+    for _ in range(routed):
         scratch += gather_semaphores()
+    scratch += [pltpu.SemaphoreType.DMA(())] + line_semaphores()
     results = pl.pallas_call(
         kernel,
         out_shape=shapes,
-        in_specs=[INSIDE] * (3 + number) + [ANY] * (routed + 1),
-        out_specs=[INSIDE] + [ANY] * (1 + number + routed),
+        in_specs=[INSIDE] * 8 + [ANY] * routed + [INSIDE],
+        out_specs=[INSIDE, ANY, ANY] + [INSIDE] * 3 + [ANY] * routed,
         scratch_shapes=scratch,
         compiler_params=kernel_params(2),
         cost_estimate=pl.CostEstimate(
             flops=60_000_000, bytes_accessed=300_000_000, transcendentals=0
         ),
         name="middle_sum",
-    )(partial, source, gain, *matrices, *experts, before)
-    return results[0], results[1], results[2 : 2 + number], results[2 + number :]
+    )(query_nope, query_rope, keys, tiled, up, out, source, gain, *experts, grads)
+    return results[:6], results[6:]
 
 
 def add_rows(target, first, second):
@@ -1167,15 +1206,12 @@
             loads[number].start()
 
         fetch(0, wg_any, wg)
-        for k in range(4):
+        for k in (3, 2, 1, 0):
             fetch(3 + k, piece(hidden_any, hidden_far_any, k), hid.at[pl.ds(k * slots, slots)])
         fetch(1, wu_any, wu)
         fetch(2, wd_any, wd)
-        for k in range(4):
+        for k in (3, 2, 1, 0):
             fetch(7 + k, piece(grad_any, grad_far_any, k), grd.at[pl.ds(k * slots, slots)])
-        for number in (0, 3, 4, 5, 6, 1, 2, 7, 8, 9, 10):
-            loads[number].wait()
-
         def back(k, which):
             source, target = ((pair, pair_back), (result, result_back), (scale, scale_back))[which]
             return remote(
@@ -1193,8 +1229,18 @@
         def first(i, carry):
             k = 3 - i
             span = pl.ds(pl.multiple_of(k * slots, 16), slots)
+
+            def ready(*numbers):
+                @pl.when(i == 0)
+                def _():
+                    for number in numbers:
+                        loads[number].wait()
+
+            ready(0, 6, 5, 4, 3)
             gate = product(hid[span], wg[...])
+            ready(1)
             up = product(hid[span], wu[...])
+            ready(2, 10, 9, 8, 7)
             grad = product_right(grd[span], wd[...])
             gates_here = gates_ref[span]
             act_part, dgate_part, dup_part = silu_back(gate, up, grad)
@@ -1207,18 +1253,11 @@
             pair[k] = low(product_right(dgate[span], wg[...]) + product_right(dup[span], wu[...]))
             deliver(k, 0)
             deliver(k, 2)
-            return carry
-
-        lax.fori_loop(0, 4, first, 0)
-
-        def second(i, carry):
-            k = 3 - i
-            span = pl.ds(pl.multiple_of(k * slots, 16), slots)
             result[k] = low(product(act[span], wd[...]))
             deliver(k, 1)
             return carry
 
-        lax.fori_loop(0, 4, second, 0)
+        lax.fori_loop(0, 4, first, 0)
         kept = []
         for which, (source, target) in enumerate(
             ((pair, pair_back), (result, result_back), (scale, scale_back))
@@ -1294,6 +1333,81 @@
         name="routed_expert",
     )(*operands, gates, *weights)
     return results
+
+
+def attention_back(branch, out, probs, expanded, query_nope, query_rope, keys, tiled, up):
+    groups, rows, width = branch.shape
+    heads, key_count = probs.shape[1], probs.shape[3]
+    rope = query_rope.shape[2]
+    score_scale = (NOPE + ROPE) ** (-0.5)
+
+    def kernel(*refs):
+        branch_ref, out_ref, probs_ref, exp_ref, nope_ref, rope_ref, keys_ref, tiled_ref, up_ref = (
+            refs[:9]
+        )
+        dnope, drope, dlatent, dkey_rope, dup, dexp = refs[9:]
+        dmixed = low(product(branch_ref[...], out_ref[...]))
+        drope_sum = jnp.zeros((rows, rope), jnp.float32)
+        dkey_sum = jnp.zeros((key_count, rope), jnp.float32)
+        for h in range(heads):
+            nope_span = slice(h * NOPE, (h + 1) * NOPE)
+            key_span = slice(h * (NOPE + VDIM), h * (NOPE + VDIM) + NOPE)
+            value_span = slice(h * (NOPE + VDIM) + NOPE, (h + 1) * (NOPE + VDIM))
+            mask = head_mask(h, heads, rope)
+            weights = probs_ref[h]
+            part = dmixed[:, h * VDIM : (h + 1) * VDIM]
+            dprobs = product_right(part, exp_ref[:, value_span])
+            wide_weights = wide(weights)
+            delta = jnp.sum(wide_weights * dprobs, axis=-1, keepdims=True)
+            dscore = low(wide_weights * (dprobs - delta) * score_scale)
+            dexp[:, key_span] = low(product_left(dscore, nope_ref[:, nope_span]))
+            dexp[:, value_span] = low(product_left(weights, part))
+            dnope[:, nope_span] = low(product(dscore, exp_ref[:, key_span]))
+            drope_sum = drope_sum + product(dscore, tiled_ref[...]) * mask
+            dkey_sum = dkey_sum + product_left(dscore, rope_ref[...] * low(mask))
+        drope[...] = drope_sum
+        dkey_rope[...] = dkey_sum
+        dlatent[...] = product_right(dexp[...], up_ref[...])
+        grad_up = product_left(keys_ref[:, :LATENT], dexp[...])
+
+        @pl.when(pl.program_id(0) == 0)
+        def _():
+            dup[...] = grad_up
+
+        @pl.when(pl.program_id(0) > 0)
+        def _():
+            dup[...] = dup[...] + grad_up
+
+    def group(array):
+        shape = array.shape
+        return pl.BlockSpec(
+            (None,) + tuple(shape[1:]), lambda g, n=len(shape) - 1: (g,) + (0,) * n
+        )
+
+    def whole(array):
+        return pl.BlockSpec(array.shape, lambda g: (0, 0))
+
+    shapes = [
+        jax.ShapeDtypeStruct((groups, rows, heads * NOPE), jnp.bfloat16),
+        jax.ShapeDtypeStruct((groups, rows, rope), jnp.float32),
+        jax.ShapeDtypeStruct((groups, key_count, LATENT), jnp.float32),
+        jax.ShapeDtypeStruct((groups, key_count, rope), jnp.float32),
+        jax.ShapeDtypeStruct(up.shape, jnp.float32),
+    ]
+    operands = [branch, out, probs, expanded, query_nope, query_rope, keys, tiled, up]
+    return pl.pallas_call(
+        kernel,
+        grid=(groups,),
+        out_shape=shapes,
+        in_specs=[whole(x) if x is out or x is up else group(x) for x in operands],
+        out_specs=[group(x) for x in shapes[:4]] + [whole(up)],
+        scratch_shapes=[pltpu.VMEM((key_count, heads * (NOPE + VDIM)), jnp.bfloat16)],
+        compiler_params=pltpu.CompilerParams(vmem_limit_bytes=40 << 20),
+        cost_estimate=pl.CostEstimate(
+            flops=20_000_000_000, bytes_accessed=30_000_000, transcendentals=0
+        ),
+        name="attention_back",
+    )(*operands)
 
 
 def body(
@@ -1337,6 +1451,25 @@
     token_count = groups_local * TOK_DEV
     score_scale = (NOPE + ROPE) ** (-0.5)
 
+    half_rope = ROPE // 2
+    rope_cols = heads_local * half_rope
+    nope_cols = heads_local * NOPE
+
+    def query_split(columns):
+        each = columns.reshape(columns.shape[0], heads_local, NOPE + ROPE)
+        parts = (each[..., :NOPE], each[..., NOPE : NOPE + half_rope], each[..., NOPE + half_rope :])
+        return [part.reshape(columns.shape[0], -1) for part in parts]
+
+    def query_join(columns):
+        rows = columns.shape[0]
+        parts = (
+            columns[:, :nope_cols],
+            columns[:, nope_cols : nope_cols + rope_cols],
+            columns[:, nope_cols + rope_cols :],
+        )
+        each = [part.reshape(rows, heads_local, -1) for part in parts]
+        return jnp.concatenate(each, axis=-1).reshape(rows, query_cols)
+
     used_cols = query_cols + down_cols
     extra_cols = experts_all + 3
     pad_cols = -(used_cols + extra_cols) % 128
@@ -1350,13 +1483,23 @@
     )
     first_local = jnp.concatenate(
         [
-            query_weight,
+            *query_split(query_weight),
             latent_down,
             router_weight,
             jnp.zeros((shard_rows, 3 + pad_cols), jnp.bfloat16),
         ],
         axis=1,
     )
+    shared_cols = shared_gate.shape[1]
+    shared_pad = -(-shared_cols // 128) * 128
+
+    def padded(weight):
+        return jnp.pad(weight, ((0, 0), (0, shared_pad - shared_cols)))
+
+    shared_own = jnp.concatenate(
+        [padded(shared_gate), padded(shared_up), padded(shared_down.T)], axis=1
+    )
+    shared_whole = lax.all_gather(shared_own, PLANE, axis=0, tiled=True)
     gains_all, normed_all, (first_full, up_local, out_local) = opening(
         tokens[0], gains, [first_local, latent_up, out_weight.T]
     )
@@ -1369,11 +1512,7 @@
     query_places = jnp.where(
         within < PROMPT_DEV, context_index * PROMPT_DEV + within, prompt_len + within - PROMPT_DEV
     )
-    key_places = jnp.arange(prompt_len + CONT_LEN, dtype=jnp.int32)
-    allowed = key_places[None, :] <= query_places[:, None]
     cosine, sine_part = rotary_tables(query_places.astype(jnp.float32), ROPE // 2)
-    cosine_heads = cosine[None, :, None, :]
-    sine_heads = sine_part[None, :, None, :]
     source = wide(tokens[0])
 
     def pack_latent(comp_rows, latent_scale):
@@ -1385,95 +1524,40 @@
             axis=-1,
         )
 
-    grad_own, routes_own, _ = lax.optimization_barrier((grad_out[0], routes[0], gains_all))
-    grad_all = axis_gather(grad_own, EXPERT_AXIS)
-    routes_all = axis_gather(routes_own, EXPERT_AXIS)
+    routes_all = axis_gather(routes[0], EXPERT_AXIS)
     first_product = product(normed_all, first_full)
     compressed = first_product[..., query_cols:used_cols]
     packed = low(pack_latent(compressed, wide(full_latent_gain)))
-    prompt_keys = axis_gather(packed[:, :PROMPT_DEV], CONTEXT_AXIS)
-    cont_keys = packed[:, PROMPT_DEV:]
-    query_raw = first_product[..., :query_cols].reshape(
-        groups_local, TOK_DEV, heads_local, NOPE + ROPE
-    )
-    query_rows = low(
+    key_count = prompt_len + CONT_LEN
+    keys = jnp.zeros((groups_local, contexts + 1, PROMPT_DEV, down_cols), jnp.bfloat16)
+    prompt_own = packed[:, :PROMPT_DEV]
+    for mask in range(contexts):
+        came = swap(prompt_own, CONTEXT_AXIS, mask) if mask else prompt_own
+        keys = lax.dynamic_update_slice(
+            keys, came[:, None], (0, jnp.bitwise_xor(context_index, mask), 0, 0)
+        )
+    keys = lax.dynamic_update_slice(
+        keys, packed[:, None, PROMPT_DEV:], (0, contexts, 0, 0)
+    ).reshape(groups_local, key_count, down_cols)
+    query_nope = low(first_product[..., :nope_cols])
+    cosine_heads = jnp.tile(cosine, (1, heads_local))[None]
+    sine_heads = jnp.tile(sine_part, (1, heads_local))[None]
+    lower = first_product[..., nope_cols : nope_cols + rope_cols]
+    upper = first_product[..., nope_cols + rope_cols : query_cols]
+    query_rope = low(
         jnp.concatenate(
-            [query_raw[..., :NOPE], rotate(query_raw[..., NOPE:], cosine_heads, sine_heads)], axis=-1
+            [
+                lower * cosine_heads - upper * sine_heads,
+                upper * cosine_heads + lower * sine_heads,
+            ],
+            axis=-1,
         )
     )
-    query_nope = query_rows[..., :NOPE]
-    query_rope = query_rows[..., NOPE:]
-    prompt_latent = prompt_keys[..., :LATENT]
-    prompt_rope = prompt_keys[..., LATENT:]
-    cont_latent = cont_keys[..., :LATENT]
-    cont_rope = cont_keys[..., LATENT:]
-    prompt_exp = low(product(prompt_latent, up_local)).reshape(
-        contexts, groups_local, PROMPT_DEV, heads_local, NOPE + VDIM
-    )
-    cont_exp = low(product(cont_latent, up_local)).reshape(
-        groups_local, CONT_LEN, heads_local, NOPE + VDIM
-    )
-    prompt_knope = prompt_exp[..., :NOPE]
-    prompt_values = prompt_exp[..., NOPE:]
-    cont_knope = cont_exp[..., :NOPE]
-    cont_values = cont_exp[..., NOPE:]
-
-    def split_keys(values):
-        return (
-            values[..., :prompt_len].reshape(
-                groups_local, heads_local, TOK_DEV, contexts, PROMPT_DEV
-            ),
-            values[..., prompt_len:],
-        )
-
-    def score_all():
-        prompt_part = jnp.einsum(
-            "gqhd,cgphd->ghqcp", query_nope, prompt_knope, preferred_element_type=jnp.float32
-        )
-        prompt_part = prompt_part + jnp.einsum(
-            "gqhd,cgpd->ghqcp", query_rope, prompt_rope, preferred_element_type=jnp.float32
-        )
-        prompt_part = prompt_part.reshape(groups_local, heads_local, TOK_DEV, prompt_len)
-        cont_part = jnp.einsum(
-            "gqhd,gphd->ghqp", query_nope, cont_knope, preferred_element_type=jnp.float32
-        )
-        cont_part = cont_part + jnp.einsum(
-            "gqhd,gpd->ghqp", query_rope, cont_rope, preferred_element_type=jnp.float32
-        )
-        raw_scores = jnp.concatenate([prompt_part, cont_part], axis=-1)
-        return jnp.where(allowed, raw_scores * score_scale, -1e30)
-
-    scores = score_all()
-    top_score = jnp.max(scores, axis=-1, keepdims=True)
-    exp_scores = jnp.exp(scores - top_score)
-    totals = jnp.sum(exp_scores, axis=-1, keepdims=True)
-    probs_all = exp_scores / totals
-    probs_low = low(probs_all)
-    probs_prompt, probs_cont = split_keys(probs_low)
-    mixed_rows = jnp.einsum(
-        "ghqcp,cgphd->gqhd", probs_prompt, prompt_values, preferred_element_type=jnp.float32
-    )
-    mixed_rows = mixed_rows + jnp.einsum(
-        "ghqp,gphd->gqhd", probs_cont, cont_values, preferred_element_type=jnp.float32
-    )
-    mixed_all = low(mixed_rows.reshape(groups_local, TOK_DEV, heads_local * VDIM))
-    partial_sum = against_rows(mixed_all, out_local)
-    shared_cols = shared_gate.shape[1]
-    shared_pad = -(-shared_cols // 128) * 128
-
-    def padded(weight):
-        return jnp.pad(weight, ((0, 0), (0, shared_pad - shared_cols)))
-
-    shared_own, _ = lax.optimization_barrier(
-        (
-            jnp.concatenate(
-                [padded(shared_gate), padded(shared_up), padded(shared_down.T)], axis=1
-            ),
-            gains_all,
-        )
-    )
-    shared_whole = lax.all_gather(shared_own, PLANE, axis=0, tiled=True)
-    grad_flat = grad_all.reshape(token_count, D)
+    tiled_rope = jnp.concatenate(
+        [keys[..., LATENT : LATENT + half_rope]] * heads_local
+        + [keys[..., LATENT + half_rope :]] * heads_local,
+        axis=-1,
+    )
     slot_experts = expert_index * local_experts + (
         expert_own ^ jnp.arange(local_experts, dtype=jnp.int32)
     )
@@ -1496,18 +1580,24 @@
     )
     picked_low = picked.astype(jnp.bfloat16).reshape(local_experts * slots, token_count)
     piece_slots = slots * local_experts // 4
-    grad_slots = low(product(picked_low, grad_flat)).reshape(4, piece_slots, D)
-    middle, hidden_all, _, (gate_full, up_full, down_full) = middle_sum(
-        low(partial_sum),
+    (middle, hidden_all, grad_all, mixed_all, probs, expanded), fetched = middle_sum(
+        query_nope,
+        query_rope,
+        keys,
+        tiled_rope,
+        up_local,
+        out_local,
         tokens[0],
         full_ffn_gain[None],
-        [],
         [expert_gate, expert_up, expert_down],
-        grad_slots,
-    )
+        grad_out[0],
+    )
+    gate_full, up_full, down_full = fetched
     hidden_flat = hidden_all.reshape(token_count, D)
 
+    grad_flat = grad_all.reshape(token_count, D)
     hidden_slots = low(product(picked_low, hidden_flat)).reshape(4, piece_slots, D)
+    grad_slots = low(product(picked_low, grad_flat)).reshape(4, piece_slots, D)
     logits = product(hidden_flat, full_router)
     expert_probs = jax.nn.softmax(logits, axis=-1)
     gate_tokens = jnp.sum(jnp.where(expert_cols[None], expert_probs[:, :, None], 0.0), axis=1)
@@ -1574,81 +1664,41 @@
             branch_all.reshape(token_count, D), mixed_all.reshape(token_count, heads_local * VDIM)
         )
     )
-    grad_mixed = low(product(branch_all, out_local)).reshape(
-        groups_local, TOK_DEV, heads_local, VDIM
-    )
-    grad_probs_prompt = jnp.einsum(
-        "gqhd,cgphd->ghqcp", grad_mixed, prompt_values, preferred_element_type=jnp.float32
-    )
-    grad_probs_cont = jnp.einsum(
-        "gqhd,gphd->ghqp", grad_mixed, cont_values, preferred_element_type=jnp.float32
-    )
-    grad_probs = jnp.concatenate(
+    grad_nope, grad_rope, grad_latent, grad_key_rope, grad_latent_up = attention_back(
+        branch_all,
+        out_local,
+        probs,
+        expanded,
+        query_nope,
+        query_rope,
+        keys,
+        tiled_rope,
+        up_local,
+    )
+    lower, upper = grad_rope[..., :rope_cols], grad_rope[..., rope_cols:]
+    grad_query_raw = jnp.concatenate(
         [
-            grad_probs_prompt.reshape(groups_local, heads_local, TOK_DEV, prompt_len),
-            grad_probs_cont,
+            grad_nope,
+            low(lower * cosine_heads + upper * sine_heads),
+            low(upper * cosine_heads - lower * sine_heads),
         ],
         axis=-1,
     )
-    delta_rows = jnp.sum(probs_all * grad_probs, axis=-1, keepdims=True)
-    grad_raw = low(probs_all * (grad_probs - delta_rows) * score_scale)
-    raw_prompt, raw_cont = split_keys(grad_raw)
-    value_prompt = jnp.einsum(
-        "ghqcp,gqhd->cgphd", probs_prompt, grad_mixed, preferred_element_type=jnp.float32
-    )
-    value_cont = jnp.einsum(
-        "ghqp,gqhd->gphd", probs_cont, grad_mixed, preferred_element_type=jnp.float32
-    )
-    knope_prompt = jnp.einsum(
-        "ghqcp,gqhd->cgphd", raw_prompt, query_nope, preferred_element_type=jnp.float32
-    )
-    knope_cont = jnp.einsum(
-        "ghqp,gqhd->gphd", raw_cont, query_nope, preferred_element_type=jnp.float32
-    )
-    krope_prompt = jnp.einsum(
-        "ghqcp,gqhd->cgpd", raw_prompt, query_rope, preferred_element_type=jnp.float32
-    )
-    krope_cont = jnp.einsum(
-        "ghqp,gqhd->gpd", raw_cont, query_rope, preferred_element_type=jnp.float32
-    )
-    grad_query_nope = jnp.einsum(
-        "ghqcp,cgphd->gqhd", raw_prompt, prompt_knope, preferred_element_type=jnp.float32
-    )
-    grad_query_nope = grad_query_nope + jnp.einsum(
-        "ghqp,gphd->gqhd", raw_cont, cont_knope, preferred_element_type=jnp.float32
-    )
-    grad_query_rope = jnp.einsum(
-        "ghqcp,cgpd->gqhd", raw_prompt, prompt_rope, preferred_element_type=jnp.float32
-    )
-    grad_query_rope = grad_query_rope + jnp.einsum(
-        "ghqp,gpd->gqhd", raw_cont, cont_rope, preferred_element_type=jnp.float32
-    )
-    grad_query_raw = jnp.concatenate(
-        [grad_query_nope, rotate(grad_query_rope, cosine_heads, -sine_heads)], axis=-1
-    )
-    grad_query_raw = low(
-        grad_query_raw.reshape(groups_local, TOK_DEV, heads_local * (NOPE + ROPE))
-    )
-    grad_exp_prompt = low(
-        jnp.concatenate([knope_prompt, value_prompt], axis=-1).reshape(
-            contexts, groups_local, PROMPT_DEV, heads_local * (NOPE + VDIM)
+    grad_key_rope = jnp.sum(
+        grad_key_rope.reshape(groups_local, key_count, 2, heads_local, half_rope), axis=3
+    ).reshape(groups_local, key_count, ROPE)
+    grad_keys = jnp.concatenate([grad_latent, grad_key_rope], axis=-1)
+    grad_keys = grad_keys.reshape(groups_local, contexts + 1, PROMPT_DEV, down_cols)
+
+    def keys_of(mask):
+        return lax.dynamic_index_in_dim(
+            grad_keys, jnp.bitwise_xor(context_index, mask), 1, keepdims=False
         )
-    )
-    grad_exp_cont = low(
-        jnp.concatenate([knope_cont, value_cont], axis=-1).reshape(
-            groups_local, CONT_LEN, heads_local * (NOPE + VDIM)
-        )
-    )
-    latent_prompt = jnp.einsum(
-        "cgpf,lf->cgpl", grad_exp_prompt, up_local, preferred_element_type=jnp.float32
-    )
-    latent_cont = jnp.einsum(
-        "gpf,lf->gpl", grad_exp_cont, up_local, preferred_element_type=jnp.float32
-    )
-    grad_prompt_keys = jnp.concatenate([latent_prompt, krope_prompt], axis=-1)
-    grad_cont_keys = jnp.concatenate([latent_cont, krope_cont], axis=-1)
-    prompt_sum = axis_scatter(grad_prompt_keys, CONTEXT_AXIS)
-    grad_packed = jnp.concatenate([prompt_sum, grad_cont_keys], axis=1)
+
+    prompt_sum = keys_of(0)
+    for mask in range(1, contexts):
+        prompt_sum = prompt_sum + wide(swap(low(keys_of(mask)), CONTEXT_AXIS, mask))
+    grad_packed = jnp.concatenate([prompt_sum, grad_keys[:, contexts]], axis=1)
     _, pack_back = jax.vjp(pack_latent, compressed, wide(full_latent_gain))
     grad_compressed, grad_latent_gain = pack_back(grad_packed)
     grad_first = jnp.concatenate(
@@ -1661,12 +1711,6 @@
     )
     grad_normed_part = low(against_rows(grad_first, first_full))
 
-    grad_latent_up = jnp.einsum(
-        "cgpl,cgpf->lf", prompt_latent, grad_exp_prompt, preferred_element_type=jnp.float32
-    )
-    grad_latent_up = grad_latent_up + jnp.einsum(
-        "gpl,gpf->lf", cont_latent, grad_exp_cont, preferred_element_type=jnp.float32
-    )
     first_back = product_left(
         normed_all.reshape(token_count, D), grad_first.reshape(token_count, first_full.shape[1])
     )
@@ -1706,7 +1750,7 @@
         block_out[None],
         grad_tokens[None],
         small_own[0],
-        first_sum[:, :query_cols],
+        query_join(first_sum[:, :query_cols]),
         down_own[:, down_start : down_start + down_cols],
         latent_own,
         up_sum,

time: 765 us -> 749 us (0.979)
  Pallas kernels: 525 us -> 568 us
  matrix products: 77.3 us -> 50.7 us
  local copies, waits for them, and re-layouts: 80.9 us -> 59.8 us
    pallas_call x1, Pallas kernels: 47.3 us -> 72 us  [opening(): pl.pallas_call(kernel, out_shape=shapes, in_specs=[INSIDE] * (2 + number)...]
    pallas_call x1 -> x2, Pallas kernels: 111 us -> 134 us  [the longest x1 118 us: middle_sum(): pl.pallas_call(kernel, out_shape=shapes, in_specs=[INSIDE] * 8 + [ANY] *...]
    dot_general x20 -> x0, matrix products: 17.8 us -> none  [the longest x1 3.33 us: body(): jnp.einsum('cgpf,lf->cgpl', grad_exp_prompt, up_local, preferred_element_...]
    dynamic_update_slice x11 -> x4, local copies, waits for them, and re-layouts: 16.4 us -> 2.55 us  [place_pieces(): lax.dynamic_update_slice(whole, piece[None], (index ^ mask,) + (0,) * fir...]
    dot_general x7 -> x4, matrix products: 25.3 us -> 16.9 us  [product(): return jnp.dot(left_side, right_side, preferred_element_type=jnp.float32)]
    unnamed x225 -> x159, local copies, waits for them, and re-layouts: 23.8 us -> 21.1 us
  transfers between devices with their start and end apart: 17 -> 14, of which waited for: 3 -> 2; matrix products, arithmetic and copies ran while one was open for 20% -> 14% of each run, Pallas kernels for 24% -> 37%
where the time goes in v2:
time: 749 us; the launch traced here: 739 us
  Pallas kernels  568 us (76%)
  local copies, waits for them, and re-layouts  59.8 us (8%)
  matrix products  50.7 us (7%)
  other arithmetic  25.2 us (3%)
  between operations  15.9 us (2%)
  starting transfers between devices  12.4 us (2%)
  waiting for transfers between devices  7.49 us (1%)
    pallas_call x1, Pallas kernels, middle_sum(): pl.pallas_call(kernel, out_shape=shapes, in_specs=[INSIDE] * 8 + [ANY] *...  118 us
    pallas_call x1, Pallas kernels, branch_sum(): pl.pallas_call(kernel, out_shape=shapes, in_specs=[INSIDE] * 4 + [ANY] *...  103 us
    pallas_call x1, Pallas kernels, routed_expert(): pl.pallas_call(kernel, out_shape=shapes, in_specs=[ANY] * len(operands) +...  102 us
    pallas_call x1, Pallas kernels, shared_and_rows(): pl.pallas_call(kernel, out_shape=shapes, in_specs=[ANY] * 5 + [INSIDE], o...  87.3 us
    pallas_call x1, Pallas kernels, opening(): pl.pallas_call(kernel, out_shape=shapes, in_specs=[INSIDE] * (2 + number)...  72 us
    pallas_call x1, Pallas kernels, closing(): pl.pallas_call(kernel, out_shape=shapes, in_specs=[INSIDE, ANY] + [INSIDE...  70 us
    unnamed x159, local copies, waits for them, and re-layouts  21.1 us
    dot_general x4, matrix products, product(): return jnp.dot(left_side, right_side, preferred_element_type=jnp.float32)  16.9 us
  transfers between devices with their start and end apart: 14, of which 2 were waited for; matrix products, arithmetic and copies ran while one was open for 14% of the time, Pallas kernels for 37%

profile of v2, /device:TPU:0, one launch (start us, length us, event | category | flops | bytes accessed | tf_op | source)
XLA Modules:
  0.0 739.4 jit_solution(1263959081973033320)
XLA Ops:
  14.2 72.0 %opening.1 = (f32[8,8,256]{2,1,0:T(8,128)S(1)}, bf16[4,128,2048]{2,1,0:T(8,128)(2,1)}, bf16[2048,1408]{1,0:T(8,128)(2,1)}, bf16[512,1024]{1,0:T(8,128)(2,1)}, bf16[2048,512]{1,0:T(8,128)(2,1)}) custom-call(bf16[128,2048]{1,0:T(8,128)(2,1)S(1)} %bitcast.170, f32[8,256]{1,0:T(8,128)S(1)} %stack.31.refs_1_, bf16[256,1408]{1,0:T(8,128)(2,1)S(1)} %concatenate.40.refs_2_, ...), custom_call_target="tpu_custom_call" | custom-call | flops 60000000 | bytes 150000000 | tf_op jit(solution)/shard_map/opening/pallas_call | solution.py:524
  86.3 6.4 fusion.2
  109.4 4.1 collective-permute-done.5
  119.8 3.5 concatenate.43.refs_3_.refs_7_
  123.4 118.3 %middle_sum.1 = (f32[128,2048]{1,0:T(8,128)}, bf16[4,128,2048]{2,1,0:T(8,128)(2,1)}, bf16[4,128,2048]{2,1,0:T(8,128)(2,1)}, bf16[4,128,512]{2,1,0:T(8,128)(2,1)S...) custom-call(bf16[4,128,512]{2,1,0:T(8,128)(2,1)S(1)} %slice.208.refs, ...), custom_call_target="tpu_custom_call" | custom-call | flops 60000000 | bytes 300000000 | tf_op jit(solution)/shard_map/middle_sum/pallas_call | solution.py:655
  241.7 2.7 fusion.60
  245.0 3.9 convolution_convert_fusion.1
  248.9 3.9 convolution_convert_fusion
  252.8 87.3 %shared_and_rows.1 = (bf16[512,768]{1,0:T(8,128)(2,1)S(1)}, f32[512,2048]{1,0:T(8,128)}, bf16[2048,2304]{1,0:T(8,128)(2,1)}, f32[3,8,256]{2,1,0:T(8,128)S(1)}, b...) custom-call(bf16[512,2048]{1,0:T(8,128)(2,1)} %bitcast.186, bf16[512,2048]{1,0:T(8,128)(2,1)} %bitcast.216, ...), custom_call_target="tpu_custom_call" | custom-call | flops 9663676416 | bytes 120000000 | tf_op jit(solution)/shard_map/shared_and_rows/pallas_call | solution.py:1165
  341.3 102.3 %routed_expert.1 = (bf16[4,224,2048]{2,1,0:T(8,128)(2,1)}, bf16[4,224,2048]{2,1,0:T(8,128)(2,1)}, f32[4,224,128]{2,1,0:T(8,128)}, bf16[2048,1408]{1,0:T(8,128)(2...) custom-call(bf16[4,224,2048]{2,1,0:T(8,128)(2,1)} %bitcast.219, bf16[4,224,2048]{2,1,0:T(8,128)(2,1)} %bitcast.221, ...), custom_call_target="tpu_custom_call" | custom-call | flops 46506442752 | bytes 200000000 | tf_op jit(solution)/shard_map/routed_expert/pallas_call | solution.py:1319
  445.3 3.3 fusion.38
  448.7 5.9 fusion.5
  454.5 102.8 %branch_sum.1 = (f32[128,2048]{1,0:T(8,128)S(1)}, f32[1,2048]{1,0:T(1,128)S(1)}, bf16[4,128,2048]{2,1,0:T(8,128)(2,1)}, bf16[4,256,1408]{2,1,0:T(8,128)(2,1)}, b...) custom-call(bf16[4,128,2048]{2,1,0:T(8,128)(2,1)} %bitcast.193, ...), custom_call_target="tpu_custom_call", output_to_operand_aliasing={{6}: (7, {}), {7}: (8, {})} | custom-call | flops 60000000 | bytes 300000000 | tf_op jit(solution)/shard_map/branch_sum/pallas_call | solution.py:891
  558.8 3.9 copy.209
  562.7 4.2 fusion.6
  573.4 15.2 %attention_back.1 = (bf16[4,128,512]{2,1,0:T(8,128)(2,1)S(1)}, f32[4,128,256]{2,1,0:T(8,128)S(1)}, f32[4,320,512]{2,1,0:T(8,128)}, f32[4,320,256]{2,1,0:T(8,128)S(1)}, f32[512,1024]{1,0:T(8,128)S(1)}) custom-call(bf16[4,128,2048]{2,1,0:T(8,128)(2,1)S(1)} %copy-done.13, bf16[2048,512]{1,0:T(8,128)(2,1)S(1)} %copy-done.5, ...), custom_call_target="tpu_custom_call" | custom-call | flops 20000000000 | bytes 30000000 | tf_op jit(solution)/shard_map/attention_back/pallas_call | solution.py:1398
  590.5 2.9 copy.192
  607.0 2.9 convert_element_type.151
  610.0 2.9 convert_element_type.152
  613.1 3.3 convert_element_type.153
  620.4 3.4 collective-permute-done.10
  631.4 7.5 %fusion.8.refs_0_ = bf16[4,128,2048]{2,1,0:T(8,128)(2,1)} fusion(bf16[4,128,1408]{2,1,0:T(8,128)(2,1)S(1)} %concatenate.50, bf16[2048,1408]{1,0:T(8,128)(2,1)} %get-tuple-element.62), kind=kOutput, calls=%fused_computation.24 | convolution fusion | flops 2953838592 | bytes 9306112 | tf_op jit(solution)/shard_map/dot_general | solution.py:65
  639.0 5.3 bitcast_convert_fusion.refs_6_
  646.2 70.0 %closing.1 = (f32[128,2048]{1,0:T(8,128)}, f32[24,256]{1,0:T(8,128)S(1)}, f32[64,640]{1,0:T(8,128)S(1)}, f32[256,1408]{1,0:T(8,128)}, f32[64,1024]{1,0:T(8,128)S(1)}, /*index=5*/f32[256,512]{1,0:T(8,128)S(1)}) custom-call(bf16[4,128,2048]{2,1,0:T(8,128)(2,1)} %fusion.8.refs_0_, bf16[128,2048]{1,0:T(8,128)(2,1)S(1)} %fusion.24.refs_1_, ...), custom_call_target="tpu_custom_call" | custom-call | flops 60000000 | bytes 200000000 | tf_op jit(solution)/shard_map/closing/pallas_call | solution.py:1057
  (300 shorter events, 85.4 us)
Async XLA Ops:
  7.2 245.6 %all-gather.2.cloned.1.call-start = ((), (), s32[]{:S(2)}) async-start(), calls=%async_computation.1 | async-start | bytes 10616832 | tf_op jit(solution)/shard_map/all_gather | solution.py:1502
  11.9 710.9 %reduce-scatter.2.cloned.1.call-start = ((), (), s32[]{:S(2)}) async-start(), calls=%async_computation.2 | async-start | bytes 10616832 | tf_op jit(solution)/shard_map/reduce_scatter | solution.py:1657
  86.3 7.5 %copy-start.53 = (f32[512]{0:T(512)}, f32[512]{0:T(512)S(1)}, u32[]{:S(2)}) copy-start(f32[512]{0:T(512)S(1)} %mul.236) | copy-start | bytes 6148
  94.5 10.0 %copy-start.30 = (bf16[4,128,576]{2,1,0:T(8,128)(2,1)}, bf16[4,128,576]{2,1,0:T(8,128)(2,1)S(1)}, u32[]{:S(2)}) copy-start(bf16[4,128,576]{2,1,0:T(8,128)(2,1)S(1)} %pad_maximum_fusion.3) | copy-start | bytes 1769476
  95.3 19.6 %collective-permute-start = (bf16[4,64,576]{2,1,0:T(8,128)(2,1)}, bf16[4,64,576]{2,1,0:T(8,128)(2,1)}, u32[]{:S(2)}, u32[]{:S(2)}) collective-permute-start(bf16[4,64,576]{2,1,0:T(8,128)(2,1)} %slice.167), channel_id=1, source_target_pairs={{0,4},{4,0},{8,12},{12,8},{1,5},{5,1},{9,13},{13,9},{2,6},{6,2},{1... | collective-permute-start | bytes 884744 | tf_op jit(solution)/shard_map/ppermute | solution.py:79
  95.7 20.2 %collective-permute-start.1 = (bf16[4,64,576]{2,1,0:T(8,128)(2,1)}, bf16[4,64,576]{2,1,0:T(8,128)(2,1)}, u32[]{:S(2)}, u32[]{:S(2)}) collective-permute-start(bf16[4,64,576]{2,1,0:T(8,128)(2,1)} %slice.167), channel_id=1, source_target_pairs={{0,8},{4,12},{8,0},{12,4},{1,9},{5,13},{9,1},{13,5},{2,10},{6,14},... | collective-permute-start | bytes 884744 | tf_op jit(solution)/shard_map/ppermute | solution.py:79
  96.3 20.7 %collective-permute-start.2 = (bf16[4,64,576]{2,1,0:T(8,128)(2,1)}, bf16[4,64,576]{2,1,0:T(8,128)(2,1)}, u32[]{:S(2)}, u32[]{:S(2)}) collective-permute-start(bf16[4,64,576]{2,1,0:T(8,128)(2,1)} %slice.167), channel_id=1, source_target_pairs={{0,12},{4,8},{8,4},{12,0},{1,13},{5,9},{9,5},{13,1},{2,14},{6,10},... | collective-permute-start | bytes 884744 | tf_op jit(solution)/shard_map/ppermute | solution.py:79
  98.0 9.2 %collective-permute-start.3 = (s32[128,6]{1,0:T(8,128)}, s32[128,6]{1,0:T(8,128)}, u32[]{:S(2)}, u32[]{:S(2)}) collective-permute-start(s32[128,6]{1,0:T(8,128)} %bitcast.28), channel_id=1, source_target_pairs={{0,1},{1,0},{2,3},{3,2},{4,5},{5,4},{6,7},{7,6},{8,9},{9,8},{10,11... | collective-permute-start | bytes 9224 | tf_op jit(solution)/shard_map/ppermute | solution.py:79
  99.6 9.0 %collective-permute-start.4 = (s32[128,6]{1,0:T(8,128)}, s32[128,6]{1,0:T(8,128)}, u32[]{:S(2)}, u32[]{:S(2)}) collective-permute-start(s32[128,6]{1,0:T(8,128)} %bitcast.28), channel_id=1, source_target_pairs={{0,2},{1,3},{2,0},{3,1},{4,6},{5,7},{6,4},{7,5},{8,10},{9,11},{10,... | collective-permute-start | bytes 9224 | tf_op jit(solution)/shard_map/ppermute | solution.py:79
  107.2 6.3 collective-permute-start.5
  241.7 7.2 copy-start.16
  244.5 200.7 %copy-start.44 = (f32[512,16]{0,1:T(8,128)}, f32[512,16]{0,1:T(8,128)S(1)}, u32[]{:S(2)}) copy-start(f32[512,16]{0,1:T(8,128)S(1)} %fusion.49) | copy-start | bytes 98308
  252.8 87.4 %slice-start = ((f32[4,224]{1,0:T(4,128)}), f32[1,224]{1,0:T(1,128)S(1)}, s32[]{:S(2)}) async-start(f32[4,224]{1,0:T(4,128)} %copy-done.58), calls=%async_computation.3 | async-start | bytes 2048 | tf_op jit(solution)/shard_map/slice | solution.py:1615
  570.6 73.7 %collective-permute-start.8 = (bf16[128,2048]{1,0:T(8,128)(2,1)}, bf16[128,2048]{1,0:T(8,128)(2,1)}, u32[]{:S(2)}, u32[]{:S(2)}) collective-permute-start(bf16[128,2048]{1,0:T(8,128)(2,1)} %get-tuple-element.199), channel_id=1, source_target_pairs={{0,3},{1,2},{2,1},{3,0},{4,7},{5,6},{6,5},{7,4},{8,11},{9,10},{10,... | collective-permute-start | bytes 1572872 | tf_op jit(solution)/shard_map/ppermute | solution.py:79
  572.7 71.7 %collective-permute-start.7 = (bf16[128,2048]{1,0:T(8,128)(2,1)}, bf16[128,2048]{1,0:T(8,128)(2,1)}, u32[]{:S(2)}, u32[]{:S(2)}) collective-permute-start(bf16[128,2048]{1,0:T(8,128)(2,1)} %get-tuple-element.200), channel_id=1, source_target_pairs={{0,2},{1,3},{2,0},{3,1},{4,6},{5,7},{6,4},{7,5},{8,10},{9,11},{10,... | collective-permute-start | bytes 1572872 | tf_op jit(solution)/shard_map/ppermute | solution.py:79
  600.4 18.4 %collective-permute-start.11 = (bf16[4,64,576]{2,1,0:T(8,128)(2,1)S(1)}, bf16[4,64,576]{2,1,0:T(8,128)(2,1)S(1)}, u32[]{:S(2)}, u32[]{:S(2)}) collective-permute-start(bf16[4,64,576]{2,1,0:T(8,128)(2,1)S(1)} %get-tuple-element.193), channel_id=1, source_target_pairs={{0,12},{4,8},{8,4},{12,0},{1,13},{5,9},{9,5},{13,1},{2,14},{6,10},... | collective-permute-start | bytes 884744 | tf_op jit(solution)/shard_map/ppermute | solution.py:79
  601.4 22.3 %collective-permute-start.10 = (bf16[4,64,576]{2,1,0:T(8,128)(2,1)S(1)}, bf16[4,64,576]{2,1,0:T(8,128)(2,1)S(1)}, u32[]{:S(2)}, u32[]{:S(2)}) collective-permute-start(bf16[4,64,576]{2,1,0:T(8,128)(2,1)S(1)} %get-tuple-element.192), channel_id=1, source_target_pairs={{0,8},{4,12},{8,0},{12,4},{1,9},{5,13},{9,1},{13,5},{2,10},{6,14},... | collective-permute-start | bytes 884744 | tf_op jit(solution)/shard_map/ppermute | solution.py:79
  602.0 21.7 %collective-permute-start.9 = (bf16[4,64,576]{2,1,0:T(8,128)(2,1)S(1)}, bf16[4,64,576]{2,1,0:T(8,128)(2,1)S(1)}, u32[]{:S(2)}, u32[]{:S(2)}) collective-permute-start(bf16[4,64,576]{2,1,0:T(8,128)(2,1)S(1)} %get-tuple-element.191), channel_id=1, source_target_pairs={{0,4},{4,0},{8,12},{12,8},{1,5},{5,1},{9,13},{13,9},{2,6},{6,2},{1... | collective-permute-start | bytes 884744 | tf_op jit(solution)/shard_map/ppermute | solution.py:79
  602.4 21.5 %copy-start.24 = (f32[4,64,576]{2,1,0:T(8,128)}, f32[4,64,576]{2,1,0:T(8,128)S(1)}, u32[]{:S(2)}) copy-start(f32[4,64,576]{2,1,0:T(8,128)S(1)} %fusion.37) | copy-start | bytes 1769476
  618.8 6.0 copy-start.54
  618.8 6.0 copy-start.56
  618.8 25.5 %collective-permute-start.6 = (bf16[128,2048]{1,0:T(8,128)(2,1)}, bf16[128,2048]{1,0:T(8,128)(2,1)}, u32[]{:S(2)}, u32[]{:S(2)}) collective-permute-start(bf16[128,2048]{1,0:T(8,128)(2,1)} %get-tuple-element.198), channel_id=1, source_target_pairs={{0,1},{1,0},{2,3},{3,2},{4,5},{5,4},{6,7},{7,6},{8,9},{9,8},{10,11... | collective-permute-start | bytes 1572872 | tf_op jit(solution)/shard_map/ppermute | solution.py:79
  631.4 7.6 %copy-start.65 = (bf16[4,128,2048]{2,1,0:T(8,128)(2,1)S(1)}, bf16[4,128,2048]{2,1,0:T(8,128)(2,1)}, u32[]{:S(2)}) copy-start(bf16[4,128,2048]{2,1,0:T(8,128)(2,1)} %get-tuple-element.61) | copy-start | bytes 6291460
  646.2 70.0 %copy-start.6 = (bf16[128,2048]{1,0:T(8,128)(2,1)}, bf16[128,2048]{1,0:T(8,128)(2,1)S(1)}, u32[]{:S(2)}) copy-start(bf16[128,2048]{1,0:T(8,128)(2,1)S(1)} %fusion.24.refs_1_) | copy-start | bytes 1572868
  (62 other events, 181.2 us)
Sparse Core Ops, SparseCore 0:
  12.0 85.8 all-gather.1
  558.5 83.2 reduce-scatter.1

commit v3 on v2

--- a/solution.py
+++ b/solution.py
@@ -918,20 +918,24 @@
     pl.semaphore_wait(pltpu.get_barrier_semaphore(), planes + count - 2)
 
 
-def closing(partial, ready_before, source, gain, grad_middle, gain_grads, matrices, spread):
-    count, rows, width = partial.shape
+def closing(grad_first, first_full, normed, ready_before, source, gain, grad_middle, gain_grads, matrices, spread):
+    rows, width = source.shape
+    count = lax.axis_size(EXPERT_AXIS)
     planes = lax.axis_size(PLANE)
-    number = len(matrices)
+    number = len(matrices) + 1
+    sizes = [first_full.shape] + [m.shape for m in matrices]
     depth = gain_grads.shape[2]
-    shard, columns = matrices[0].shape[0] // planes, matrices[0].shape[1]
+    shard, columns = first_full.shape[0] // planes, first_full.shape[1]
     thin = shard // count
 
     def kernel(*refs):
-        partial_ref, _, source_ref, gain_ref, middle_ref, gains_ref = refs[:6]
-        sources = refs[6 : 6 + number]
-        grad_tokens, gains_out, thin_out = refs[6 + number : 9 + number]
-        results = refs[9 + number : 9 + 2 * number]
-        scratch = list(refs[9 + 2 * number :])
+        first_ref, full_ref, normed_ref, _, source_ref, gain_ref, middle_ref, gains_ref = refs[:8]
+        sources = list(refs[8 : 7 + number])
+        grad_tokens, gains_out, thin_out = refs[7 + number : 10 + number]
+        results = refs[10 + number : 10 + 2 * number]
+        scratch = list(refs[10 + 2 * number :])
+        partial_ref, back_ref = scratch.pop(), scratch.pop()
+        sources = [back_ref] + sources
         inbox, reduce_send, reduce_recv, gain_row = scratch[:4]
         gain_part, gain_box, gain_send, gain_recv = scratch[4:8]
         gain_held, gain_far, far_send, far_recv, thin_box, thin_send, thin_recv = scratch[8:15]
@@ -1023,19 +1027,38 @@
             for i in range(number)
         ]
         tasks[0] = first_task(tasks[0])
+        for task in tasks[1:]:
+            next(task)
+
+        def back_tile(i, carry):
+            span = pl.ds(pl.multiple_of(i * 256, 256), 256)
+            back_ref[span] = low(product_left(normed_ref[:, span], first_ref[...]))
+            return carry
+
+        lax.fori_loop(0, width // 256, back_tile, 0)
+        for task in tasks:
+            next(task)
+
+        def partial_tile(i, carry):
+            span = pl.ds(pl.multiple_of(i * 2 * rows, 2 * rows), 2 * rows)
+            tile = low(product_right(first_ref[span], full_ref[...]))
+            partial_ref[2 * i] = tile[:rows]
+            partial_ref[2 * i + 1] = tile[rows:]
+            return carry
+
+        lax.fori_loop(0, count // 2, partial_tile, 0)
         line = line_task()
-        for stage in range(6):
-            for task in tasks:
+        for stage in range(5):
+            for task in tasks if stage < 4 else tasks[:1]:
                 next(task)
-            if stage:
-                next(line)
+            next(line)
         run_tasks(line, *tasks)
 
     shapes = [
         jax.ShapeDtypeStruct((rows, width), jnp.float32),
         jax.ShapeDtypeStruct(gain_grads.shape[1:], jnp.float32),
         jax.ShapeDtypeStruct((thin, columns - spread), jnp.float32),
-    ] + [jax.ShapeDtypeStruct((m.shape[0] // planes, m.shape[1]), jnp.float32) for m in matrices]
+    ] + [jax.ShapeDtypeStruct((m[0] // planes, m[1]), jnp.float32) for m in sizes]
     scratch = [pltpu.VMEM((count + 1, rows, width), jnp.bfloat16)]
     scratch += line_semaphores()
     scratch += [
@@ -1052,12 +1075,16 @@
         pltpu.SemaphoreType.DMA((count,)),
         pltpu.SemaphoreType.DMA((count,)),
     ]
-    for m in matrices:
-        scratch += plane_scatter_scratch(m.shape[0] // planes, m.shape[1])
+    for m in sizes:
+        scratch += plane_scatter_scratch(m[0] // planes, m[1])
+    scratch += [
+        pltpu.VMEM(first_full.shape, jnp.bfloat16),
+        pltpu.VMEM((count, rows, width), jnp.bfloat16),
+    ]
     results = pl.pallas_call(
         kernel,
         out_shape=shapes,
-        in_specs=[INSIDE, ANY] + [INSIDE] * 4 + [ANY] * number,
+        in_specs=[INSIDE] * 3 + [ANY] + [INSIDE] * 4 + [ANY] * len(matrices),
         out_specs=[INSIDE] * (3 + number),
         scratch_shapes=scratch,
         compiler_params=kernel_params(4),
@@ -1065,7 +1092,7 @@
             flops=60_000_000, bytes_accessed=200_000_000, transcendentals=0
         ),
         name="closing",
-    )(partial, ready_before, source, gain, grad_middle, gain_grads, *matrices)
+    )(grad_first, first_full, normed, ready_before, source, gain, grad_middle, gain_grads, *matrices)
     return results[:3], results[3:]
 
 
@@ -1345,7 +1372,7 @@
         branch_ref, out_ref, probs_ref, exp_ref, nope_ref, rope_ref, keys_ref, tiled_ref, up_ref = (
             refs[:9]
         )
-        dnope, drope, dlatent, dkey_rope, dup, dexp = refs[9:]
+        dnope, drope, dkeys, dup, dexp = refs[9:]
         dmixed = low(product(branch_ref[...], out_ref[...]))
         drope_sum = jnp.zeros((rows, rope), jnp.float32)
         dkey_sum = jnp.zeros((key_count, rope), jnp.float32)
@@ -1366,8 +1393,13 @@
             drope_sum = drope_sum + product(dscore, tiled_ref[...]) * mask
             dkey_sum = dkey_sum + product_left(dscore, rope_ref[...] * low(mask))
         drope[...] = drope_sum
-        dkey_rope[...] = dkey_sum
-        dlatent[...] = product_right(dexp[...], up_ref[...])
+        lane = lax.broadcasted_iota(jnp.int32, (rope, ROPE), 0)
+        column = lax.broadcasted_iota(jnp.int32, (rope, ROPE), 1)
+        half = ROPE // 2
+        target = lane // (rope // 2) * half + lax.rem(lane, half)
+        fold = low(jnp.where(target == column, 1.0, 0.0))
+        dkeys[:, :LATENT] = product_right(dexp[...], up_ref[...])
+        dkeys[:, LATENT:] = product(low(dkey_sum), fold)
         grad_up = product_left(keys_ref[:, :LATENT], dexp[...])
 
         @pl.when(pl.program_id(0) == 0)
@@ -1390,8 +1422,7 @@
     shapes = [
         jax.ShapeDtypeStruct((groups, rows, heads * NOPE), jnp.bfloat16),
         jax.ShapeDtypeStruct((groups, rows, rope), jnp.float32),
-        jax.ShapeDtypeStruct((groups, key_count, LATENT), jnp.float32),
-        jax.ShapeDtypeStruct((groups, key_count, rope), jnp.float32),
+        jax.ShapeDtypeStruct((groups, key_count, LATENT + ROPE), jnp.float32),
         jax.ShapeDtypeStruct(up.shape, jnp.float32),
     ]
     operands = [branch, out, probs, expanded, query_nope, query_rope, keys, tiled, up]
@@ -1400,7 +1431,7 @@
         grid=(groups,),
         out_shape=shapes,
         in_specs=[whole(x) if x is out or x is up else group(x) for x in operands],
-        out_specs=[group(x) for x in shapes[:4]] + [whole(up)],
+        out_specs=[group(x) for x in shapes[:3]] + [whole(up)],
         scratch_shapes=[pltpu.VMEM((key_count, heads * (NOPE + VDIM)), jnp.bfloat16)],
         compiler_params=pltpu.CompilerParams(vmem_limit_bytes=40 << 20),
         cost_estimate=pl.CostEstimate(
@@ -1664,7 +1695,7 @@
             branch_all.reshape(token_count, D), mixed_all.reshape(token_count, heads_local * VDIM)
         )
     )
-    grad_nope, grad_rope, grad_latent, grad_key_rope, grad_latent_up = attention_back(
+    grad_nope, grad_rope, grad_keys, grad_latent_up = attention_back(
         branch_all,
         out_local,
         probs,
@@ -1684,10 +1715,6 @@
         ],
         axis=-1,
     )
-    grad_key_rope = jnp.sum(
-        grad_key_rope.reshape(groups_local, key_count, 2, heads_local, half_rope), axis=3
-    ).reshape(groups_local, key_count, ROPE)
-    grad_keys = jnp.concatenate([grad_latent, grad_key_rope], axis=-1)
     grad_keys = grad_keys.reshape(groups_local, contexts + 1, PROMPT_DEV, down_cols)
 
     def keys_of(mask):
@@ -1709,11 +1736,6 @@
         ],
         axis=-1,
     )
-    grad_normed_part = low(against_rows(grad_first, first_full))
-
-    first_back = product_left(
-        normed_all.reshape(token_count, D), grad_first.reshape(token_count, first_full.shape[1])
-    )
     gain_rows = jnp.concatenate(
         [
             jnp.zeros((plane_count, 1, shard_rows), jnp.float32),
@@ -1731,13 +1753,15 @@
         middle + axis_scatter(branch_out.reshape(groups_local, TOK_DEV, D), EXPERT_AXIS)
     )
     (grad_tokens, gain_sum, down_own), sums = closing(
-        grad_normed_part,
+        grad_first.reshape(token_count, -1),
+        first_full,
+        normed_all.reshape(token_count, D),
         block_out,
         tokens[0],
         full_attn_gain[None],
         grad_middle,
         gain_rows,
-        [low(first_back), low(grad_latent_up), grad_out_weight],
+        [low(grad_latent_up), grad_out_weight],
         query_cols // 128 * 128,
     )
     first_sum, up_sum, out_sum = sums

time: 749 us -> 740 us (0.988)
  matrix products: 50.7 us -> 37.5 us
  local copies, waits for them, and re-layouts: 59.8 us -> 50.1 us
  Pallas kernels: 568 us -> 576 us
  waiting for transfers between devices: 7.49 us -> 15.1 us
    ppermute x12, waiting for transfers between devices: 7.45 us -> 15.1 us  [swap(): return lax.ppermute(values, axis, [(i, i ^ mask) for i in range(count)])]
    dot_general x1 -> x0, matrix products: 7.55 us -> none  [against_rows(): lax.dot_general(left_side, right_side, (((left_side.ndim - 1,), (1,)), ((...]
    dot_general x4 -> x3, matrix products: 16.2 us -> 10.9 us  [product_left(): lax.dot_general(left_side, right_side, (((0,), (0,)), ((), ())), preferre...]
    unnamed x159 -> x127, local copies, waits for them, and re-layouts: 21.1 us -> 15.7 us
  transfers between devices with their start and end apart: 14 -> 14, of which waited for: 2 -> 3; matrix products, arithmetic and copies ran while one was open for 14% -> 12% of each run, Pallas kernels for 37% -> 39%
where the time goes in v3:
time: 740 us; the launch traced here: 731 us
  Pallas kernels  576 us (78%)
  local copies, waits for them, and re-layouts  50.1 us (7%)
  matrix products  37.5 us (5%)
  other arithmetic  24.5 us (3%)
  between operations  15.8 us (2%)
  waiting for transfers between devices  15.1 us (2%)
  starting transfers between devices  12.5 us (2%)
    pallas_call x1, Pallas kernels, middle_sum(): pl.pallas_call(kernel, out_shape=shapes, in_specs=[INSIDE] * 8 + [ANY] *...  118 us
    pallas_call x1, Pallas kernels, branch_sum(): pl.pallas_call(kernel, out_shape=shapes, in_specs=[INSIDE] * 4 + [ANY] *...  103 us
    pallas_call x1, Pallas kernels, routed_expert(): pl.pallas_call(kernel, out_shape=shapes, in_specs=[ANY] * len(operands) +...  102 us
    pallas_call x1, Pallas kernels, shared_and_rows(): pl.pallas_call(kernel, out_shape=shapes, in_specs=[ANY] * 5 + [INSIDE], o...  87.4 us
    pallas_call x1, Pallas kernels, closing(): pl.pallas_call(kernel, out_shape=shapes, in_specs=[INSIDE] * 3 + [ANY] +...  77.3 us
    pallas_call x1, Pallas kernels, opening(): pl.pallas_call(kernel, out_shape=shapes, in_specs=[INSIDE] * (2 + number)...  72 us
    dot_general x4, matrix products, product(): return jnp.dot(left_side, right_side, preferred_element_type=jnp.float32)  16.9 us
    unnamed x127, local copies, waits for them, and re-layouts  15.7 us
  transfers between devices with their start and end apart: 14, of which 3 were waited for; matrix products, arithmetic and copies ran while one was open for 12% of the time, Pallas kernels for 39%

profile of v3, /device:TPU:0, one launch (start us, length us, event | category | flops | bytes accessed | tf_op | source)
XLA Modules:
  0.0 731.2 jit_solution(648045919210508155)
XLA Ops:
  14.2 72.0 %opening.1 = (f32[8,8,256]{2,1,0:T(8,128)S(1)}, bf16[4,128,2048]{2,1,0:T(8,128)(2,1)}, bf16[2048,1408]{1,0:T(8,128)(2,1)}, bf16[512,1024]{1,0:T(8,128)(2,1)}, bf16[2048,512]{1,0:T(8,128)(2,1)}) custom-call(bf16[128,2048]{1,0:T(8,128)(2,1)S(1)} %bitcast.170, f32[8,256]{1,0:T(8,128)S(1)} %stack.31.refs_1_, bf16[256,1408]{1,0:T(8,128)(2,1)S(1)} %concatenate.32.refs_2_, ...), custom_call_target="tpu_custom_call" | custom-call | flops 60000000 | bytes 150000000 | tf_op jit(solution)/shard_map/opening/pallas_call | solution.py:524
  86.3 6.4 fusion
  99.3 2.6 collective-permute-start.4
  109.4 4.4 collective-permute-done.5
  120.1 3.5 concatenate.35.refs_3_.refs_7_
  123.6 118.4 %middle_sum.1 = (f32[128,2048]{1,0:T(8,128)}, bf16[4,128,2048]{2,1,0:T(8,128)(2,1)}, bf16[4,128,2048]{2,1,0:T(8,128)(2,1)}, bf16[4,128,512]{2,1,0:T(8,128)(2,1)S...) custom-call(bf16[4,128,512]{2,1,0:T(8,128)(2,1)S(1)} %slice.210.refs, ...), custom_call_target="tpu_custom_call" | custom-call | flops 60000000 | bytes 300000000 | tf_op jit(solution)/shard_map/middle_sum/pallas_call | solution.py:655
  242.1 2.7 fusion.45
  245.3 3.9 convolution_convert_fusion.1
  249.2 3.9 convolution_convert_fusion
  253.1 87.4 %shared_and_rows.1 = (bf16[512,768]{1,0:T(8,128)(2,1)S(1)}, f32[512,2048]{1,0:T(8,128)}, bf16[2048,2304]{1,0:T(8,128)(2,1)}, f32[3,8,256]{2,1,0:T(8,128)S(1)}, b...) custom-call(bf16[512,2048]{1,0:T(8,128)(2,1)} %bitcast.183, bf16[512,2048]{1,0:T(8,128)(2,1)} %bitcast.217, ...), custom_call_target="tpu_custom_call" | custom-call | flops 9663676416 | bytes 120000000 | tf_op jit(solution)/shard_map/shared_and_rows/pallas_call | solution.py:1192
  341.6 102.3 %routed_expert.1 = (bf16[4,224,2048]{2,1,0:T(8,128)(2,1)}, bf16[4,224,2048]{2,1,0:T(8,128)(2,1)}, f32[4,224,128]{2,1,0:T(8,128)}, bf16[2048,1408]{1,0:T(8,128)(2...) custom-call(bf16[4,224,2048]{2,1,0:T(8,128)(2,1)} %bitcast.220, bf16[4,224,2048]{2,1,0:T(8,128)(2,1)} %bitcast.222, ...), custom_call_target="tpu_custom_call" | custom-call | flops 46506442752 | bytes 200000000 | tf_op jit(solution)/shard_map/routed_expert/pallas_call | solution.py:1346
  445.6 3.3 fusion.23
  448.9 5.9 fusion.3
  454.8 102.8 %branch_sum.1 = (f32[128,2048]{1,0:T(8,128)S(1)}, f32[1,2048]{1,0:T(1,128)S(1)}, bf16[4,128,2048]{2,1,0:T(8,128)(2,1)}, bf16[4,256,1408]{2,1,0:T(8,128)(2,1)}, b...) custom-call(bf16[4,128,2048]{2,1,0:T(8,128)(2,1)} %bitcast.191, ...), custom_call_target="tpu_custom_call", output_to_operand_aliasing={{6}: (7, {}), {7}: (8, {})} | custom-call | flops 60000000 | bytes 300000000 | tf_op jit(solution)/shard_map/branch_sum/pallas_call | solution.py:891
  559.0 3.9 copy.210
  562.9 4.0 fusion.4
  570.6 2.6 collective-permute-start.8
  573.6 15.5 %attention_back.1 = (bf16[4,128,512]{2,1,0:T(8,128)(2,1)S(1)}, f32[4,128,256]{2,1,0:T(8,128)S(1)}, f32[4,320,576]{2,1,0:T(8,128)}, f32[512,1024]{1,0:T(8,128)S(1)}) custom-call(bf16[4,128,2048]{2,1,0:T(8,128)(2,1)S(1)} %copy-done.10, bf16[2048,512]{1,0:T(8,128)(2,1)S(1)} %copy-done.5, bf16[4,4,128,320]{3,2,1,0:T(8,128)(2,1)S(1)} %copy-done.11, ...), custom_call_target="tpu_custom_call" | custom-call | flops 20000000000 | bytes 30000000 | tf_op jit(solution)/shard_map/attention_back/pallas_call | solution.py:1429
  594.1 2.6 bitcast_convert_fusion.refs_9_
  598.8 2.9 convert_element_type.143
  601.8 3.0 convert_element_type.144
  604.9 3.3 convert_element_type.145
  612.2 10.0 %collective-permute-done.10 = bf16[4,64,576]{2,1,0:T(8,128)(2,1)S(1)} collective-permute-done((bf16[4,64,576]{2,1,0:T(8,128)(2,1)S(1)}, bf16[4,64,576]{2,1,0:T(8,128)(2,1)S(1)}, u32[]{:S(2)}, u32[]{:S(2)}) %collective-permute-start.10) | collective-permute-done | bytes 294944 | tf_op jit(solution)/shard_map/ppermute | solution.py:79
  632.8 77.3 %closing.1 = (f32[128,2048]{1,0:T(8,128)}, f32[24,256]{1,0:T(8,128)S(1)}, f32[64,640]{1,0:T(8,128)S(1)}, f32[256,1408]{1,0:T(8,128)}, f32[64,1024]{1,0:T(8,128)S(1)}, /*index=5*/f32[256,512]{1,0:T(8,128)S(1)}) custom-call(bf16[512,1408]{1,0:T(8,128)(2,1)} %bitcast.187, bf16[2048,1408]{1,0:T(8,128)(2,1)} %get-tuple-element.61.refs_1_, ...), custom_call_target="tpu_custom_call" | custom-call | flops 60000000 | bytes 200000000 | tf_op jit(solution)/shard_map/closing/pallas_call | solution.py:1084
  (262 shorter events, 70.8 us)
Async XLA Ops:
  7.2 245.9 %all-gather.2.cloned.1.call-start = ((), (), s32[]{:S(2)}) async-start(), calls=%async_computation.1 | async-start | bytes 10616832 | tf_op jit(solution)/shard_map/all_gather | solution.py:1533
  12.0 704.8 %reduce-scatter.2.cloned.1.call-start = ((), (), s32[]{:S(2)}) async-start(), calls=%async_computation.2 | async-start | bytes 10616832 | tf_op jit(solution)/shard_map/reduce_scatter | solution.py:1688
  13.7 79.1 %copy-start.24 = (f32[128,32]{1,0:T(8,128)}, f32[128,32]{1,0:T(8,128)S(1)}, u32[]{:S(2)}) copy-start(f32[128,32]{1,0:T(8,128)S(1)} %copy.180) | copy-start | bytes 49156
  86.3 6.8 copy-start.40
  94.3 10.0 %copy-start.17 = (bf16[4,128,576]{2,1,0:T(8,128)(2,1)}, bf16[4,128,576]{2,1,0:T(8,128)(2,1)S(1)}, u32[]{:S(2)}) copy-start(bf16[4,128,576]{2,1,0:T(8,128)(2,1)S(1)} %pad_maximum_fusion.2) | copy-start | bytes 1769476
  95.1 20.1 %collective-permute-start = (bf16[4,64,576]{2,1,0:T(8,128)(2,1)}, bf16[4,64,576]{2,1,0:T(8,128)(2,1)}, u32[]{:S(2)}, u32[]{:S(2)}) collective-permute-start(bf16[4,64,576]{2,1,0:T(8,128)(2,1)} %slice.167), channel_id=1, source_target_pairs={{0,4},{4,0},{8,12},{12,8},{1,5},{5,1},{9,13},{13,9},{2,6},{6,2},{1... | collective-permute-start | bytes 884744 | tf_op jit(solution)/shard_map/ppermute | solution.py:79
  95.5 20.7 %collective-permute-start.1 = (bf16[4,64,576]{2,1,0:T(8,128)(2,1)}, bf16[4,64,576]{2,1,0:T(8,128)(2,1)}, u32[]{:S(2)}, u32[]{:S(2)}) collective-permute-start(bf16[4,64,576]{2,1,0:T(8,128)(2,1)} %slice.167), channel_id=1, source_target_pairs={{0,8},{4,12},{8,0},{12,4},{1,9},{5,13},{9,1},{13,5},{2,10},{6,14},... | collective-permute-start | bytes 884744 | tf_op jit(solution)/shard_map/ppermute | solution.py:79
  96.0 21.2 %collective-permute-start.2 = (bf16[4,64,576]{2,1,0:T(8,128)(2,1)}, bf16[4,64,576]{2,1,0:T(8,128)(2,1)}, u32[]{:S(2)}, u32[]{:S(2)}) collective-permute-start(bf16[4,64,576]{2,1,0:T(8,128)(2,1)} %slice.167), channel_id=1, source_target_pairs={{0,12},{4,8},{8,4},{12,0},{1,13},{5,9},{9,5},{13,1},{2,14},{6,10},... | collective-permute-start | bytes 884744 | tf_op jit(solution)/shard_map/ppermute | solution.py:79
  97.7 9.7 %collective-permute-start.3 = (s32[128,6]{1,0:T(8,128)}, s32[128,6]{1,0:T(8,128)}, u32[]{:S(2)}, u32[]{:S(2)}) collective-permute-start(s32[128,6]{1,0:T(8,128)} %bitcast.28), channel_id=1, source_target_pairs={{0,1},{1,0},{2,3},{3,2},{4,5},{5,4},{6,7},{7,6},{8,9},{9,8},{10,11... | collective-permute-start | bytes 9224 | tf_op jit(solution)/shard_map/ppermute | solution.py:79
  99.3 9.2 %collective-permute-start.4 = (s32[128,6]{1,0:T(8,128)}, s32[128,6]{1,0:T(8,128)}, u32[]{:S(2)}, u32[]{:S(2)}) collective-permute-start(s32[128,6]{1,0:T(8,128)} %bitcast.28), channel_id=1, source_target_pairs={{0,2},{1,3},{2,0},{3,1},{4,6},{5,7},{6,4},{7,5},{8,10},{9,11},{10,... | collective-permute-start | bytes 9224 | tf_op jit(solution)/shard_map/ppermute | solution.py:79
  107.4 6.3 collective-permute-start.5
  253.1 87.4 %slice-start = ((f32[4,224]{1,0:T(4,128)}), f32[1,224]{1,0:T(1,128)S(1)}, s32[]{:S(2)}) async-start(f32[4,224]{1,0:T(4,128)} %copy-done.44), calls=%async_computation.3 | async-start | bytes 2048 | tf_op jit(solution)/shard_map/slice | solution.py:1646
  566.9 6.3 copy-start.5
  570.6 59.1 %collective-permute-start.8 = (bf16[128,2048]{1,0:T(8,128)(2,1)}, bf16[128,2048]{1,0:T(8,128)(2,1)}, u32[]{:S(2)}, u32[]{:S(2)}) collective-permute-start(bf16[128,2048]{1,0:T(8,128)(2,1)} %get-tuple-element.197), channel_id=1, source_target_pairs={{0,3},{1,2},{2,1},{3,0},{4,7},{5,6},{6,5},{7,4},{8,11},{9,10},{10,... | collective-permute-start | bytes 1572872 | tf_op jit(solution)/shard_map/ppermute | solution.py:79
  573.2 56.5 %collective-permute-start.7 = (bf16[128,2048]{1,0:T(8,128)(2,1)}, bf16[128,2048]{1,0:T(8,128)(2,1)}, u32[]{:S(2)}, u32[]{:S(2)}) collective-permute-start(bf16[128,2048]{1,0:T(8,128)(2,1)} %get-tuple-element.198), channel_id=1, source_target_pairs={{0,2},{1,3},{2,0},{3,1},{4,6},{5,7},{6,4},{7,5},{8,10},{9,11},{10,... | collective-permute-start | bytes 1572872 | tf_op jit(solution)/shard_map/ppermute | solution.py:79
  591.0 19.6 %collective-permute-start.11 = (bf16[4,64,576]{2,1,0:T(8,128)(2,1)S(1)}, bf16[4,64,576]{2,1,0:T(8,128)(2,1)S(1)}, u32[]{:S(2)}, u32[]{:S(2)}) collective-permute-start(bf16[4,64,576]{2,1,0:T(8,128)(2,1)S(1)} %get-tuple-element.190), channel_id=1, source_target_pairs={{0,12},{4,8},{8,4},{12,0},{1,13},{5,9},{9,5},{13,1},{2,14},{6,10},... | collective-permute-start | bytes 884744 | tf_op jit(solution)/shard_map/ppermute | solution.py:79
  592.0 30.2 %collective-permute-start.10 = (bf16[4,64,576]{2,1,0:T(8,128)(2,1)S(1)}, bf16[4,64,576]{2,1,0:T(8,128)(2,1)S(1)}, u32[]{:S(2)}, u32[]{:S(2)}) collective-permute-start(bf16[4,64,576]{2,1,0:T(8,128)(2,1)S(1)} %get-tuple-element.191), channel_id=1, source_target_pairs={{0,8},{4,12},{8,0},{12,4},{1,9},{5,13},{9,1},{13,5},{2,10},{6,14},... | collective-permute-start | bytes 884744 | tf_op jit(solution)/shard_map/ppermute | solution.py:79
  592.7 29.5 %collective-permute-start.9 = (bf16[4,64,576]{2,1,0:T(8,128)(2,1)S(1)}, bf16[4,64,576]{2,1,0:T(8,128)(2,1)S(1)}, u32[]{:S(2)}, u32[]{:S(2)}) collective-permute-start(bf16[4,64,576]{2,1,0:T(8,128)(2,1)S(1)} %get-tuple-element.189), channel_id=1, source_target_pairs={{0,4},{4,0},{8,12},{12,8},{1,5},{5,1},{9,13},{13,9},{2,6},{6,2},{1... | collective-permute-start | bytes 884744 | tf_op jit(solution)/shard_map/ppermute | solution.py:79
  608.2 15.2 %copy-start.41 = (f32[512]{0:T(512)S(1)}, f32[512]{0:T(512)}, u32[]{:S(2)}) copy-start(f32[512]{0:T(512)} %copy-done.40) | copy-start | bytes 6148
  608.2 15.2 %copy-start.43 = (f32[4,128]{1,0:T(4,128)S(1)}, f32[4,128]{1,0:T(4,128)}, u32[]{:S(2)}) copy-start(f32[4,128]{1,0:T(4,128)} %copy-done.42) | copy-start | bytes 6148
  610.6 14.5 %copy-start.46 = (f32[4,128]{1,0:T(4,128)S(1)}, f32[4,128]{1,0:T(4,128)}, u32[]{:S(2)}) copy-start(f32[4,128]{1,0:T(4,128)} %copy-done.45) | copy-start | bytes 6148
  610.6 14.5 %copy-start.25 = (f32[128,32]{1,0:T(8,128)S(1)}, f32[128,32]{1,0:T(8,128)}, u32[]{:S(2)}) copy-start(f32[128,32]{1,0:T(8,128)} %copy-done.24) | copy-start | bytes 49156
  610.6 19.7 %collective-permute-start.6 = (bf16[128,2048]{1,0:T(8,128)(2,1)}, bf16[128,2048]{1,0:T(8,128)(2,1)}, u32[]{:S(2)}, u32[]{:S(2)}) collective-permute-start(bf16[128,2048]{1,0:T(8,128)(2,1)} %get-tuple-element.196), channel_id=1, source_target_pairs={{0,1},{1,0},{2,3},{3,2},{4,5},{5,4},{6,7},{7,6},{8,9},{9,8},{10,11... | collective-permute-start | bytes 1572872 | tf_op jit(solution)/shard_map/ppermute | solution.py:79
  632.8 77.4 %copy-start.6 = (bf16[128,2048]{1,0:T(8,128)(2,1)}, bf16[128,2048]{1,0:T(8,128)(2,1)S(1)}, u32[]{:S(2)}) copy-start(bf16[128,2048]{1,0:T(8,128)(2,1)S(1)} %fusion.19.refs_3_) | copy-start | bytes 1572868
  (46 other events, 140.5 us)
Sparse Core Ops, SparseCore 0:
  12.1 85.8 all-gather.1
  558.7 88.7 reduce-scatter.1

commit v4 on v3

--- a/solution.py
+++ b/solution.py
@@ -536,12 +536,20 @@
     return results[0], results[1], results[2:]
 
 
+def rope_fold(rope):
+    lane = lax.broadcasted_iota(jnp.int32, (rope, ROPE), 0)
+    column = lax.broadcasted_iota(jnp.int32, (rope, ROPE), 1)
+    half = ROPE // 2
+    target = lane // (rope // 2) * half + lax.rem(lane, half)
+    return low(jnp.where(target == column, 1.0, 0.0))
+
+
 def head_mask(head, heads, rope):
     lanes = lax.broadcasted_iota(jnp.int32, (1, rope), 1)
     return jnp.where(lax.rem(lanes, rope // 2) // (ROPE // 2) == head, 1.0, 0.0)
 
 
-def middle_sum(query_nope, query_rope, keys, tiled, up, out, source, gain, experts, grads):
+def middle_sum(query_nope, query_rope, keys, up, out, source, gain, experts, grads):
     count, rows = query_nope.shape[:2]
     key_count, rope = keys.shape[1], query_rope.shape[2]
     heads = query_nope.shape[2] // NOPE
@@ -551,10 +559,10 @@
     score_scale = (NOPE + ROPE) ** (-0.5)
 
     def kernel(*refs):
-        nope_ref, rope_ref, keys_ref, tiled_ref, up_ref, out_ref, source_ref, gain_ref = refs[:8]
-        expert_refs = refs[8 : 8 + routed]
-        grads_ref = refs[8 + routed]
-        outputs = refs[9 + routed :]
+        nope_ref, rope_ref, keys_ref, up_ref, out_ref, source_ref, gain_ref = refs[:7]
+        expert_refs = refs[7 : 7 + routed]
+        grads_ref = refs[7 + routed]
+        outputs = refs[8 + routed :]
         middle_ref, hidden_all, grads_all, mixed, probs, expanded = outputs[:6]
         targets = outputs[6 : 6 + routed]
         scratch = list(outputs[6 + routed :])
@@ -612,13 +620,14 @@
 
         def attend(g, carry):
             expanded[g] = low(product(keys_ref[g, :, :LATENT], up_ref[...]))
+            tiled = low(product_right(keys_ref[g, :, LATENT:], rope_fold(rope)))
             for h in range(heads):
                 start = h * (NOPE + VDIM)
                 scores = product_right(
                     nope_ref[g, :, h * NOPE : (h + 1) * NOPE],
                     expanded[g, :, start : start + NOPE],
                 ) + product_right(
-                    rope_ref[g] * low(head_mask(h, heads, rope)), tiled_ref[g]
+                    rope_ref[g] * low(head_mask(h, heads, rope)), tiled
                 )
                 scores = jnp.where(allowed, scores * score_scale, -1e30)
                 powers = jnp.exp(scores - jnp.max(scores, axis=-1, keepdims=True))
@@ -655,7 +664,7 @@
     results = pl.pallas_call(
         kernel,
         out_shape=shapes,
-        in_specs=[INSIDE] * 8 + [ANY] * routed + [INSIDE],
+        in_specs=[INSIDE] * 7 + [ANY] * routed + [INSIDE],
         out_specs=[INSIDE, ANY, ANY] + [INSIDE] * 3 + [ANY] * routed,
         scratch_shapes=scratch,
         compiler_params=kernel_params(2),
@@ -663,7 +672,7 @@
             flops=60_000_000, bytes_accessed=300_000_000, transcendentals=0
         ),
         name="middle_sum",
-    )(query_nope, query_rope, keys, tiled, up, out, source, gain, *experts, grads)
+    )(query_nope, query_rope, keys, up, out, source, gain, *experts, grads)
     return results[:6], results[6:]
 
 
@@ -1232,13 +1241,21 @@
             loads[number] = pltpu.make_async_copy(source, target, load.at[number])
             loads[number].start()
 
+        def fetch_rows(number, source, source_far, target, k):
+            span = pl.ds(k * slots, slots)
+            fetch(number + k, piece(source, source_far, k), target.at[span])
+
         fetch(0, wg_any, wg)
-        for k in (3, 2, 1, 0):
-            fetch(3 + k, piece(hidden_any, hidden_far_any, k), hid.at[pl.ds(k * slots, slots)])
+        fetch_rows(3, hidden_any, hidden_far_any, hid, 3)
+        loads[0].wait()
+        loads[6].wait()
         fetch(1, wu_any, wu)
         fetch(2, wd_any, wd)
         for k in (3, 2, 1, 0):
-            fetch(7 + k, piece(grad_any, grad_far_any, k), grd.at[pl.ds(k * slots, slots)])
+            fetch_rows(7, grad_any, grad_far_any, grd, k)
+            if k < 3:
+                fetch_rows(3, hidden_any, hidden_far_any, hid, k)
+
         def back(k, which):
             source, target = ((pair, pair_back), (result, result_back), (scale, scale_back))[which]
             return remote(
@@ -1263,11 +1280,10 @@
                     for number in numbers:
                         loads[number].wait()
 
-            ready(0, 6, 5, 4, 3)
             gate = product(hid[span], wg[...])
             ready(1)
             up = product(hid[span], wu[...])
-            ready(2, 10, 9, 8, 7)
+            ready(2, 10, 9, 8, 7, 5, 4, 3)
             grad = product_right(grd[span], wd[...])
             gates_here = gates_ref[span]
             act_part, dgate_part, dup_part = silu_back(gate, up, grad)
@@ -1362,17 +1378,17 @@
     return results
 
 
-def attention_back(branch, out, probs, expanded, query_nope, query_rope, keys, tiled, up):
+def attention_back(branch, out, probs, expanded, query_nope, query_rope, keys, up):
     groups, rows, width = branch.shape
     heads, key_count = probs.shape[1], probs.shape[3]
     rope = query_rope.shape[2]
     score_scale = (NOPE + ROPE) ** (-0.5)
 
     def kernel(*refs):
-        branch_ref, out_ref, probs_ref, exp_ref, nope_ref, rope_ref, keys_ref, tiled_ref, up_ref = (
-            refs[:9]
-        )
-        dnope, drope, dkeys, dup, dexp = refs[9:]
+        branch_ref, out_ref, probs_ref, exp_ref, nope_ref, rope_ref, keys_ref, up_ref = refs[:8]
+        dnope, drope, dkeys, dup, dexp = refs[8:]
+        fold = rope_fold(rope)
+        tiled = low(product_right(keys_ref[:, LATENT:], fold))
         dmixed = low(product(branch_ref[...], out_ref[...]))
         drope_sum = jnp.zeros((rows, rope), jnp.float32)
         dkey_sum = jnp.zeros((key_count, rope), jnp.float32)
@@ -1390,14 +1406,9 @@
             dexp[:, key_span] = low(product_left(dscore, nope_ref[:, nope_span]))
             dexp[:, value_span] = low(product_left(weights, part))
             dnope[:, nope_span] = low(product(dscore, exp_ref[:, key_span]))
-            drope_sum = drope_sum + product(dscore, tiled_ref[...]) * mask
+            drope_sum = drope_sum + product(dscore, tiled) * mask
             dkey_sum = dkey_sum + product_left(dscore, rope_ref[...] * low(mask))
         drope[...] = drope_sum
-        lane = lax.broadcasted_iota(jnp.int32, (rope, ROPE), 0)
-        column = lax.broadcasted_iota(jnp.int32, (rope, ROPE), 1)
-        half = ROPE // 2
-        target = lane // (rope // 2) * half + lax.rem(lane, half)
-        fold = low(jnp.where(target == column, 1.0, 0.0))
         dkeys[:, :LATENT] = product_right(dexp[...], up_ref[...])
         dkeys[:, LATENT:] = product(low(dkey_sum), fold)
         grad_up = product_left(keys_ref[:, :LATENT], dexp[...])
@@ -1425,7 +1436,7 @@
         jax.ShapeDtypeStruct((groups, key_count, LATENT + ROPE), jnp.float32),
         jax.ShapeDtypeStruct(up.shape, jnp.float32),
     ]
-    operands = [branch, out, probs, expanded, query_nope, query_rope, keys, tiled, up]
+    operands = [branch, out, probs, expanded, query_nope, query_rope, keys, up]
     return pl.pallas_call(
         kernel,
         grid=(groups,),
@@ -1584,11 +1595,6 @@
             axis=-1,
         )
     )
-    tiled_rope = jnp.concatenate(
-        [keys[..., LATENT : LATENT + half_rope]] * heads_local
-        + [keys[..., LATENT + half_rope :]] * heads_local,
-        axis=-1,
-    )
     slot_experts = expert_index * local_experts + (
         expert_own ^ jnp.arange(local_experts, dtype=jnp.int32)
     )
@@ -1615,7 +1621,6 @@
         query_nope,
         query_rope,
         keys,
-        tiled_rope,
         up_local,
         out_local,
         tokens[0],
@@ -1703,7 +1708,6 @@
         query_nope,
         query_rope,
         keys,
-        tiled_rope,
         up_local,
     )
     lower, upper = grad_rope[..., :rope_cols], grad_rope[..., rope_cols:]

time: 740 us -> 737 us (level)
    unnamed x127 -> x129, local copies, waits for them, and re-layouts: 15.7 us -> 17.7 us
  transfers between devices with their start and end apart: 14 -> 14, of which waited for: 3 -> 2; matrix products, arithmetic and copies ran while one was open for 12% -> 11% of each run, Pallas kernels for 39% -> 39%
where the time goes in v4:
time: 737 us; the launch traced here: 728 us
  Pallas kernels  577 us (78%)
  local copies, waits for them, and re-layouts  48 us (7%)
  matrix products  38.5 us (5%)
  other arithmetic  23.1 us (3%)
  between operations  15.8 us (2%)
  waiting for transfers between devices  14.3 us (2%)
  starting transfers between devices  11.5 us (2%)
    pallas_call x1, Pallas kernels, middle_sum(): pl.pallas_call(kernel, out_shape=shapes, in_specs=[INSIDE] * 7 + [ANY] *...  119 us
    pallas_call x1, Pallas kernels, routed_expert(): pl.pallas_call(kernel, out_shape=shapes, in_specs=[ANY] * len(operands) +...  103 us
    pallas_call x1, Pallas kernels, branch_sum(): pl.pallas_call(kernel, out_shape=shapes, in_specs=[INSIDE] * 4 + [ANY] *...  103 us
    pallas_call x1, Pallas kernels, shared_and_rows(): pl.pallas_call(kernel, out_shape=shapes, in_specs=[ANY] * 5 + [INSIDE], o...  87.4 us
    pallas_call x1, Pallas kernels, closing(): pl.pallas_call(kernel, out_shape=shapes, in_specs=[INSIDE] * 3 + [ANY] +...  77.3 us
    pallas_call x1, Pallas kernels, opening(): pl.pallas_call(kernel, out_shape=shapes, in_specs=[INSIDE] * (2 + number)...  72 us
    unnamed x129, local copies, waits for them, and re-layouts  17.7 us
    dot_general x4, matrix products, product(): return jnp.dot(left_side, right_side, preferred_element_type=jnp.float32)  16.9 us
  transfers between devices with their start and end apart: 14, of which 2 were waited for; matrix products, arithmetic and copies ran while one was open for 11% of the time, Pallas kernels for 39%

profile of v4, /device:TPU:0, one launch (start us, length us, event | category | flops | bytes accessed | tf_op | source)
XLA Modules:
  0.0 728.3 jit_solution(14949275450063869721)
XLA Ops:
  14.2 72.0 %opening.1 = (f32[8,8,256]{2,1,0:T(8,128)S(1)}, bf16[4,128,2048]{2,1,0:T(8,128)(2,1)}, bf16[2048,1408]{1,0:T(8,128)(2,1)}, bf16[512,1024]{1,0:T(8,128)(2,1)}, bf16[2048,512]{1,0:T(8,128)(2,1)}) custom-call(bf16[128,2048]{1,0:T(8,128)(2,1)S(1)} %bitcast.168, f32[8,256]{1,0:T(8,128)S(1)} %stack.31.refs_1_, bf16[256,1408]{1,0:T(8,128)(2,1)S(1)} %concatenate.29.refs_2_, ...), custom_call_target="tpu_custom_call" | custom-call | flops 60000000 | bytes 150000000 | tf_op jit(solution)/shard_map/opening/pallas_call | solution.py:524
  86.3 6.4 fusion
  99.3 2.6 collective-permute-start.4
  109.4 4.4 collective-permute-done.5
  118.8 119.0 %middle_sum.1 = (f32[128,2048]{1,0:T(8,128)}, bf16[4,128,2048]{2,1,0:T(8,128)(2,1)}, bf16[4,128,2048]{2,1,0:T(8,128)(2,1)}, bf16[4,128,512]{2,1,0:T(8,128)(2,1)S...) custom-call(bf16[4,128,512]{2,1,0:T(8,128)(2,1)S(1)} %slice.195.refs, ...), custom_call_target="tpu_custom_call" | custom-call | flops 60000000 | bytes 300000000 | tf_op jit(solution)/shard_map/middle_sum/pallas_call | solution.py:664
  237.8 2.7 fusion.44
  240.9 3.9 convolution_convert_fusion.1
  244.8 3.9 convolution_convert_fusion
  248.8 87.4 %shared_and_rows.1 = (bf16[512,768]{1,0:T(8,128)(2,1)S(1)}, f32[512,2048]{1,0:T(8,128)}, bf16[2048,2304]{1,0:T(8,128)(2,1)}, f32[3,8,256]{2,1,0:T(8,128)S(1)}, b...) custom-call(bf16[512,2048]{1,0:T(8,128)(2,1)} %bitcast.181, bf16[512,2048]{1,0:T(8,128)(2,1)} %bitcast.215, ...), custom_call_target="tpu_custom_call" | custom-call | flops 9663676416 | bytes 120000000 | tf_op jit(solution)/shard_map/shared_and_rows/pallas_call | solution.py:1201
  337.3 103.2 %routed_expert.1 = (bf16[4,224,2048]{2,1,0:T(8,128)(2,1)}, bf16[4,224,2048]{2,1,0:T(8,128)(2,1)}, f32[4,224,128]{2,1,0:T(8,128)}, bf16[2048,1408]{1,0:T(8,128)(2...) custom-call(bf16[4,224,2048]{2,1,0:T(8,128)(2,1)} %bitcast.218, bf16[4,224,2048]{2,1,0:T(8,128)(2,1)} %bitcast.220, ...), custom_call_target="tpu_custom_call" | custom-call | flops 46506442752 | bytes 200000000 | tf_op jit(solution)/shard_map/routed_expert/pallas_call | solution.py:1362
  442.2 3.3 fusion.23
  445.5 6.1 fusion.3
  451.7 102.8 %branch_sum.1 = (f32[128,2048]{1,0:T(8,128)S(1)}, f32[1,2048]{1,0:T(1,128)S(1)}, bf16[4,128,2048]{2,1,0:T(8,128)(2,1)}, bf16[4,256,1408]{2,1,0:T(8,128)(2,1)}, b...) custom-call(bf16[4,128,2048]{2,1,0:T(8,128)(2,1)} %bitcast.189, ...), custom_call_target="tpu_custom_call", output_to_operand_aliasing={{6}: (7, {}), {7}: (8, {})} | custom-call | flops 60000000 | bytes 300000000 | tf_op jit(solution)/shard_map/branch_sum/pallas_call | solution.py:900
  555.9 4.2 copy.210
  560.1 4.7 fusion.4
  571.0 15.5 %attention_back.1 = (bf16[4,128,512]{2,1,0:T(8,128)(2,1)S(1)}, f32[4,128,256]{2,1,0:T(8,128)S(1)}, f32[4,320,576]{2,1,0:T(8,128)}, f32[512,1024]{1,0:T(8,128)S(1)}) custom-call(bf16[4,128,2048]{2,1,0:T(8,128)(2,1)S(1)} %copy-done.9, bf16[2048,512]{1,0:T(8,128)(2,1)S(1)} %copy-done.4, bf16[4,4,128,320]{3,2,1,0:T(8,128)(2,1)S(1)} %copy-done.10, ...), custom_call_target="tpu_custom_call" | custom-call | flops 20000000000 | bytes 30000000 | tf_op jit(solution)/shard_map/attention_back/pallas_call | solution.py:1440
  591.2 2.6 bitcast_convert_fusion.refs_9_
  595.8 3.0 convert_element_type.143
  598.9 2.9 convert_element_type.144
  601.9 3.3 convert_element_type.145
  605.2 2.4 convolution_bitcast_fusion
  609.5 9.9 %collective-permute-done.10 = bf16[4,64,576]{2,1,0:T(8,128)(2,1)S(1)} collective-permute-done((bf16[4,64,576]{2,1,0:T(8,128)(2,1)S(1)}, bf16[4,64,576]{2,1,0:T(8,128)(2,1)S(1)}, u32[]{:S(2)}, u32[]{:S(2)}) %collective-permute-start.10) | collective-permute-done | bytes 294944 | tf_op jit(solution)/shard_map/ppermute | solution.py:79
  624.9 2.9 concatenate.35
  630.0 77.3 %closing.1 = (f32[128,2048]{1,0:T(8,128)}, f32[24,256]{1,0:T(8,128)S(1)}, f32[64,640]{1,0:T(8,128)S(1)}, f32[256,1408]{1,0:T(8,128)}, f32[64,1024]{1,0:T(8,128)S(1)}, /*index=5*/f32[256,512]{1,0:T(8,128)S(1)}) custom-call(bf16[512,1408]{1,0:T(8,128)(2,1)} %bitcast.185, bf16[2048,1408]{1,0:T(8,128)(2,1)} %get-tuple-element.61.refs_1_, ...), custom_call_target="tpu_custom_call" | custom-call | flops 60000000 | bytes 200000000 | tf_op jit(solution)/shard_map/closing/pallas_call | solution.py:1093
  (261 shorter events, 66.1 us)
Async XLA Ops:
  7.2 241.6 %all-gather.2.cloned.1.call-start = ((), (), s32[]{:S(2)}) async-start(), calls=%async_computation.1 | async-start | bytes 10616832 | tf_op jit(solution)/shard_map/all_gather | solution.py:1544
  12.0 701.8 %reduce-scatter.2.cloned.1.call-start = ((), (), s32[]{:S(2)}) async-start(), calls=%async_computation.2 | async-start | bytes 10616832 | tf_op jit(solution)/shard_map/reduce_scatter | solution.py:1693
  13.8 79.1 %copy-start.23 = (f32[128,32]{1,0:T(8,128)}, f32[128,32]{1,0:T(8,128)S(1)}, u32[]{:S(2)}) copy-start(f32[128,32]{1,0:T(8,128)S(1)} %copy.180) | copy-start | bytes 49156
  94.3 10.0 %copy-start.16 = (bf16[4,128,576]{2,1,0:T(8,128)(2,1)}, bf16[4,128,576]{2,1,0:T(8,128)(2,1)S(1)}, u32[]{:S(2)}) copy-start(bf16[4,128,576]{2,1,0:T(8,128)(2,1)S(1)} %pad_maximum_fusion.2) | copy-start | bytes 1769476
  95.1 19.4 %collective-permute-start = (bf16[4,64,576]{2,1,0:T(8,128)(2,1)}, bf16[4,64,576]{2,1,0:T(8,128)(2,1)}, u32[]{:S(2)}, u32[]{:S(2)}) collective-permute-start(bf16[4,64,576]{2,1,0:T(8,128)(2,1)} %slice.155), channel_id=1, source_target_pairs={{0,4},{4,0},{8,12},{12,8},{1,5},{5,1},{9,13},{13,9},{2,6},{6,2},{1... | collective-permute-start | bytes 884744 | tf_op jit(solution)/shard_map/ppermute | solution.py:79
  95.5 20.0 %collective-permute-start.1 = (bf16[4,64,576]{2,1,0:T(8,128)(2,1)}, bf16[4,64,576]{2,1,0:T(8,128)(2,1)}, u32[]{:S(2)}, u32[]{:S(2)}) collective-permute-start(bf16[4,64,576]{2,1,0:T(8,128)(2,1)} %slice.155), channel_id=1, source_target_pairs={{0,8},{4,12},{8,0},{12,4},{1,9},{5,13},{9,1},{13,5},{2,10},{6,14},... | collective-permute-start | bytes 884744 | tf_op jit(solution)/shard_map/ppermute | solution.py:79
  96.0 20.5 %collective-permute-start.2 = (bf16[4,64,576]{2,1,0:T(8,128)(2,1)}, bf16[4,64,576]{2,1,0:T(8,128)(2,1)}, u32[]{:S(2)}, u32[]{:S(2)}) collective-permute-start(bf16[4,64,576]{2,1,0:T(8,128)(2,1)} %slice.155), channel_id=1, source_target_pairs={{0,12},{4,8},{8,4},{12,0},{1,13},{5,9},{9,5},{13,1},{2,14},{6,10},... | collective-permute-start | bytes 884744 | tf_op jit(solution)/shard_map/ppermute | solution.py:79
  97.7 9.8 %collective-permute-start.3 = (s32[128,6]{1,0:T(8,128)}, s32[128,6]{1,0:T(8,128)}, u32[]{:S(2)}, u32[]{:S(2)}) collective-permute-start(s32[128,6]{1,0:T(8,128)} %bitcast.28), channel_id=1, source_target_pairs={{0,1},{1,0},{2,3},{3,2},{4,5},{5,4},{6,7},{7,6},{8,9},{9,8},{10,11... | collective-permute-start | bytes 9224 | tf_op jit(solution)/shard_map/ppermute | solution.py:79
  99.3 9.2 %collective-permute-start.4 = (s32[128,6]{1,0:T(8,128)}, s32[128,6]{1,0:T(8,128)}, u32[]{:S(2)}, u32[]{:S(2)}) collective-permute-start(s32[128,6]{1,0:T(8,128)} %bitcast.28), channel_id=1, source_target_pairs={{0,2},{1,3},{2,0},{3,1},{4,6},{5,7},{6,4},{7,5},{8,10},{9,11},{10,... | collective-permute-start | bytes 9224 | tf_op jit(solution)/shard_map/ppermute | solution.py:79
  107.4 6.3 collective-permute-start.5
  114.1 126.5 %copy-start.34 = (s32[4,512]{1,0:T(4,128)}, s32[4,512]{1,0:T(4,128)S(1)}, u32[]{:S(2)}) copy-start(s32[4,512]{1,0:T(4,128)S(1)} %fusion.15) | copy-start | bytes 24580
  248.8 87.4 %slice-start = ((f32[4,224]{1,0:T(4,128)}), f32[1,224]{1,0:T(1,128)S(1)}, s32[]{:S(2)}) async-start(f32[4,224]{1,0:T(4,128)} %copy-done.41), calls=%async_computation.3 | async-start | bytes 2048 | tf_op jit(solution)/shard_map/slice | solution.py:1651
  337.3 104.4 %copy-start.35 = (s32[4,512]{1,0:T(4,128)S(1)}, s32[4,512]{1,0:T(4,128)}, u32[]{:S(2)}) copy-start(s32[4,512]{1,0:T(4,128)} %copy-done.34) | copy-start | bytes 24580
  568.5 59.5 %collective-permute-start.8 = (bf16[128,2048]{1,0:T(8,128)(2,1)}, bf16[128,2048]{1,0:T(8,128)(2,1)}, u32[]{:S(2)}, u32[]{:S(2)}) collective-permute-start(bf16[128,2048]{1,0:T(8,128)(2,1)} %get-tuple-element.197), channel_id=1, source_target_pairs={{0,3},{1,2},{2,1},{3,0},{4,7},{5,6},{6,5},{7,4},{8,11},{9,10},{10,... | collective-permute-start | bytes 1572872 | tf_op jit(solution)/shard_map/ppermute | solution.py:79
  569.4 58.6 %collective-permute-start.7 = (bf16[128,2048]{1,0:T(8,128)(2,1)}, bf16[128,2048]{1,0:T(8,128)(2,1)}, u32[]{:S(2)}, u32[]{:S(2)}) collective-permute-start(bf16[128,2048]{1,0:T(8,128)(2,1)} %get-tuple-element.198), channel_id=1, source_target_pairs={{0,2},{1,3},{2,0},{3,1},{4,6},{5,7},{6,4},{7,5},{8,10},{9,11},{10,... | collective-permute-start | bytes 1572872 | tf_op jit(solution)/shard_map/ppermute | solution.py:79
  588.1 19.5 %collective-permute-start.11 = (bf16[4,64,576]{2,1,0:T(8,128)(2,1)S(1)}, bf16[4,64,576]{2,1,0:T(8,128)(2,1)S(1)}, u32[]{:S(2)}, u32[]{:S(2)}) collective-permute-start(bf16[4,64,576]{2,1,0:T(8,128)(2,1)S(1)} %get-tuple-element.190), channel_id=1, source_target_pairs={{0,12},{4,8},{8,4},{12,0},{1,13},{5,9},{9,5},{13,1},{2,14},{6,10},... | collective-permute-start | bytes 884744 | tf_op jit(solution)/shard_map/ppermute | solution.py:79
  589.1 30.2 %collective-permute-start.10 = (bf16[4,64,576]{2,1,0:T(8,128)(2,1)S(1)}, bf16[4,64,576]{2,1,0:T(8,128)(2,1)S(1)}, u32[]{:S(2)}, u32[]{:S(2)}) collective-permute-start(bf16[4,64,576]{2,1,0:T(8,128)(2,1)S(1)} %get-tuple-element.191), channel_id=1, source_target_pairs={{0,8},{4,12},{8,0},{12,4},{1,9},{5,13},{9,1},{13,5},{2,10},{6,14},... | collective-permute-start | bytes 884744 | tf_op jit(solution)/shard_map/ppermute | solution.py:79
  589.8 29.5 %collective-permute-start.9 = (bf16[4,64,576]{2,1,0:T(8,128)(2,1)S(1)}, bf16[4,64,576]{2,1,0:T(8,128)(2,1)S(1)}, u32[]{:S(2)}, u32[]{:S(2)}) collective-permute-start(bf16[4,64,576]{2,1,0:T(8,128)(2,1)S(1)} %get-tuple-element.189), channel_id=1, source_target_pairs={{0,4},{4,0},{8,12},{12,8},{1,5},{5,1},{9,13},{13,9},{2,6},{6,2},{1... | collective-permute-start | bytes 884744 | tf_op jit(solution)/shard_map/ppermute | solution.py:79
  605.2 15.4 %copy-start.37 = (f32[512]{0:T(512)S(1)}, f32[512]{0:T(512)}, u32[]{:S(2)}) copy-start(f32[512]{0:T(512)} %copy-done.36) | copy-start | bytes 6148
  605.2 15.4 %copy-start.39 = (f32[4,128]{1,0:T(4,128)S(1)}, f32[4,128]{1,0:T(4,128)}, u32[]{:S(2)}) copy-start(f32[4,128]{1,0:T(4,128)} %copy-done.38) | copy-start | bytes 6148
  607.6 15.3 %copy-start.43 = (f32[4,128]{1,0:T(4,128)S(1)}, f32[4,128]{1,0:T(4,128)}, u32[]{:S(2)}) copy-start(f32[4,128]{1,0:T(4,128)} %copy-done.42) | copy-start | bytes 6148
  607.6 15.3 %copy-start.24 = (f32[128,32]{1,0:T(8,128)S(1)}, f32[128,32]{1,0:T(8,128)}, u32[]{:S(2)}) copy-start(f32[128,32]{1,0:T(8,128)} %copy-done.23) | copy-start | bytes 49156
  607.6 20.4 %collective-permute-start.6 = (bf16[128,2048]{1,0:T(8,128)(2,1)}, bf16[128,2048]{1,0:T(8,128)(2,1)}, u32[]{:S(2)}, u32[]{:S(2)}) collective-permute-start(bf16[128,2048]{1,0:T(8,128)(2,1)} %get-tuple-element.196), channel_id=1, source_target_pairs={{0,1},{1,0},{2,3},{3,2},{4,5},{5,4},{6,7},{7,6},{8,9},{9,8},{10,11... | collective-permute-start | bytes 1572872 | tf_op jit(solution)/shard_map/ppermute | solution.py:79
  629.9 77.3 %copy-start.5 = (bf16[128,2048]{1,0:T(8,128)(2,1)}, bf16[128,2048]{1,0:T(8,128)(2,1)S(1)}, u32[]{:S(2)}) copy-start(bf16[128,2048]{1,0:T(8,128)(2,1)S(1)} %fusion.19.refs_3_) | copy-start | bytes 1572868
  (47 other events, 142.4 us)
Sparse Core Ops, SparseCore 0:
  12.1 85.8 all-gather.1
  555.6 87.8 reduce-scatter.1

commit v5 on v4

--- a/solution.py
+++ b/solution.py
@@ -1061,7 +1061,7 @@
             for task in tasks if stage < 4 else tasks[:1]:
                 next(task)
             next(line)
-        run_tasks(line, *tasks)
+        run_tasks(*tasks, line)
 
     shapes = [
         jax.ShapeDtypeStruct((rows, width), jnp.float32),

time: 737 us -> 738 us (level)
  no operation moved by 1% of the time
where the time goes in v5:
time: 738 us; the launch traced here: 729 us
  Pallas kernels  578 us (78%)
  local copies, waits for them, and re-layouts  48 us (7%)
  matrix products  38.5 us (5%)
  other arithmetic  23.1 us (3%)
  between operations  15.8 us (2%)
  waiting for transfers between devices  14.3 us (2%)
  starting transfers between devices  11.5 us (2%)
    pallas_call x1, Pallas kernels, middle_sum(): pl.pallas_call(kernel, out_shape=shapes, in_specs=[INSIDE] * 7 + [ANY] *...  119 us
    pallas_call x1, Pallas kernels, routed_expert(): pl.pallas_call(kernel, out_shape=shapes, in_specs=[ANY] * len(operands) +...  103 us
    pallas_call x1, Pallas kernels, branch_sum(): pl.pallas_call(kernel, out_shape=shapes, in_specs=[INSIDE] * 4 + [ANY] *...  103 us
    pallas_call x1, Pallas kernels, shared_and_rows(): pl.pallas_call(kernel, out_shape=shapes, in_specs=[ANY] * 5 + [INSIDE], o...  87.4 us
    pallas_call x1, Pallas kernels, closing(): pl.pallas_call(kernel, out_shape=shapes, in_specs=[INSIDE] * 3 + [ANY] +...  77.7 us
    pallas_call x1, Pallas kernels, opening(): pl.pallas_call(kernel, out_shape=shapes, in_specs=[INSIDE] * (2 + number)...  72 us
    unnamed x129, local copies, waits for them, and re-layouts  17.7 us
    dot_general x4, matrix products, product(): return jnp.dot(left_side, right_side, preferred_element_type=jnp.float32)  16.9 us
  transfers between devices with their start and end apart: 14, of which 2 were waited for; matrix products, arithmetic and copies ran while one was open for 11% of the time, Pallas kernels for 39%

profile of v5, /device:TPU:0, one launch (start us, length us, event | category | flops | bytes accessed | tf_op | source)
XLA Modules:
  0.0 728.8 jit_solution(6035040449583799759)
XLA Ops:
  14.2 72.0 %opening.1 = (f32[8,8,256]{2,1,0:T(8,128)S(1)}, bf16[4,128,2048]{2,1,0:T(8,128)(2,1)}, bf16[2048,1408]{1,0:T(8,128)(2,1)}, bf16[512,1024]{1,0:T(8,128)(2,1)}, bf16[2048,512]{1,0:T(8,128)(2,1)}) custom-call(bf16[128,2048]{1,0:T(8,128)(2,1)S(1)} %bitcast.168, f32[8,256]{1,0:T(8,128)S(1)} %stack.31.refs_1_, bf16[256,1408]{1,0:T(8,128)(2,1)S(1)} %concatenate.29.refs_2_, ...), custom_call_target="tpu_custom_call" | custom-call | flops 60000000 | bytes 150000000 | tf_op jit(solution)/shard_map/opening/pallas_call | solution.py:524
  86.3 6.4 fusion
  99.3 2.6 collective-permute-start.4
  109.4 4.4 collective-permute-done.5
  118.8 119.0 %middle_sum.1 = (f32[128,2048]{1,0:T(8,128)}, bf16[4,128,2048]{2,1,0:T(8,128)(2,1)}, bf16[4,128,2048]{2,1,0:T(8,128)(2,1)}, bf16[4,128,512]{2,1,0:T(8,128)(2,1)S...) custom-call(bf16[4,128,512]{2,1,0:T(8,128)(2,1)S(1)} %slice.195.refs, ...), custom_call_target="tpu_custom_call" | custom-call | flops 60000000 | bytes 300000000 | tf_op jit(solution)/shard_map/middle_sum/pallas_call | solution.py:664
  237.8 2.7 fusion.44
  240.9 3.9 convolution_convert_fusion.1
  244.8 3.9 convolution_convert_fusion
  248.8 87.4 %shared_and_rows.1 = (bf16[512,768]{1,0:T(8,128)(2,1)S(1)}, f32[512,2048]{1,0:T(8,128)}, bf16[2048,2304]{1,0:T(8,128)(2,1)}, f32[3,8,256]{2,1,0:T(8,128)S(1)}, b...) custom-call(bf16[512,2048]{1,0:T(8,128)(2,1)} %bitcast.181, bf16[512,2048]{1,0:T(8,128)(2,1)} %bitcast.215, ...), custom_call_target="tpu_custom_call" | custom-call | flops 9663676416 | bytes 120000000 | tf_op jit(solution)/shard_map/shared_and_rows/pallas_call | solution.py:1201
  337.3 103.2 %routed_expert.1 = (bf16[4,224,2048]{2,1,0:T(8,128)(2,1)}, bf16[4,224,2048]{2,1,0:T(8,128)(2,1)}, f32[4,224,128]{2,1,0:T(8,128)}, bf16[2048,1408]{1,0:T(8,128)(2...) custom-call(bf16[4,224,2048]{2,1,0:T(8,128)(2,1)} %bitcast.218, bf16[4,224,2048]{2,1,0:T(8,128)(2,1)} %bitcast.220, ...), custom_call_target="tpu_custom_call" | custom-call | flops 46506442752 | bytes 200000000 | tf_op jit(solution)/shard_map/routed_expert/pallas_call | solution.py:1362
  442.2 3.3 fusion.23
  445.5 6.1 fusion.3
  451.7 102.8 %branch_sum.1 = (f32[128,2048]{1,0:T(8,128)S(1)}, f32[1,2048]{1,0:T(1,128)S(1)}, bf16[4,128,2048]{2,1,0:T(8,128)(2,1)}, bf16[4,256,1408]{2,1,0:T(8,128)(2,1)}, b...) custom-call(bf16[4,128,2048]{2,1,0:T(8,128)(2,1)} %bitcast.189, ...), custom_call_target="tpu_custom_call", output_to_operand_aliasing={{6}: (7, {}), {7}: (8, {})} | custom-call | flops 60000000 | bytes 300000000 | tf_op jit(solution)/shard_map/branch_sum/pallas_call | solution.py:900
  555.9 4.2 copy.210
  560.1 4.7 fusion.4
  571.0 15.5 %attention_back.1 = (bf16[4,128,512]{2,1,0:T(8,128)(2,1)S(1)}, f32[4,128,256]{2,1,0:T(8,128)S(1)}, f32[4,320,576]{2,1,0:T(8,128)}, f32[512,1024]{1,0:T(8,128)S(1)}) custom-call(bf16[4,128,2048]{2,1,0:T(8,128)(2,1)S(1)} %copy-done.9, bf16[2048,512]{1,0:T(8,128)(2,1)S(1)} %copy-done.4, bf16[4,4,128,320]{3,2,1,0:T(8,128)(2,1)S(1)} %copy-done.10, ...), custom_call_target="tpu_custom_call" | custom-call | flops 20000000000 | bytes 30000000 | tf_op jit(solution)/shard_map/attention_back/pallas_call | solution.py:1440
  591.2 2.6 bitcast_convert_fusion.refs_9_
  595.8 3.0 convert_element_type.143
  598.9 2.9 convert_element_type.144
  601.9 3.3 convert_element_type.145
  605.2 2.4 convolution_bitcast_fusion
  609.5 9.9 %collective-permute-done.10 = bf16[4,64,576]{2,1,0:T(8,128)(2,1)S(1)} collective-permute-done((bf16[4,64,576]{2,1,0:T(8,128)(2,1)S(1)}, bf16[4,64,576]{2,1,0:T(8,128)(2,1)S(1)}, u32[]{:S(2)}, u32[]{:S(2)}) %collective-permute-start.10) | collective-permute-done | bytes 294944 | tf_op jit(solution)/shard_map/ppermute | solution.py:79
  624.9 2.9 concatenate.35
  630.0 77.7 %closing.1 = (f32[128,2048]{1,0:T(8,128)}, f32[24,256]{1,0:T(8,128)S(1)}, f32[64,640]{1,0:T(8,128)S(1)}, f32[256,1408]{1,0:T(8,128)}, f32[64,1024]{1,0:T(8,128)S(1)}, /*index=5*/f32[256,512]{1,0:T(8,128)S(1)}) custom-call(bf16[512,1408]{1,0:T(8,128)(2,1)} %bitcast.185, bf16[2048,1408]{1,0:T(8,128)(2,1)} %get-tuple-element.61.refs_1_, ...), custom_call_target="tpu_custom_call" | custom-call | flops 60000000 | bytes 200000000 | tf_op jit(solution)/shard_map/closing/pallas_call | solution.py:1093
  (261 shorter events, 66.1 us)
Async XLA Ops:
  7.2 241.6 %all-gather.2.cloned.1.call-start = ((), (), s32[]{:S(2)}) async-start(), calls=%async_computation.1 | async-start | bytes 10616832 | tf_op jit(solution)/shard_map/all_gather | solution.py:1544
  12.0 702.3 %reduce-scatter.2.cloned.1.call-start = ((), (), s32[]{:S(2)}) async-start(), calls=%async_computation.2 | async-start | bytes 10616832 | tf_op jit(solution)/shard_map/reduce_scatter | solution.py:1693
  13.8 79.1 %copy-start.23 = (f32[128,32]{1,0:T(8,128)}, f32[128,32]{1,0:T(8,128)S(1)}, u32[]{:S(2)}) copy-start(f32[128,32]{1,0:T(8,128)S(1)} %copy.180) | copy-start | bytes 49156
  94.3 10.0 %copy-start.16 = (bf16[4,128,576]{2,1,0:T(8,128)(2,1)}, bf16[4,128,576]{2,1,0:T(8,128)(2,1)S(1)}, u32[]{:S(2)}) copy-start(bf16[4,128,576]{2,1,0:T(8,128)(2,1)S(1)} %pad_maximum_fusion.2) | copy-start | bytes 1769476
  95.1 19.4 %collective-permute-start = (bf16[4,64,576]{2,1,0:T(8,128)(2,1)}, bf16[4,64,576]{2,1,0:T(8,128)(2,1)}, u32[]{:S(2)}, u32[]{:S(2)}) collective-permute-start(bf16[4,64,576]{2,1,0:T(8,128)(2,1)} %slice.155), channel_id=1, source_target_pairs={{0,4},{4,0},{8,12},{12,8},{1,5},{5,1},{9,13},{13,9},{2,6},{6,2},{1... | collective-permute-start | bytes 884744 | tf_op jit(solution)/shard_map/ppermute | solution.py:79
  95.5 20.0 %collective-permute-start.1 = (bf16[4,64,576]{2,1,0:T(8,128)(2,1)}, bf16[4,64,576]{2,1,0:T(8,128)(2,1)}, u32[]{:S(2)}, u32[]{:S(2)}) collective-permute-start(bf16[4,64,576]{2,1,0:T(8,128)(2,1)} %slice.155), channel_id=1, source_target_pairs={{0,8},{4,12},{8,0},{12,4},{1,9},{5,13},{9,1},{13,5},{2,10},{6,14},... | collective-permute-start | bytes 884744 | tf_op jit(solution)/shard_map/ppermute | solution.py:79
  96.0 20.5 %collective-permute-start.2 = (bf16[4,64,576]{2,1,0:T(8,128)(2,1)}, bf16[4,64,576]{2,1,0:T(8,128)(2,1)}, u32[]{:S(2)}, u32[]{:S(2)}) collective-permute-start(bf16[4,64,576]{2,1,0:T(8,128)(2,1)} %slice.155), channel_id=1, source_target_pairs={{0,12},{4,8},{8,4},{12,0},{1,13},{5,9},{9,5},{13,1},{2,14},{6,10},... | collective-permute-start | bytes 884744 | tf_op jit(solution)/shard_map/ppermute | solution.py:79
  97.7 9.8 %collective-permute-start.3 = (s32[128,6]{1,0:T(8,128)}, s32[128,6]{1,0:T(8,128)}, u32[]{:S(2)}, u32[]{:S(2)}) collective-permute-start(s32[128,6]{1,0:T(8,128)} %bitcast.28), channel_id=1, source_target_pairs={{0,1},{1,0},{2,3},{3,2},{4,5},{5,4},{6,7},{7,6},{8,9},{9,8},{10,11... | collective-permute-start | bytes 9224 | tf_op jit(solution)/shard_map/ppermute | solution.py:79
  99.3 9.2 %collective-permute-start.4 = (s32[128,6]{1,0:T(8,128)}, s32[128,6]{1,0:T(8,128)}, u32[]{:S(2)}, u32[]{:S(2)}) collective-permute-start(s32[128,6]{1,0:T(8,128)} %bitcast.28), channel_id=1, source_target_pairs={{0,2},{1,3},{2,0},{3,1},{4,6},{5,7},{6,4},{7,5},{8,10},{9,11},{10,... | collective-permute-start | bytes 9224 | tf_op jit(solution)/shard_map/ppermute | solution.py:79
  107.4 6.3 collective-permute-start.5
  114.1 126.5 %copy-start.34 = (s32[4,512]{1,0:T(4,128)}, s32[4,512]{1,0:T(4,128)S(1)}, u32[]{:S(2)}) copy-start(s32[4,512]{1,0:T(4,128)S(1)} %fusion.15) | copy-start | bytes 24580
  248.8 87.4 %slice-start = ((f32[4,224]{1,0:T(4,128)}), f32[1,224]{1,0:T(1,128)S(1)}, s32[]{:S(2)}) async-start(f32[4,224]{1,0:T(4,128)} %copy-done.41), calls=%async_computation.3 | async-start | bytes 2048 | tf_op jit(solution)/shard_map/slice | solution.py:1651
  337.3 104.4 %copy-start.35 = (s32[4,512]{1,0:T(4,128)S(1)}, s32[4,512]{1,0:T(4,128)}, u32[]{:S(2)}) copy-start(s32[4,512]{1,0:T(4,128)} %copy-done.34) | copy-start | bytes 24580
  568.5 59.5 %collective-permute-start.8 = (bf16[128,2048]{1,0:T(8,128)(2,1)}, bf16[128,2048]{1,0:T(8,128)(2,1)}, u32[]{:S(2)}, u32[]{:S(2)}) collective-permute-start(bf16[128,2048]{1,0:T(8,128)(2,1)} %get-tuple-element.197), channel_id=1, source_target_pairs={{0,3},{1,2},{2,1},{3,0},{4,7},{5,6},{6,5},{7,4},{8,11},{9,10},{10,... | collective-permute-start | bytes 1572872 | tf_op jit(solution)/shard_map/ppermute | solution.py:79
  569.4 58.6 %collective-permute-start.7 = (bf16[128,2048]{1,0:T(8,128)(2,1)}, bf16[128,2048]{1,0:T(8,128)(2,1)}, u32[]{:S(2)}, u32[]{:S(2)}) collective-permute-start(bf16[128,2048]{1,0:T(8,128)(2,1)} %get-tuple-element.198), channel_id=1, source_target_pairs={{0,2},{1,3},{2,0},{3,1},{4,6},{5,7},{6,4},{7,5},{8,10},{9,11},{10,... | collective-permute-start | bytes 1572872 | tf_op jit(solution)/shard_map/ppermute | solution.py:79
  588.1 19.5 %collective-permute-start.11 = (bf16[4,64,576]{2,1,0:T(8,128)(2,1)S(1)}, bf16[4,64,576]{2,1,0:T(8,128)(2,1)S(1)}, u32[]{:S(2)}, u32[]{:S(2)}) collective-permute-start(bf16[4,64,576]{2,1,0:T(8,128)(2,1)S(1)} %get-tuple-element.190), channel_id=1, source_target_pairs={{0,12},{4,8},{8,4},{12,0},{1,13},{5,9},{9,5},{13,1},{2,14},{6,10},... | collective-permute-start | bytes 884744 | tf_op jit(solution)/shard_map/ppermute | solution.py:79
  589.1 30.2 %collective-permute-start.10 = (bf16[4,64,576]{2,1,0:T(8,128)(2,1)S(1)}, bf16[4,64,576]{2,1,0:T(8,128)(2,1)S(1)}, u32[]{:S(2)}, u32[]{:S(2)}) collective-permute-start(bf16[4,64,576]{2,1,0:T(8,128)(2,1)S(1)} %get-tuple-element.191), channel_id=1, source_target_pairs={{0,8},{4,12},{8,0},{12,4},{1,9},{5,13},{9,1},{13,5},{2,10},{6,14},... | collective-permute-start | bytes 884744 | tf_op jit(solution)/shard_map/ppermute | solution.py:79
  589.8 29.5 %collective-permute-start.9 = (bf16[4,64,576]{2,1,0:T(8,128)(2,1)S(1)}, bf16[4,64,576]{2,1,0:T(8,128)(2,1)S(1)}, u32[]{:S(2)}, u32[]{:S(2)}) collective-permute-start(bf16[4,64,576]{2,1,0:T(8,128)(2,1)S(1)} %get-tuple-element.189), channel_id=1, source_target_pairs={{0,4},{4,0},{8,12},{12,8},{1,5},{5,1},{9,13},{13,9},{2,6},{6,2},{1... | collective-permute-start | bytes 884744 | tf_op jit(solution)/shard_map/ppermute | solution.py:79
  605.2 15.4 %copy-start.37 = (f32[512]{0:T(512)S(1)}, f32[512]{0:T(512)}, u32[]{:S(2)}) copy-start(f32[512]{0:T(512)} %copy-done.36) | copy-start | bytes 6148
  605.2 15.4 %copy-start.39 = (f32[4,128]{1,0:T(4,128)S(1)}, f32[4,128]{1,0:T(4,128)}, u32[]{:S(2)}) copy-start(f32[4,128]{1,0:T(4,128)} %copy-done.38) | copy-start | bytes 6148
  607.6 15.3 %copy-start.43 = (f32[4,128]{1,0:T(4,128)S(1)}, f32[4,128]{1,0:T(4,128)}, u32[]{:S(2)}) copy-start(f32[4,128]{1,0:T(4,128)} %copy-done.42) | copy-start | bytes 6148
  607.6 15.3 %copy-start.24 = (f32[128,32]{1,0:T(8,128)S(1)}, f32[128,32]{1,0:T(8,128)}, u32[]{:S(2)}) copy-start(f32[128,32]{1,0:T(8,128)} %copy-done.23) | copy-start | bytes 49156
  607.6 20.4 %collective-permute-start.6 = (bf16[128,2048]{1,0:T(8,128)(2,1)}, bf16[128,2048]{1,0:T(8,128)(2,1)}, u32[]{:S(2)}, u32[]{:S(2)}) collective-permute-start(bf16[128,2048]{1,0:T(8,128)(2,1)} %get-tuple-element.196), channel_id=1, source_target_pairs={{0,1},{1,0},{2,3},{3,2},{4,5},{5,4},{6,7},{7,6},{8,9},{9,8},{10,11... | collective-permute-start | bytes 1572872 | tf_op jit(solution)/shard_map/ppermute | solution.py:79
  629.9 77.7 %copy-start.5 = (bf16[128,2048]{1,0:T(8,128)(2,1)}, bf16[128,2048]{1,0:T(8,128)(2,1)S(1)}, u32[]{:S(2)}) copy-start(bf16[128,2048]{1,0:T(8,128)(2,1)S(1)} %fusion.19.refs_3_) | copy-start | bytes 1572868
  (47 other events, 142.4 us)
Sparse Core Ops, SparseCore 0:
  12.1 85.8 all-gather.1
  555.6 87.8 reduce-scatter.1
